TPU v7x, 32 devices: a whole 2x2x4 slice. The times are simulated.
32 devices in a mesh: tok: 8 (over z, y), head: 4 (over x, core).
Axes of the slice: x: 2, y: 2, z: 4, core: 2. Of those that a mesh axis runs over, the one named last changes fastest.
Arguments:
- prefill_states: bfloat16 [1, 2048, 2048], P(None, 'tok'), may hold values from -6 to 6
- decode_states: bfloat16 [64, 2048], P('tok'), may hold values from -6 to 6
- attn_gain: float32 [2048], replicated, may hold values from 0.1 to 1.9
- w_qkv: bfloat16 [2048, 3, 2048], P(None, None, 'head'), may hold values from -0.125 to 0.125
- w_out: bfloat16 [2048, 2048], P('head'), may hold values from -0.125 to 0.125
- ffn_gain: float32 [2048], replicated, may hold values from 0.1 to 1.9
- w_gate_up: bfloat16 [2048, 2, 5120], P(None, None, 'tok'), may hold values from -0.125 to 0.125
- w_down: bfloat16 [5120, 2048], P('tok'), may hold values from -0.078125 to 0.078125
- prefill_pool: bfloat16 [384, 128, 512], P('tok', None, 'head')
- prefill_pages: int32 [8, 48], P('tok'), may hold values from 0 to 47, as said below
- prefill_lengths: int32 [1], replicated, may hold values from 1 to 6144, as said below
- prefill_home: int32 [8], replicated, may hold values from 0 to 7, each once
- decode_pool: bfloat16 [512, 128, 4096], P('tok', None, 'head')
- decode_pages: int32 [64, 32], P('tok'), may hold values from 0 to 63, as said below
- decode_lengths: int32 [64], P('tok'), may hold values from 1 to 4096, as said below
- decode_home: int32 [64], replicated, may hold values from 0 to 63, each once
Outputs:
- prefill_out: bfloat16 [1, 2048, 2048], P(None, ('tok', 'head'))
- decode_out: bfloat16 [64, 2048], P(('tok', 'head'))
Inputs may be any that keep to these rules, and one draw needn't show every extreme that they name: `prefill_pages`: each row is an ordering of all 48 pages of the prefill pool on that row's tok index. `prefill_lengths`: one prefill request has exactly 6144 cached tokens. `decode_pages`: slot s lies on tok index s // 8; within one tok index the first ceil(length / 128) pages of its slots are all different. `decode_lengths`: every tok index hosts one decode request of exactly 4096 cached tokens.
All inputs are finite; a program needn't handle non-finite values.
Results may differ from a plain program's by a relative error of at most 0.017.
The roundings to bfloat16 on the way count: a program that leaves them out, or rounds other values in their place, can miss the bound.
Values may be sent and summed in bfloat16 or wider, within the bound.
No kernel may reach another device: no remote copies, remote signals or barrier semaphores. Data moves between devices by JAX's collectives and lax.ppermute only.
A program may use at most 128 MiB of HBM per device.

v0:
```python
import math

import jax
import jax.numpy as jnp
from jax import lax
from jax.sharding import PartitionSpec as P

HD = 64


EPSILON = 1e-06
SCALE = 0.125
MASKED = -1e30


def rms_norm(rows, gain):
    values = rows.astype(jnp.float32)
    inverse = lax.rsqrt(jnp.mean(values * values, axis=-1, keepdims=True) + EPSILON)
    return (values * inverse * gain).astype(jnp.bfloat16)


def inner(left, right):
    return lax.dot_general(
        left, right, (((1,), (1,)), ((), ())), preferred_element_type=jnp.float32
    )


def shards(
    prefill_states,
    decode_states,
    attn_gain,
    w_qkv,
    w_out,
    ffn_gain,
    w_gate_up,
    w_down,
    prefill_pool,
    prefill_pages,
    prefill_lengths,
    prefill_home,
    decode_pool,
    decode_pages,
    decode_lengths,
    decode_home,
):
    n_tok = lax.axis_size("tok")
    n_head = lax.axis_size("head")
    my_tok = lax.axis_index("tok")
    my_head = lax.axis_index("head")
    requests, positions, width = prefill_states.shape
    hosted = decode_states.shape[0]
    heads_per = w_qkv.shape[2] // HD
    stretch = positions * n_tok
    units = requests * heads_per
    features = heads_per * HD
    normed_pre = rms_norm(prefill_states, attn_gain).reshape(requests * positions, width)
    normed_dec = rms_norm(decode_states, attn_gain)
    normed = jnp.concatenate([normed_pre, normed_dec], axis=0)
    projected = jnp.dot(
        normed, w_qkv.reshape(width, 3 * features), preferred_element_type=jnp.float32
    ).astype(jnp.bfloat16)
    proj_pre = projected[: requests * positions].reshape(requests, positions, 3, heads_per, HD)
    proj_dec = projected[requests * positions :]
    unit_ids = jnp.arange(units, dtype=jnp.int32)
    host_ids = jnp.arange(n_tok, dtype=jnp.int32)
    hosted_unit = jnp.sum(
        jnp.where(prefill_home[None, :] == host_ids[:, None], unit_ids[None, :], 0), axis=1
    )
    by_unit = jnp.transpose(proj_pre, (0, 3, 1, 2, 4)).reshape(units, positions * 3 * HD)
    outgoing = jnp.take(by_unit, hosted_unit, axis=0)
    pre_cols = positions * 3 * HD
    spread = jnp.broadcast_to(
        proj_dec.reshape(1, hosted * 3 * features), (n_tok, hosted * 3 * features)
    )
    outgoing = jnp.concatenate([outgoing, spread], axis=1)
    arrived = lax.all_to_all(outgoing, "tok", split_axis=0, concat_axis=0, tiled=True)
    arrived_dec = arrived[:, pre_cols:].reshape(n_tok * hosted, 3, heads_per, HD)
    arrived_pre = arrived[:, :pre_cols].reshape(stretch, 3, HD)
    query_rows = arrived_pre[:, 0]
    key_rows = arrived_pre[:, 1]
    value_rows = arrived_pre[:, 2]
    my_unit = hosted_unit[my_tok]
    length = prefill_lengths[my_unit // heads_per]
    cache = jnp.take(prefill_pool, prefill_pages[0], axis=0).reshape(-1, 2 * HD)
    cache_keys = cache[:, :HD]
    cache_values = cache[:, HD:]
    span = cache.shape[0]
    block = math.gcd(stretch, 512)

    def attend(start):
        rows = lax.dynamic_slice_in_dim(query_rows, start, block, 0)
        score_cache = inner(rows, cache_keys) * SCALE
        score_cache = jnp.where(jnp.arange(span)[None, :] < length, score_cache, MASKED)
        score_stretch = inner(rows, key_rows) * SCALE
        row_pos = start + jnp.arange(block)[:, None]
        score_stretch = jnp.where(jnp.arange(stretch)[None, :] <= row_pos, score_stretch, MASKED)
        top = jnp.maximum(
            jnp.max(score_cache, axis=1, keepdims=True),
            jnp.max(score_stretch, axis=1, keepdims=True),
        )
        weight_cache = jnp.exp(score_cache - top)
        weight_stretch = jnp.exp(score_stretch - top)
        total = jnp.sum(weight_cache, axis=1, keepdims=True) + jnp.sum(
            weight_stretch, axis=1, keepdims=True
        )
        mixed = jnp.dot(
            weight_cache.astype(jnp.bfloat16), cache_values, preferred_element_type=jnp.float32
        )
        mixed = mixed + jnp.dot(
            weight_stretch.astype(jnp.bfloat16), value_rows, preferred_element_type=jnp.float32
        )
        return (mixed / total).astype(jnp.bfloat16)

    starts = jnp.arange(stretch // block, dtype=jnp.int32) * block
    attn_unit = lax.map(attend, starts).reshape(stretch, HD)
    slots = my_tok * hosted + jnp.arange(hosted, dtype=jnp.int32)
    all_requests = jnp.arange(decode_home.shape[0], dtype=jnp.int32)
    anchor = jnp.sum(
        jnp.where(decode_home[None, :] == slots[:, None], all_requests[None, :], 0), axis=1
    )
    mine = jnp.take(arrived_dec, anchor, axis=0)

    def decode_one(operands):
        pages, slot_length, rows = operands
        cache_slot = jnp.take(decode_pool, pages, axis=0).reshape(-1, heads_per, 2 * HD)
        query = rows[0]
        scores = (
            jnp.einsum(
                "hd,khd->hk", query, cache_slot[:, :, :HD], preferred_element_type=jnp.float32
            )
            * SCALE
        )
        scores = jnp.where(jnp.arange(cache_slot.shape[0])[None, :] < slot_length, scores, MASKED)
        own_score = (
            jnp.sum(query.astype(jnp.float32) * rows[1].astype(jnp.float32), axis=1, keepdims=True)
            * SCALE
        )
        top = jnp.maximum(jnp.max(scores, axis=1, keepdims=True), own_score)
        weights = jnp.exp(scores - top)
        own_weight = jnp.exp(own_score - top)
        total = jnp.sum(weights, axis=1, keepdims=True) + own_weight
        mixed = jnp.einsum(
            "hk,khd->hd",
            weights.astype(jnp.bfloat16),
            cache_slot[:, :, HD:],
            preferred_element_type=jnp.float32,
        )
        mixed = mixed + own_weight.astype(jnp.bfloat16).astype(jnp.float32) * rows[2].astype(
            jnp.float32
        )
        return (mixed / total).astype(jnp.bfloat16).reshape(features)

    decode_attn = lax.map(decode_one, (decode_pages, decode_lengths, mine))
    backward = attn_unit.reshape(n_tok, positions * HD)
    back_cols = positions * HD
    spread_back = jnp.broadcast_to(
        decode_attn.reshape(1, hosted * features), (n_tok, hosted * features)
    )
    backward = jnp.concatenate([backward, spread_back], axis=1)
    returned = lax.all_to_all(backward, "tok", split_axis=0, concat_axis=0, tiled=True)
    by_slot = returned[:, back_cols:].reshape(n_tok * hosted, features)
    my_slots = lax.dynamic_slice_in_dim(decode_home, my_tok * hosted, hosted, 0)
    attn_dec = jnp.take(by_slot, my_slots, axis=0)
    attn_pre = jnp.take(returned[:, :back_cols], prefill_home, axis=0).reshape(
        requests, heads_per, positions, HD
    )
    block_rows = positions // n_head
    decode_share = hosted // n_head
    per = requests * block_rows + decode_share
    pre_rows = jnp.transpose(attn_pre, (0, 2, 1, 3)).reshape(requests, n_head, block_rows, features)
    pre_rows = jnp.transpose(pre_rows, (1, 0, 2, 3)).reshape(
        n_head, requests * block_rows, features
    )
    dec_rows = attn_dec.reshape(n_head, decode_share, features)
    ordered = jnp.concatenate([pre_rows, dec_rows], axis=1).reshape(n_head * per, features)
    mixed_rows = lax.psum_scatter(
        jnp.dot(ordered, w_out, preferred_element_type=jnp.float32).astype(jnp.bfloat16),
        "head",
        scatter_dimension=0,
        tiled=True,
    ).astype(jnp.float32)
    own_pre = lax.dynamic_slice_in_dim(prefill_states, my_head * block_rows, block_rows, 1).reshape(
        requests * block_rows, width
    )
    own_dec = lax.dynamic_slice_in_dim(decode_states, my_head * decode_share, decode_share, 0)
    resid = jnp.concatenate([own_pre, own_dec], axis=0).astype(jnp.float32) + mixed_rows
    normed_mid = rms_norm(resid, ffn_gain)
    piece = lax.all_gather(normed_mid, "tok", axis=0, tiled=True)
    gate = jnp.dot(piece, w_gate_up[:, 0], preferred_element_type=jnp.float32)
    upper = jnp.dot(piece, w_gate_up[:, 1], preferred_element_type=jnp.float32)
    hidden = (jax.nn.gelu(gate, approximate=True) * upper).astype(jnp.bfloat16)
    summed = lax.psum(
        jnp.dot(hidden, w_down, preferred_element_type=jnp.float32).astype(jnp.bfloat16), "tok"
    ).astype(jnp.float32)
    ffn_rows = lax.dynamic_slice_in_dim(summed, my_tok * per, per, 0)
    result = (resid + ffn_rows).astype(jnp.bfloat16)
    prefill_out = result[: requests * block_rows].reshape(requests, block_rows, width)
    decode_out = result[requests * block_rows :]
    return (prefill_out, decode_out)


def solution(mesh):
    placed = (
        P(None, "tok", None),
        P("tok", None),
        P(),
        P(None, None, "head"),
        P("head", None),
        P(),
        P(None, None, "tok"),
        P("tok", None),
        P("tok", None, "head"),
        P("tok", None),
        P(),
        P(),
        P("tok", None, "head"),
        P("tok", None),
        P("tok"),
        P(),
    )
    return jax.shard_map(
        shards,
        mesh=mesh,
        in_specs=placed,
        out_specs=(P(None, ("tok", "head"), None), P(("tok", "head"), None)),
        check_vma=False,
    )
```

profile of v0, /device:TPU:0, one launch (start us, length us, event | category | flops | bytes accessed | tf_op | source)
XLA Modules:
  0.0 828.6 jit_solution(12424663167465588288)
XLA Ops:
  7.2 9.0 %copy.73 = bf16[2048,3,512]{0,2,1:T(8,128)(2,1)} copy(bf16[2048,3,512]{2,0,1:T(8,128)(2,1)} %param.23) | data formatting | bytes 12582912 | tf_op args[3]
  45.5 7.8 all-to-all-start
  56.9 5.3 bitcast_select_fusion.1
  66.9 10.9 %all-to-all-done = bf16[8,2,30720]{2,1,0:T(2,128)(2,1)} async-done(((bf16[8,2,30720]{2,1,0:T(2,128)(2,1)}), bf16[8,2,30720]{2,1,0:T(2,128)(2,1)}, u32[]{:S(2)}, u32[]{:S(2)}) %all-to-all-start) | async-done | bytes 983072 | tf_op jit(solution)/shard_map/all_to_all | solution.py:76
  77.8 5.7 reshape.364
  90.2 6.0 fusion.84
  98.0 72.7 %while.20 = (s32[]{:T(128)}, bf16[4,512,64]{1,2,0:T(8,128)(2,1)S(1)}, s32[]{:T(128)}, s32[4]{0:T(128)S(1)}, bf16[2048,64]{1,0:T(8,128)(2,1)}, /*index=5*/bf16[61...) while((s32[]{:T(128)}, ...), condition=%wide.region_8.9_spmd, body=%wide.region_3.8_spmd.sunk | while | flops 1116837376 | bytes 90302728 | solution.py:115
  173.5 419.9 %while.21 = (s32[]{:T(128)}, bf16[8,512]{1,0:T(8,128)(2,1)S(1)}, s32[8]{0:T(128)S(1)}, bf16[8,3,8,64]{3,2,1,0:T(8,128)(2,1)S(1)}, s32[8,32]{1,0:T(8,128)}, /*ind...) while((s32[]{:T(128)}, bf16[8,512]{1,0:T(8,128)(2,1)S(1)}, s32[8]{0:T(128)S(1)}, ...), condition=%wide.region_14.15_spmd, body=%wide.region_10.14_spmd.sunk | while | flops 12855116 | bytes 76063016 | solution.py:153
  174.4 10.8 %gather_fusion = bf16[32,128,1024]{2,1,0:T(8,128)(2,1)} fusion(bf16[64,128,1024]{2,1,0:T(8,128)(2,1)} %get-tuple-element.346, s32[1024]{0:T(1024)S(1)} %pad_clamp_fusion.7), kind=kCustom, calls=%fused_computation.clone.1 | custom fusion | bytes 16777344 | tf_op jit(solution)/shard_map/while/body/eval_jaxpr/jit(_take)/gather | solution.py:125
  185.2 8.8 %copy.155 = bf16[512,8,8,128]{3,2,1,0:T(8,128)(2,1)} copy(bf16[512,8,8,128]{3,1,2,0:T(8,128)(2,1)} %bitcast.173) | data formatting | bytes 16777216 | tf_op jit(solution)/shard_map/while
  194.7 16.5 %bitcast_select_fusion.3 = bf16[4096,8,128]{2,1,0:T(8,128)(2,1)S(1)} fusion(bf16[512,8,8,128]{3,2,1,0:T(8,128)(2,1)} %copy.155, pred[4096]{0:T(1024)(128)(4,1)S(1)} %broadcast_bitcast_fusion.3), kind=kLoop, calls=%fused_computation.34.clone.1 | loop fusion | flops 4194304 | bytes 16781312 | tf_op jit(solution)/shard_map/while/body/eval_jaxpr/jit(_take)/select_n | solution.py:125
  211.3 4.9 fusion.137
  220.3 5.7 fusion.142
  226.9 10.8 %gather_fusion = bf16[32,128,1024]{2,1,0:T(8,128)(2,1)} fusion(bf16[64,128,1024]{2,1,0:T(8,128)(2,1)} %get-tuple-element.346, s32[1024]{0:T(1024)S(1)} %pad_clamp_fusion.7), kind=kCustom, calls=%fused_computation.clone.1 | custom fusion | bytes 16777344 | tf_op jit(solution)/shard_map/while/body/eval_jaxpr/jit(_take)/gather | solution.py:125
  237.7 8.8 %copy.155 = bf16[512,8,8,128]{3,2,1,0:T(8,128)(2,1)} copy(bf16[512,8,8,128]{3,1,2,0:T(8,128)(2,1)} %bitcast.173) | data formatting | bytes 16777216 | tf_op jit(solution)/shard_map/while
  247.2 16.5 %bitcast_select_fusion.3 = bf16[4096,8,128]{2,1,0:T(8,128)(2,1)S(1)} fusion(bf16[512,8,8,128]{3,2,1,0:T(8,128)(2,1)} %copy.155, pred[4096]{0:T(1024)(128)(4,1)S(1)} %broadcast_bitcast_fusion.3), kind=kLoop, calls=%fused_computation.34.clone.1 | loop fusion | flops 4194304 | bytes 16781312 | tf_op jit(solution)/shard_map/while/body/eval_jaxpr/jit(_take)/select_n | solution.py:125
  272.7 5.7 fusion.142
  279.3 10.8 %gather_fusion = bf16[32,128,1024]{2,1,0:T(8,128)(2,1)} fusion(bf16[64,128,1024]{2,1,0:T(8,128)(2,1)} %get-tuple-element.346, s32[1024]{0:T(1024)S(1)} %pad_clamp_fusion.7), kind=kCustom, calls=%fused_computation.clone.1 | custom fusion | bytes 16777344 | tf_op jit(solution)/shard_map/while/body/eval_jaxpr/jit(_take)/gather | solution.py:125
  290.1 8.8 %copy.155 = bf16[512,8,8,128]{3,2,1,0:T(8,128)(2,1)} copy(bf16[512,8,8,128]{3,1,2,0:T(8,128)(2,1)} %bitcast.173) | data formatting | bytes 16777216 | tf_op jit(solution)/shard_map/while
  299.6 16.5 %bitcast_select_fusion.3 = bf16[4096,8,128]{2,1,0:T(8,128)(2,1)S(1)} fusion(bf16[512,8,8,128]{3,2,1,0:T(8,128)(2,1)} %copy.155, pred[4096]{0:T(1024)(128)(4,1)S(1)} %broadcast_bitcast_fusion.3), kind=kLoop, calls=%fused_computation.34.clone.1 | loop fusion | flops 4194304 | bytes 16781312 | tf_op jit(solution)/shard_map/while/body/eval_jaxpr/jit(_take)/select_n | solution.py:125
  325.2 5.7 fusion.142
  331.8 10.8 %gather_fusion = bf16[32,128,1024]{2,1,0:T(8,128)(2,1)} fusion(bf16[64,128,1024]{2,1,0:T(8,128)(2,1)} %get-tuple-element.346, s32[1024]{0:T(1024)S(1)} %pad_clamp_fusion.7), kind=kCustom, calls=%fused_computation.clone.1 | custom fusion | bytes 16777344 | tf_op jit(solution)/shard_map/while/body/eval_jaxpr/jit(_take)/gather | solution.py:125
  342.6 8.8 %copy.155 = bf16[512,8,8,128]{3,2,1,0:T(8,128)(2,1)} copy(bf16[512,8,8,128]{3,1,2,0:T(8,128)(2,1)} %bitcast.173) | data formatting | bytes 16777216 | tf_op jit(solution)/shard_map/while
  352.1 16.5 %bitcast_select_fusion.3 = bf16[4096,8,128]{2,1,0:T(8,128)(2,1)S(1)} fusion(bf16[512,8,8,128]{3,2,1,0:T(8,128)(2,1)} %copy.155, pred[4096]{0:T(1024)(128)(4,1)S(1)} %broadcast_bitcast_fusion.3), kind=kLoop, calls=%fused_computation.34.clone.1 | loop fusion | flops 4194304 | bytes 16781312 | tf_op jit(solution)/shard_map/while/body/eval_jaxpr/jit(_take)/select_n | solution.py:125
  377.6 5.7 fusion.142
  384.3 10.8 %gather_fusion = bf16[32,128,1024]{2,1,0:T(8,128)(2,1)} fusion(bf16[64,128,1024]{2,1,0:T(8,128)(2,1)} %get-tuple-element.346, s32[1024]{0:T(1024)S(1)} %pad_clamp_fusion.7), kind=kCustom, calls=%fused_computation.clone.1 | custom fusion | bytes 16777344 | tf_op jit(solution)/shard_map/while/body/eval_jaxpr/jit(_take)/gather | solution.py:125
  395.0 8.8 %copy.155 = bf16[512,8,8,128]{3,2,1,0:T(8,128)(2,1)} copy(bf16[512,8,8,128]{3,1,2,0:T(8,128)(2,1)} %bitcast.173) | data formatting | bytes 16777216 | tf_op jit(solution)/shard_map/while
  404.6 16.5 %bitcast_select_fusion.3 = bf16[4096,8,128]{2,1,0:T(8,128)(2,1)S(1)} fusion(bf16[512,8,8,128]{3,2,1,0:T(8,128)(2,1)} %copy.155, pred[4096]{0:T(1024)(128)(4,1)S(1)} %broadcast_bitcast_fusion.3), kind=kLoop, calls=%fused_computation.34.clone.1 | loop fusion | flops 4194304 | bytes 16781312 | tf_op jit(solution)/shard_map/while/body/eval_jaxpr/jit(_take)/select_n | solution.py:125
  430.1 5.7 fusion.142
  436.7 10.8 %gather_fusion = bf16[32,128,1024]{2,1,0:T(8,128)(2,1)} fusion(bf16[64,128,1024]{2,1,0:T(8,128)(2,1)} %get-tuple-element.346, s32[1024]{0:T(1024)S(1)} %pad_clamp_fusion.7), kind=kCustom, calls=%fused_computation.clone.1 | custom fusion | bytes 16777344 | tf_op jit(solution)/shard_map/while/body/eval_jaxpr/jit(_take)/gather | solution.py:125
  447.5 8.8 %copy.155 = bf16[512,8,8,128]{3,2,1,0:T(8,128)(2,1)} copy(bf16[512,8,8,128]{3,1,2,0:T(8,128)(2,1)} %bitcast.173) | data formatting | bytes 16777216 | tf_op jit(solution)/shard_map/while
  457.0 16.5 %bitcast_select_fusion.3 = bf16[4096,8,128]{2,1,0:T(8,128)(2,1)S(1)} fusion(bf16[512,8,8,128]{3,2,1,0:T(8,128)(2,1)} %copy.155, pred[4096]{0:T(1024)(128)(4,1)S(1)} %broadcast_bitcast_fusion.3), kind=kLoop, calls=%fused_computation.34.clone.1 | loop fusion | flops 4194304 | bytes 16781312 | tf_op jit(solution)/shard_map/while/body/eval_jaxpr/jit(_take)/select_n | solution.py:125
  482.6 5.7 fusion.142
  489.2 10.8 %gather_fusion = bf16[32,128,1024]{2,1,0:T(8,128)(2,1)} fusion(bf16[64,128,1024]{2,1,0:T(8,128)(2,1)} %get-tuple-element.346, s32[1024]{0:T(1024)S(1)} %pad_clamp_fusion.7), kind=kCustom, calls=%fused_computation.clone.1 | custom fusion | bytes 16777344 | tf_op jit(solution)/shard_map/while/body/eval_jaxpr/jit(_take)/gather | solution.py:125
  500.0 8.8 %copy.155 = bf16[512,8,8,128]{3,2,1,0:T(8,128)(2,1)} copy(bf16[512,8,8,128]{3,1,2,0:T(8,128)(2,1)} %bitcast.173) | data formatting | bytes 16777216 | tf_op jit(solution)/shard_map/while
  509.5 16.5 %bitcast_select_fusion.3 = bf16[4096,8,128]{2,1,0:T(8,128)(2,1)S(1)} fusion(bf16[512,8,8,128]{3,2,1,0:T(8,128)(2,1)} %copy.155, pred[4096]{0:T(1024)(128)(4,1)S(1)} %broadcast_bitcast_fusion.3), kind=kLoop, calls=%fused_computation.34.clone.1 | loop fusion | flops 4194304 | bytes 16781312 | tf_op jit(solution)/shard_map/while/body/eval_jaxpr/jit(_take)/select_n | solution.py:125
  535.0 5.7 fusion.142
  541.6 10.8 %gather_fusion = bf16[32,128,1024]{2,1,0:T(8,128)(2,1)} fusion(bf16[64,128,1024]{2,1,0:T(8,128)(2,1)} %get-tuple-element.346, s32[1024]{0:T(1024)S(1)} %pad_clamp_fusion.7), kind=kCustom, calls=%fused_computation.clone.1 | custom fusion | bytes 16777344 | tf_op jit(solution)/shard_map/while/body/eval_jaxpr/jit(_take)/gather | solution.py:125
  552.4 8.8 %copy.155 = bf16[512,8,8,128]{3,2,1,0:T(8,128)(2,1)} copy(bf16[512,8,8,128]{3,1,2,0:T(8,128)(2,1)} %bitcast.173) | data formatting | bytes 16777216 | tf_op jit(solution)/shard_map/while
  562.0 16.5 %bitcast_select_fusion.3 = bf16[4096,8,128]{2,1,0:T(8,128)(2,1)S(1)} fusion(bf16[512,8,8,128]{3,2,1,0:T(8,128)(2,1)} %copy.155, pred[4096]{0:T(1024)(128)(4,1)S(1)} %broadcast_bitcast_fusion.3), kind=kLoop, calls=%fused_computation.34.clone.1 | loop fusion | flops 4194304 | bytes 16781312 | tf_op jit(solution)/shard_map/while/body/eval_jaxpr/jit(_take)/select_n | solution.py:125
  587.5 5.7 fusion.142
  600.1 9.3 %all-to-all-done.1 = bf16[8,2,10240]{2,1,0:T(2,128)(2,1)S(1)} async-done(((bf16[8,2,10240]{2,1,0:T(2,128)(2,1)}), bf16[8,2,10240]{2,1,0:T(2,128)(2,1)S(1)}, u32[]{:S(2)}, u32[]{:S(2)}) %all-to-all-start.1) | async-done | bytes 327712 | tf_op jit(solution)/shard_map/all_to_all | solution.py:160
  622.9 15.9 %fusion = bf16[72,2048]{1,0:T(8,128)(2,1)S(1)} fusion(bf16[264,2048]{1,0:T(8,128)(2,1)} %convolution_convert_fusion.1), kind=kCustom, calls=%all-reduce-scatter | all-reduce-scatter fusion | flops 589825 | bytes 1376768
  645.5 11.7 %fusion.83 = (bf16[2048,1,640]{2,1,0:T(2,128)(2,1)}, bf16[2048,1,640]{2,1,0:T(2,128)(2,1)}) fusion(bf16[2048,2,640]{2,1,0:T(2,128)(2,1)} %param.26), kind=kLoop, calls=%fused_computation.159 | loop fusion | bytes 10485760 | tf_op jit(solution)/shard_map/slice | solution.py:189
  657.2 42.0 %all-gather.3.cloned.1.call-done = bf16[8,66,2048]{2,1,0:T(8,128)(2,1)} async-done(((bf16[1,66,2048]{2,1,0:T(8,128)(2,1)}), bf16[8,66,2048]{2,1,0:T(8,128)(2,1)}) %all-gather.3.cloned.1.call-update) | async-done | bytes 2162704 | tf_op jit(solution)/shard_map/all_gather | solution.py:188
  702.1 6.1 fusion.52
  708.2 9.0 %convolution_convert_fusion = bf16[528,2048]{1,0:T(8,128)(2,1)} fusion(bf16[640,2048]{1,0:T(8,128)(2,1)S(1)} %copy-done, bf16[528,2048]{1,0:T(8,128)(2,1)} %reshape.355, bf16[2048,1,640]{2,1,0:T(2,128)(2,1)} %get-tuple-element.162, f32[528,640]{1,0:T(8,128)} %fusion.52), kind=kOutput, calls=%fused_computation.69 | convolution fusion | flops 2772701184 | bytes 10919936 | tf_op jit(solution)/shard_map/dot_general | solution.py:193
  717.2 101.7 %all-reduce.4.cloned.1.call-done = bf16[528,2048]{1,0:T(8,128)(2,1)} async-done(((bf16[528,2048]{1,0:T(8,128)(2,1)}), bf16[528,2048]{1,0:T(8,128)(2,1)}) %all-reduce.4.cloned.1.call-update) | async-done | bytes 2162704 | tf_op jit(solution)/shard_map/psum | solution.py:192
  (329 shorter events, 224.8 us)
Async XLA Ops:
  7.2 701.0 %copy-start = (bf16[640,2048]{1,0:T(8,128)(2,1)S(1)}, bf16[640,2048]{1,0:T(8,128)(2,1)}, u32[]{:S(2)}) copy-start(bf16[640,2048]{1,0:T(8,128)(2,1)} %param.27) | copy-start | bytes 7864324
  7.2 10.5 %copy-start.7 = (bf16[8,2048]{1,0:T(8,128)(2,1)S(1)}, bf16[8,2048]{1,0:T(8,128)(2,1)}, u32[]{:S(2)}) copy-start(bf16[8,2048]{1,0:T(8,128)(2,1)} %param.21) | copy-start | bytes 98308
  7.2 10.7 %copy-start.8 = (f32[2048]{0:T(1024)S(1)}, f32[2048]{0:T(1024)}, u32[]{:S(2)}) copy-start(f32[2048]{0:T(1024)} %param.22) | copy-start | bytes 24580
  19.5 5.6 copy-start.14
  19.5 6.3 copy-start.13
  24.2 0.9 copy-start.5
  27.1 7.1 slice-start
  39.3 14.1 %copy-start.17 = (s32[1,48]{1,0:T(1,128)S(1)}, s32[1,48]{1,0:T(1,128)}, u32[]{:S(2)}) copy-start(s32[1,48]{1,0:T(1,128)} %param.29) | copy-start | bytes 580
  45.5 32.3 %all-to-all-start = ((bf16[8,2,30720]{2,1,0:T(2,128)(2,1)}), bf16[8,2,30720]{2,1,0:T(2,128)(2,1)}, u32[]{:S(2)}, u32[]{:S(2)}) async-start(bf16[8,2,30720]{2,1,0:T(2,128)(2,1)} %reshape.363), calls=%async_computation | async-start | bytes 1966080 | tf_op jit(solution)/shard_map/all_to_all | solution.py:76
  96.2 1.8 copy-start.6
  98.0 75.5 %copy-start.18 = (s32[8]{0:T(128)S(1)}, s32[8]{0:T(128)}, u32[]{:S(2)}) copy-start(s32[8]{0:T(128)} %param.34) | copy-start | bytes 100
  101.3 2.9 copy-start.3
  103.5 3.8 copy-start.1
  110.9 4.5 copy-start.2
  119.5 2.9 copy-start.3
  121.7 3.8 copy-start.1
  129.1 4.5 copy-start.2
  137.6 2.9 copy-start.3
  139.8 3.8 copy-start.1
  147.2 4.5 copy-start.2
  155.8 2.9 copy-start.3
  158.0 3.8 copy-start.1
  165.4 4.5 copy-start.2
  593.4 5.6 copy-start.11
  593.4 5.6 copy-start.16
  593.4 5.7 copy-start.15
  595.4 14.0 %all-to-all-start.1 = ((bf16[8,2,10240]{2,1,0:T(2,128)(2,1)}), bf16[8,2,10240]{2,1,0:T(2,128)(2,1)S(1)}, u32[]{:S(2)}, u32[]{:S(2)}) async-start(bf16[8,2,10240]{2,1,0:T(2,128)(2,1)} %reshape.365), calls=%async_computation.1 | async-start | bytes 655360 | tf_op jit(solution)/shard_map/all_to_all | solution.py:160
  599.0 100.2 %all-gather.3.cloned.1.call-start = ((), (), s32[]{:S(2)}) async-start(), calls=%async_computation.3 | async-start | bytes 2654208 | tf_op jit(solution)/shard_map/all_gather | solution.py:188
  610.7 4.2 copy-start.10
  619.5 21.5 %copy-start.12 = (u32[32]{0:T(128)S(1)}, u32[32]{0:T(128)}, u32[]{:S(2)}) copy-start(u32[32]{0:T(128)} %constant.180) | copy-start | bytes 388
  619.5 25.0 %copy-start.9 = (f32[2048]{0:T(1024)S(1)}, f32[2048]{0:T(1024)}, u32[]{:S(2)}) copy-start(f32[2048]{0:T(1024)} %param.25) | copy-start | bytes 24580
  638.8 3.4 copy-start.4
  638.9 3.3 collective-permute-start
  645.4 173.4 %all-reduce.4.cloned.1.call-start = ((), (), s32[]{:S(2)}) async-start(), calls=%async_computation.2 | async-start | bytes 4325376 | tf_op jit(solution)/shard_map/psum | solution.py:192
Sparse Core Ops, SparseCore 0:
  645.5 53.5 all-gather.2
  717.3 101.5 all-reduce.3
where the time goes:
time: 838 us; the launch traced here: 829 us
  local copies, waits for them, and re-layouts  288 us (34%)
  other arithmetic  194 us (23%)
  waiting for transfers between devices  164 us (20%)
  matrix products  129 us (15%)
  blocking collectives  15.9 us (2%)
  between operations  15.6 us (2%)
  starting transfers between devices  12.8 us (2%)
  loops' own time  8.91 us (1%)
    select_n x16, other arithmetic, decode_one(): jnp.take(decode_pool, pages, axis=0).reshape(-1, heads_per, 2 * HD)  138 us
    psum x1, waiting for transfers between devices, shards(): lax.psum(jnp.dot(hidden, w_down, preferred_element_type=jnp.float32).asty...  102 us
    gather x8, local copies, waits for them, and re-layouts, decode_one(): jnp.take(decode_pool, pages, axis=0).reshape(-1, heads_per, 2 * HD)  86.3 us
    while x32, local copies, waits for them, and re-layouts  70.1 us
    dot_general x8, matrix products, decode_one(): jnp.einsum('hk,khd->hd', weights.astype(jnp.bfloat16), cache_slot[:, :, H...  45.5 us
    all_gather x1, waiting for transfers between devices, shards(): piece = lax.all_gather(normed_mid, 'tok', axis=0, tiled=True)  42 us
    slice x8, local copies, waits for them, and re-layouts, decode_one(): cache_slot[:, :, :HD]  39.2 us
    unnamed x44, local copies, waits for them, and re-layouts  30.5 us
  transfers between devices with their start and end apart: 5, of which 4 were waited for; matrix products, arithmetic and copies ran while one was open for 3% of the time, Pallas kernels for 0%

commit v1 on v0

v1 whole, which is shorter than its diff:
```python
import functools
import jax
import jax.numpy as jnp
from jax import lax
from jax.experimental import pallas as pl
from jax.experimental.pallas import tpu as pltpu
from jax.sharding import PartitionSpec as P

HD = 64
PAGE = 128
EPSILON = 1e-06
SCALE = 0.125
MASKED = -1e30
LOG2E = 1.4426950408889634
BLOCK = 512
F32 = jnp.float32
BF16 = jnp.bfloat16
VMEM = pl.BlockSpec(memory_space=pltpu.VMEM)
SMEM = pl.BlockSpec(memory_space=pltpu.SMEM)
ANY = pl.BlockSpec(memory_space=pl.ANY)


def contract_last(left, right):
    return lax.dot_general(left, right, (((1,), (1,)), ((), ())), preferred_element_type=F32)


def prefill_kernel(positions, n_pages, scal, pages, msg, pool, out, kv, queries, scores, top, acc, sems):
    blocks = msg.shape[0]
    stretch = blocks * positions
    half = positions // 2
    length = scal[0]
    used = pl.cdiv(length, BLOCK)
    cached = used * BLOCK
    per_chunk = BLOCK // PAGE
    n_copies = used * per_chunk

    def page_copy(index):
        page = pages[jnp.minimum(index, n_pages - 1)]
        return pltpu.make_async_copy(
            pool.at[page], kv.at[pl.ds(pl.multiple_of(index * PAGE, PAGE), PAGE), pl.ds(0, 2 * HD)], sems.at[index]
        )

    @pl.loop(0, n_copies)
    def _(index):
        page_copy(index).start()

    lane = lax.broadcasted_iota(jnp.int32, (positions, 4 * HD), 1)
    tail = lax.broadcasted_iota(jnp.int32, (half, 2 * HD), 1)
    one_hot = jnp.where(tail == 2 * HD - 1, 1.0, 0.0).astype(BF16)

    @pl.loop(0, blocks)
    def _(b):
        packed = msg[b, pl.ds(positions, half), :].astype(F32) * (SCALE * LOG2E)
        high = packed.astype(BF16)
        low = (packed - high.astype(F32)).astype(BF16)
        zero = jnp.zeros((half, HD), BF16)
        row = pl.multiple_of(b * positions, positions)
        for part in range(2):
            lanes = slice(part * HD, (part + 1) * HD)
            rows = pl.ds(row + part * half, half)
            queries[rows, 0 : 2 * HD] = jnp.concatenate([high[:, lanes], zero], axis=1)
            queries[rows, 2 * HD : 4 * HD] = jnp.where(
                tail < HD, jnp.concatenate([low[:, lanes], zero], axis=1), one_hot
            )
        own = msg[b, pl.ds(0, positions), :]
        spot = pl.multiple_of(cached + row, positions)
        kv[pl.ds(spot, positions), 0 : 2 * HD] = own
        side = lax.broadcasted_iota(jnp.int32, (positions, 2 * HD), 1)
        fill = jnp.where(side == 2 * HD - 1, 0.0, 1.0).astype(BF16)
        kv[pl.ds(spot, positions), 2 * HD : 4 * HD] = jnp.where(side < HD, own, fill)

    @pl.loop(0, n_copies)
    def _(index):
        page_copy(index).wait()
        rows = pl.ds(pl.multiple_of(index * PAGE, PAGE), PAGE)
        side = lax.broadcasted_iota(jnp.int32, (PAGE, 2 * HD), 1)
        place = index * PAGE + lax.broadcasted_iota(jnp.int32, (PAGE, 2 * HD), 0)
        bias = jnp.where(place < length, 0.0, MASKED)
        fill = jnp.where(side == 2 * HD - 1, bias, 1.0).astype(BF16)
        kv[rows, 2 * HD : 4 * HD] = jnp.where(side < HD, kv[rows, 0 : 2 * HD], fill)

    def chunk(c):
        return kv[pl.ds(pl.multiple_of(c * BLOCK, BLOCK), BLOCK), :]

    def raise_top(values):
        best = top[...]
        for k in range(BLOCK // 128):
            best = jnp.maximum(best, values[:, k * 128 : (k + 1) * 128])
        top[...] = best

    def score(i, c):
        values = contract_last(queries[pl.ds(pl.multiple_of(i * BLOCK, BLOCK), BLOCK), :], chunk(c))
        scores[c] = values
        raise_top(values)

    def score_diagonal(i):
        c = used + i
        values = contract_last(queries[pl.ds(pl.multiple_of(i * BLOCK, BLOCK), BLOCK), :], chunk(c))
        rows = lax.broadcasted_iota(jnp.int32, (BLOCK, BLOCK), 0)
        cols = lax.broadcasted_iota(jnp.int32, (BLOCK, BLOCK), 1)
        values = jnp.where(cols <= rows, values, MASKED)
        scores[c] = values
        raise_top(values)

    final = acc.at[1]
    total = acc.at[0]

    def settle():
        best = jnp.max(top[...], axis=1, keepdims=True)
        final[:, 0:128] = jnp.broadcast_to(best, (BLOCK, 128))
        top[...] = jnp.full_like(top, -jnp.inf)
        total[...] = jnp.zeros_like(total)

    def mix(c):
        best = final[:, 0:128]
        values = scores[c]
        weights = jnp.concatenate(
            [jnp.exp2(values[:, k * 128 : (k + 1) * 128] - best).astype(BF16) for k in range(BLOCK // 128)], axis=1
        )
        total[...] += jnp.dot(weights, chunk(c), preferred_element_type=F32)

    def emit(i):
        mixed = (total[:, HD : 2 * HD] / total[:, 3 * HD : 3 * HD + 1]).astype(BF16)
        for k in range(BLOCK // positions):
            part = mixed[k * positions : (k + 1) * positions]
            out[i * (BLOCK // positions) + k] = jnp.concatenate([part[:half], part[half:]], axis=1)

    top[...] = jnp.full_like(top, -jnp.inf)

    @pl.loop(0, used)
    def _(c):
        score(0, c)

    score_diagonal(0)
    settle()
    steps = stretch // BLOCK

    @pl.loop(1, steps)
    def _(i):
        @pl.loop(0, used + i)
        def _(c):
            mix(c)
            score(i, c)

        emit(i - 1)
        score_diagonal(i)
        settle()

    @pl.loop(0, used + steps)
    def _(c):
        mix(c)

    emit(steps - 1)


def prefill_attention(length, pages, msg, pool):
    blocks, rows, _ = msg.shape
    positions = rows * 2 // 3
    n_pages = pool.shape[0]
    stretch = blocks * positions
    chunks = pl.cdiv(n_pages * PAGE, BLOCK) + stretch // BLOCK
    keys = chunks * BLOCK
    return pl.pallas_call(
        functools.partial(prefill_kernel, positions, n_pages),
        out_shape=jax.ShapeDtypeStruct((blocks, positions // 2, 2 * HD), BF16),
        in_specs=[SMEM, SMEM, VMEM, ANY],
        out_specs=VMEM,
        scratch_shapes=[
            pltpu.VMEM((keys, 4 * HD), BF16),
            pltpu.VMEM((stretch, 4 * HD), BF16),
            pltpu.VMEM((chunks, BLOCK, BLOCK), F32),
            pltpu.VMEM((BLOCK, 128), F32),
            pltpu.VMEM((2, BLOCK, 4 * HD), F32),
            pltpu.SemaphoreType.DMA((pl.cdiv(n_pages * PAGE, BLOCK) * (BLOCK // PAGE),)),
        ],
        compiler_params=pltpu.CompilerParams(vmem_limit_bytes=48 * 2**20),
        cost_estimate=pl.CostEstimate(flops=4 * stretch * keys * HD, bytes_accessed=4 * 2**20, transcendentals=stretch * keys),
    )(length, pages, msg, pool)


def decode_kernel(heads, scal, pages, x, gain, w, pool, out, buf, wbuf, normed, qrows, cacherows, rowout, wsems, sems):
    slots = pages.shape[0]
    width = heads * 2 * HD
    per_group = BLOCK // PAGE
    depth = pages.shape[1]
    w_copies = [pltpu.make_async_copy(w.at[j], wbuf.at[j], wsems.at[j]) for j in range(3)]
    for copy in w_copies:
        copy.start()

    def groups(s):
        return pl.cdiv(scal[s], BLOCK)

    def page_copy(s, start, index):
        page = pages[s, jnp.minimum(index, depth - 1)]
        place = start * per_group + index
        return pltpu.make_async_copy(
            pool.at[page], buf.at[pl.ds(pl.multiple_of(place * PAGE, PAGE), PAGE), :], sems.at[place]
        )

    def begin(s, start):
        @pl.loop(0, groups(s) * per_group)
        def _(index):
            page_copy(s, start, index).start()

        return start + groups(s)

    lax.fori_loop(0, slots, begin, 0)
    values = x[...].astype(F32)
    inverse = lax.rsqrt(jnp.mean(values * values, axis=-1, keepdims=True) + EPSILON)
    normed[...] = (values * inverse * gain[...]).astype(BF16)
    rows = values.shape[0]
    zero = jnp.zeros((rows, HD), F32)
    parts = []
    for j in range(3):
        w_copies[j].wait()
        parts.append(jnp.dot(normed[...], wbuf[j], preferred_element_type=F32).astype(BF16).astype(F32))
    for g in range(heads):
        cut = slice(g * HD, (g + 1) * HD)
        span = slice(g * 2 * HD, (g + 1) * 2 * HD)
        qrows[:, span] = jnp.concatenate([parts[0][:, cut] * SCALE, zero], axis=1)
        cacherows[:, span] = jnp.concatenate([parts[1][:, cut], parts[2][:, cut]], axis=1)
    owner = lax.broadcasted_iota(jnp.int32, (8, width), 1) // (2 * HD)
    diagonal = owner == lax.broadcasted_iota(jnp.int32, (8, width), 0)

    def slot(s, start):
        row = scal[slots + s]
        length = scal[s]
        query = jnp.where(diagonal, jnp.broadcast_to(qrows[pl.ds(row, 1), :], (8, width)), 0.0)
        own = jnp.broadcast_to(cacherows[pl.ds(row, 1), :], (8, width))
        own_score = jnp.sum(query * own, axis=1, keepdims=True)
        query = query.astype(BF16)

        def step(g, carry):
            best, total, mixed = carry

            for k in range(per_group):
                page_copy(s, start, g * per_group + k).wait()
            cache = buf[pl.ds(pl.multiple_of((start + g) * BLOCK, BLOCK), BLOCK), :]
            values = contract_last(query, cache)
            place = g * BLOCK + lax.broadcasted_iota(jnp.int32, (8, BLOCK), 1)
            values = jnp.where(place < length, values, MASKED)
            newer = jnp.maximum(best, jnp.max(values, axis=1, keepdims=True))
            shrink = jnp.exp(best - newer)
            weights = jnp.exp(values - newer)
            total = total * shrink + jnp.sum(weights, axis=1, keepdims=True)
            mixed = mixed * shrink + jnp.dot(weights.astype(BF16), cache, preferred_element_type=F32)
            return newer, total, mixed

        best, total, mixed = lax.fori_loop(
            0, groups(s), step, (own_score, jnp.zeros((8, 1), F32), jnp.zeros((8, width), F32))
        )
        own_weight = jnp.exp(own_score - best)
        total = total + own_weight
        mixed = mixed + own_weight.astype(BF16).astype(F32) * own
        mixed = jnp.where(diagonal, mixed / total, 0.0)
        rowout[pl.ds(s, 1), :] = jnp.sum(mixed, axis=0, keepdims=True)
        return start + groups(s)

    lax.fori_loop(0, slots, slot, 0)
    done = rowout[...].astype(BF16)
    for g in range(0, heads, 2):
        out[:, g * HD : (g + 2) * HD] = jnp.concatenate(
            [done[:, g * 2 * HD + HD : (g + 1) * 2 * HD], done[:, (g + 1) * 2 * HD + HD : (g + 2) * 2 * HD]], axis=1
        )


def decode_attention(scal, pages, x, gain, w, pool):
    slots = pages.shape[0]
    features = w.shape[2]
    heads = features // HD
    width = heads * 2 * HD
    rows = x.shape[0]
    most = pool.shape[0] + slots * (BLOCK // PAGE - 1)
    return pl.pallas_call(
        functools.partial(decode_kernel, heads),
        out_shape=jax.ShapeDtypeStruct((slots, features), BF16),
        in_specs=[SMEM, SMEM, VMEM, VMEM, ANY, ANY],
        out_specs=VMEM,
        scratch_shapes=[
            pltpu.VMEM((most * PAGE, width), BF16),
            pltpu.VMEM(w.shape, BF16),
            pltpu.VMEM(x.shape, BF16),
            pltpu.VMEM((rows, width), F32),
            pltpu.VMEM((rows, width), F32),
            pltpu.VMEM((slots, width), F32),
            pltpu.SemaphoreType.DMA((3,)),
            pltpu.SemaphoreType.DMA((most,)),
        ],
        compiler_params=pltpu.CompilerParams(vmem_limit_bytes=48 * 2**20),
        cost_estimate=pl.CostEstimate(flops=2 * 10**9, bytes_accessed=22 * 2**20, transcendentals=10**6),
    )(scal, pages, x, gain, w, pool)


def qkv_kernel(requests, heads, home, x, gain, w, out, normed, keys):
    j = pl.program_id(0)
    rows = x.shape[0]
    positions = rows // requests
    half = positions // 2

    @pl.when(j == 0)
    def _():
        values = x[...].astype(F32)
        inverse = lax.rsqrt(jnp.mean(values * values, axis=-1, keepdims=True) + EPSILON)
        normed[...] = (values * inverse * gain[...]).astype(BF16)

    y = jnp.dot(normed[...], w[0], preferred_element_type=F32).astype(BF16)

    @pl.when(j == 0)
    def _():
        for r in range(requests):
            for g in range(heads):
                part = y[r * positions : (r + 1) * positions, g * HD : (g + 1) * HD]
                out[home[r * heads + g], positions : positions + half, :] = jnp.concatenate(
                    [part[:half], part[half:]], axis=1
                )

    @pl.when(j == 1)
    def _():
        keys[...] = y

    @pl.when(j == 2)
    def _():
        for r in range(requests):
            span = slice(r * positions, (r + 1) * positions)
            for g in range(heads):
                cut = slice(g * HD, (g + 1) * HD)
                out[home[r * heads + g], 0:positions, :] = jnp.concatenate([keys[span, cut], y[span, cut]], axis=1)


def qkv_messages(home, x, gain, w, requests):
    rows, width = x.shape
    features = w.shape[2]
    heads = features // HD
    units = requests * heads
    positions = rows // requests
    return pl.pallas_call(
        functools.partial(qkv_kernel, requests, heads),
        grid=(3,),
        out_shape=jax.ShapeDtypeStruct((units, positions * 3 // 2, 2 * HD), BF16),
        in_specs=[
            SMEM,
            pl.BlockSpec((rows, width), lambda j: (0, 0)),
            pl.BlockSpec((1, width), lambda j: (0, 0)),
            pl.BlockSpec((1, width, features), lambda j: (j, 0, 0)),
        ],
        out_specs=pl.BlockSpec((units, positions * 3 // 2, 2 * HD), lambda j: (0, 0, 0)),
        scratch_shapes=[pltpu.VMEM((rows, width), BF16), pltpu.VMEM((rows, features), BF16)],
        compiler_params=pltpu.CompilerParams(vmem_limit_bytes=32 * 2**20),
        cost_estimate=pl.CostEstimate(flops=2 * rows * width * 3 * features, bytes_accessed=10 * 2**20, transcendentals=0),
    )(home, x, gain, w)


def project_kernel(requests, heads, scal, received, gathered, w_out, *rest):
    outs, rows_in, decode_in = rest[:-2], rest[-2], rest[-1]
    n_head = len(outs)
    units = requests * heads
    per = outs[0].shape[0]
    half = received.shape[1]
    positions = 2 * half
    block_rows = positions // n_head
    share = per - requests * block_rows
    hosted = share * n_head
    decode_in[...] = gathered[...].astype(F32)
    rows_in[...] = jnp.zeros_like(rows_in)
    for r in range(requests):
        for g in range(0, heads, 2):
            left = received[scal[r * heads + g]].astype(F32)
            right = received[scal[r * heads + g + 1]].astype(F32)
            both = jnp.concatenate(
                [
                    jnp.concatenate([left[:, :HD], right[:, :HD]], axis=1),
                    jnp.concatenate([left[:, HD:], right[:, HD:]], axis=1),
                ],
                axis=0,
            )
            for h in range(n_head):
                rows_in[h, r * block_rows : (r + 1) * block_rows, g * HD : (g + 2) * HD] = both[
                    h * block_rows : (h + 1) * block_rows
                ]
    for j in range(hosted):
        rows_in[j // share, requests * block_rows + j % share, :] = decode_in[pl.ds(scal[units + j], 1), :][0]
    for k in range(n_head):
        mine = rows_in[scal[units + hosted + k]].astype(BF16)
        y = jnp.dot(mine, w_out[...], preferred_element_type=F32).astype(BF16)
        outs[k][...] = y[:per]


def project_out(scal, received, gathered, w_out, requests, heads, n_head, hosted):
    positions = 2 * received.shape[1]
    per = requests * (positions // n_head) + hosted // n_head
    padded = -(-per // 16) * 16
    features, width = w_out.shape
    return pl.pallas_call(
        functools.partial(project_kernel, requests, heads),
        out_shape=[jax.ShapeDtypeStruct((per, width), BF16)] * n_head,
        in_specs=[SMEM, VMEM, VMEM, VMEM],
        out_specs=[VMEM] * n_head,
        scratch_shapes=[pltpu.VMEM((n_head, padded, features), F32), pltpu.VMEM(gathered.shape, F32)],
        compiler_params=pltpu.CompilerParams(vmem_limit_bytes=32 * 2**20),
        cost_estimate=pl.CostEstimate(flops=2 * n_head * per * features * width, bytes_accessed=4 * 2**20, transcendentals=0),
    )(scal, received, gathered, w_out)


def feed_kernel(count, *refs):
    rows, (gate_up, down), outs = refs[:count], refs[count : count + 2], refs[count + 2 : 2 * count + 2]
    weights, down_weights, sems = refs[2 * count + 2 :]
    hidden_units = down.shape[0]
    tile = 128 if hidden_units % 128 == 0 else hidden_units
    steps = hidden_units // tile

    def load(step):
        cols = pl.ds(step * tile, tile)
        return pltpu.make_async_copy(gate_up.at[:, :, cols], weights.at[:, :, cols], sems.at[step])

    for step in range(steps):
        load(step).start()
    down_copy = pltpu.make_async_copy(down, down_weights, sems.at[steps])
    down_copy.start()
    hidden = [[] for _ in range(count)]
    for step in range(steps):
        load(step).wait()
        cols = slice(step * tile, (step + 1) * tile)
        both = jnp.concatenate([weights[0, :, cols], weights[1, :, cols]], axis=1) if tile == 128 else None
        for index in range(count):
            if tile == 128:
                y = jnp.dot(rows[index][...], both, preferred_element_type=F32)
                gate, upper = y[:, :tile], y[:, tile:]
            else:
                gate = jnp.dot(rows[index][...], weights[0], preferred_element_type=F32)
                upper = jnp.dot(rows[index][...], weights[1], preferred_element_type=F32)
            hidden[index].append((jax.nn.gelu(gate, approximate=True) * upper).astype(BF16))
    down_copy.wait()
    for index in range(count):
        full = jnp.concatenate(hidden[index], axis=1)
        outs[index][...] = jnp.dot(full, down_weights[...], preferred_element_type=F32).astype(BF16)


def feed_forward(chunks, gate_up, down):
    count = len(chunks)
    per, width = chunks[0].shape
    hidden_units = down.shape[0]
    return pl.pallas_call(
        functools.partial(feed_kernel, count),
        out_shape=[jax.ShapeDtypeStruct((per, width), BF16)] * count,
        in_specs=[VMEM] * count + [ANY, ANY],
        out_specs=[VMEM] * count,
        scratch_shapes=[
            pltpu.VMEM(gate_up.shape, BF16),
            pltpu.VMEM(down.shape, BF16),
            pltpu.SemaphoreType.DMA((hidden_units // 128 + 1,)),
        ],
        compiler_params=pltpu.CompilerParams(vmem_limit_bytes=32 * 2**20),
        cost_estimate=pl.CostEstimate(
            flops=6 * count * per * width * hidden_units, bytes_accessed=8 * 2**20, transcendentals=count * per * hidden_units
        ),
    )(*chunks, gate_up, down)


def ring_of(n_tok):
    if n_tok == 8:
        return [0, 2, 4, 6, 7, 5, 3, 1]
    return list(range(n_tok))


def shards(
    prefill_states,
    decode_states,
    attn_gain,
    w_qkv,
    w_out,
    ffn_gain,
    w_gate_up,
    w_down,
    prefill_pool,
    prefill_pages,
    prefill_lengths,
    prefill_home,
    decode_pool,
    decode_pages,
    decode_lengths,
    decode_home,
):
    n_tok = lax.axis_size("tok")
    n_head = lax.axis_size("head")
    my_tok = lax.axis_index("tok")
    my_head = lax.axis_index("head")
    requests, positions, width = prefill_states.shape
    hosted = decode_states.shape[0]
    features = w_qkv.shape[2]
    heads = features // HD
    units = requests * heads
    ring = ring_of(n_tok)
    ahead = [(ring[i], ring[(i + 1) % n_tok]) for i in range(n_tok)]
    behind = [(b, a) for a, b in ahead]
    far = n_tok // 2
    near = (n_tok - 1) // 2

    gain = attn_gain.reshape(1, width)
    w_three = jnp.transpose(w_qkv, (1, 0, 2))
    copies = jnp.broadcast_to(decode_states[None], (n_tok, hosted, width))
    all_decode = lax.all_to_all(copies, "tok", split_axis=0, concat_axis=0, tiled=True).reshape(n_tok * hosted, width)
    messages = qkv_messages(prefill_home, prefill_states.reshape(requests * positions, width), gain, w_three, requests)
    arrived = lax.all_to_all(messages, "tok", split_axis=0, concat_axis=0, tiled=True)

    slots = my_tok * hosted + jnp.arange(hosted, dtype=jnp.int32)
    all_requests = jnp.arange(decode_home.shape[0], dtype=jnp.int32)
    anchor = jnp.sum(jnp.where(decode_home[None, :] == slots[:, None], all_requests[None, :], 0), axis=1)
    decode_attn = decode_attention(
        jnp.concatenate([decode_lengths, anchor]), decode_pages, all_decode, gain, w_three, decode_pool
    )
    gathered = lax.all_gather(decode_attn, "tok", axis=0, tiled=True)
    gate_up = jnp.transpose(w_gate_up, (1, 0, 2))

    unit_ids = jnp.arange(units, dtype=jnp.int32)
    my_unit = jnp.sum(jnp.where(prefill_home == my_tok, unit_ids, 0))
    length = lax.dynamic_slice_in_dim(prefill_lengths, my_unit // heads, 1, 0)
    attn = prefill_attention(length, prefill_pages.reshape(-1), arrived, prefill_pool)
    returned = lax.all_to_all(attn, "tok", split_axis=0, concat_axis=0, tiled=True)

    my_slots = lax.dynamic_slice_in_dim(decode_home, my_tok * hosted, hosted, 0)
    targets = my_head ^ jnp.arange(n_head, dtype=jnp.int32)
    parts = project_out(
        jnp.concatenate([prefill_home, my_slots, targets]), returned, gathered, w_out, requests, heads, n_head, hosted
    )
    block_rows = positions // n_head
    share = hosted // n_head
    own_pre = lax.dynamic_slice_in_dim(prefill_states, my_head * block_rows, block_rows, 1)
    own_dec = lax.dynamic_slice_in_dim(decode_states, my_head * share, share, 0)
    resid = jnp.concatenate([own_pre.reshape(requests * block_rows, width), own_dec], axis=0).astype(F32)
    resid = resid + parts[0].astype(F32)
    for k in range(1, n_head):
        resid = resid + lax.ppermute(parts[k], "head", [(i, i ^ k) for i in range(n_head)]).astype(F32)
    mean = jnp.mean(resid * resid, axis=-1, keepdims=True)
    normed_mid = (resid * lax.rsqrt(mean + EPSILON) * ffn_gain).astype(BF16)

    plus, minus = {}, {}
    up, down = normed_mid, normed_mid
    (own_part,) = feed_forward([normed_mid], gate_up, w_down)
    for k in range(1, far + 1):
        up = lax.ppermute(up, "tok", ahead)
        if k <= near:
            down = lax.ppermute(down, "tok", behind)
            minus[k], plus[k] = feed_forward([up, down], gate_up, w_down)
        else:
            (minus[k],) = feed_forward([up], gate_up, w_down)
            plus[k] = minus[k]

    def joined(part, other):
        return (part.astype(F32) + other.astype(F32)).astype(BF16)

    up, down = plus[far], minus[near]
    for k in range(far - 1, 0, -1):
        up = joined(plus[k], lax.ppermute(up, "tok", ahead))
        if k < near:
            down = joined(minus[k], lax.ppermute(down, "tok", behind))
    up = lax.ppermute(up, "tok", ahead).astype(F32)
    down = lax.ppermute(down, "tok", behind).astype(F32)
    result = (resid + (own_part.astype(F32) + up + down)).astype(BF16)
    prefill_out = result[: requests * block_rows].reshape(requests, block_rows, width)
    return (prefill_out, result[requests * block_rows :])


def solution(mesh):
    placed = (
        P(None, "tok", None),
        P("tok", None),
        P(),
        P(None, None, "head"),
        P("head", None),
        P(),
        P(None, None, "tok"),
        P("tok", None),
        P("tok", None, "head"),
        P("tok", None),
        P(),
        P(),
        P("tok", None, "head"),
        P("tok", None),
        P("tok"),
        P(),
    )
    return jax.shard_map(
        shards,
        mesh=mesh,
        in_specs=placed,
        out_specs=(P(None, ("tok", "head"), None), P(("tok", "head"), None)),
        check_vma=False,
    )
```

time: 838 us -> 231 us (0.28); the launches traced: 829 us -> 230 us
  local copies, waits for them, and re-layouts: 288 us -> 13.1 us
  other arithmetic: 194 us -> 1.28 us
  matrix products: 129 us -> 0 us
  waiting for transfers between devices: 164 us -> 69 us
  Pallas kernels: 0 us -> 81 us
  starting transfers between devices: 12.8 us -> 33.3 us
  blocking collectives: 15.9 us -> 31.1 us
  between operations: 15.6 us -> 1.53 us
  loops' own time: 8.91 us -> 0 us
    select_n x23 -> x0, other arithmetic: 145 us -> none  [the longest x16 138 us: decode_one(): jnp.take(decode_pool, pages, axis=0).reshape(-1, heads_per, 2 * HD)]
    dot_general x36 -> x0, matrix products: 129 us -> none  [the longest x8 45.5 us: decode_one(): jnp.einsum('hk,khd->hd', weights.astype(jnp.bfloat16), cache_slot[:, :, H...]
    psum x1 -> x0, waiting for transfers between devices: 102 us -> none  [shards(): lax.psum(jnp.dot(hidden, w_down, preferred_element_type=jnp.float32).asty...]
    gather x15 -> x0, local copies, waits for them, and re-layouts: 94.8 us -> none  [the longest x8 86.3 us: decode_one(): jnp.take(decode_pool, pages, axis=0).reshape(-1, heads_per, 2 * HD)]
    pallas_call x0 -> x9, Pallas kernels: none -> 81 us  [the longest x1 34.3 us: prefill_attention(): pl.pallas_call(functools.partial(prefill_kernel, positions, n_pages), out...]
    while x33 -> x0, local copies, waits for them, and re-layouts: 70.4 us -> none
    slice x20 -> x1, local copies, waits for them, and re-layouts: 63.6 us -> 0.6 us  [shards(): return (prefill_out, result[requests * block_rows:])]
    ppermute x0 -> x17, waiting for transfers between devices: none -> 48.8 us  [the longest x4 22.5 us: shards(): up = lax.ppermute(up, 'tok', ahead)]
  transfers between devices with their start and end apart: 5 -> 20, of which waited for: 4 -> 11; matrix products, arithmetic and copies ran while one was open for 3% -> 2% of each run, Pallas kernels for 0% -> 32%
where the time goes in v1:
time: 231 us; the launch traced here: 230 us
  Pallas kernels  81 us (35%)
  waiting for transfers between devices  69 us (30%)
  starting transfers between devices  33.3 us (14%)
  blocking collectives  31.1 us (13%)
  local copies, waits for them, and re-layouts  13.1 us (6%)
    pallas_call x1, Pallas kernels, prefill_attention(): pl.pallas_call(functools.partial(prefill_kernel, positions, n_pages), out...  34.3 us
    all_gather x1, blocking collectives, shards(): gathered = lax.all_gather(decode_attn, 'tok', axis=0, tiled=True)  31.1 us
    ppermute x4, waiting for transfers between devices, shards(): up = lax.ppermute(up, 'tok', ahead)  22.5 us
    pallas_call x5, Pallas kernels, feed_forward(): pl.pallas_call(functools.partial(feed_kernel, count), out_shape=[jax.Shap...  22.1 us
    all_to_all x1, waiting for transfers between devices, shards(): lax.all_to_all(messages, 'tok', split_axis=0, concat_axis=0, tiled=True)  20.2 us
    pallas_call x1, Pallas kernels, decode_attention(): pl.pallas_call(functools.partial(decode_kernel, heads), out_shape=jax.Sha...  17.9 us
    ppermute x2, waiting for transfers between devices, shards(): down = joined(minus[k], lax.ppermute(down, 'tok', behind))  13.3 us
    ppermute x3, waiting for transfers between devices, shards(): lax.ppermute(parts[k], 'head', [(i, i ^ k) for i in range(n_head)])  12.4 us
  transfers between devices with their start and end apart: 20, of which 11 were waited for; matrix products, arithmetic and copies ran while one was open for 2% of the time, Pallas kernels for 32%

profile of v1, /device:TPU:0, one launch (start us, length us, event | category | flops | bytes accessed | tf_op | source)
XLA Modules:
  0.0 230.2 jit_solution(8464042851653042621)
XLA Ops:
  0.6 2.8 %copy-done.1 = bf16[2048,3,512]{2,0,1:T(8,128)(2,1)S(1)} copy-done((bf16[2048,3,512]{2,0,1:T(8,128)(2,1)S(1)}, bf16[2048,3,512]{2,0,1:T(8,128)(2,1)}, u32[]{:S(2)}) %copy-start.1) | copy-done | bytes 6291480
  3.4 1.2 copy-done.3
  4.6 0.7 copy-done.4
  5.3 0.7 copy-done.7
  6.0 4.4 %shard_map.167 = bf16[8,384,128]{2,1,0:T(8,128)(2,1)} custom-call(s32[8]{0:T(128)S(1)} %copy-done.7, bf16[256,2048]{1,0:T(8,128)(2,1)S(1)} %bitcast.19, f32[1,2048]{1,0:T(1,128)S(1)} %bitcast.21, bf16[3,2048,512]{2,1,0:T(8,128)(2,1)S(1)} %bitcast.18), custom_call_target="tpu_custom_call" | custom-call | flops 1610612736 | bytes 10485760 | tf_op jit(solution)/shard_map/pallas_call | solution.py:336
  10.4 7.3 %all-to-all-start = ((bf16[8,384,128]{2,1,0:T(8,128)(2,1)}), bf16[8,384,128]{2,1,0:T(8,128)(2,1)S(1)}, u32[]{:S(2)}, u32[]{:S(2)}) async-start(bf16[8,384,128]{2,1,0:T(8,128)(2,1)} %shard_map.167), calls=%async_computation | async-start | bytes 1572864 | tf_op jit(solution)/shard_map/all_to_all | solution.py:503
  17.7 20.2 %all-to-all-done.msg = bf16[8,384,128]{2,1,0:T(8,128)(2,1)S(1)} async-done(((bf16[8,384,128]{2,1,0:T(8,128)(2,1)}), bf16[8,384,128]{2,1,0:T(8,128)(2,1)S(1)}, u32[]{:S(2)}, u32[]{:S(2)}) %all-to-all-start) | async-done | bytes 786464 | tf_op jit(solution)/shard_map/all_to_all | solution.py:503
  37.8 0.7 broadcast_in_dim.18
  38.5 3.6 %all-to-all-start.2 = ((bf16[8,8,2048]{2,1,0:T(8,128)(2,1)}), bf16[8,8,2048]{2,1,0:T(8,128)(2,1)S(1)}, u32[]{:S(2)}, u32[]{:S(2)}) async-start(bf16[8,8,2048]{2,1,0:T(8,128)(2,1)} %broadcast_in_dim.18), calls=%async_computation.2 | async-start | bytes 524288 | tf_op jit(solution)/shard_map/all_to_all | solution.py:501
  42.9 1.4 copy-done.9
  44.3 34.3 %shard_map.168 = bf16[8,128,128]{2,1,0:T(8,128)(2,1)} custom-call(s32[1]{0:T(128)S(6)} %copy.22.scal, s32[48]{0:T(128)S(1)} %bitcast.23, bf16[8,384,128]{2,1,0:T(8,128)(2,1)S(1)} %all-to-all-done.msg, bf16[48,128,128]{2,1,0:T(8,128)(2,1)S(1)} %copy-done.9), custom_call_target="tpu_custom_call" | custom-call | flops 4294967296 | bytes 4194304 | tf_op jit(solution)/shard_map/pallas_call | solution.py:163
  78.6 6.0 %all-to-all-start.1 = ((bf16[8,128,128]{2,1,0:T(8,128)(2,1)}), bf16[8,128,128]{2,1,0:T(8,128)(2,1)S(1)}, u32[]{:S(2)}, u32[]{:S(2)}) async-start(bf16[8,128,128]{2,1,0:T(8,128)(2,1)} %shard_map.168), calls=%async_computation.1 | async-start | bytes 524288 | tf_op jit(solution)/shard_map/all_to_all | solution.py:518
  85.0 17.9 %shard_map.169 = bf16[8,512]{1,0:T(8,128)(2,1)S(1)} custom-call(s32[16]{0:T(128)S(1)} %pad_add_fusion.1.scal, s32[8,32]{1,0:T(8,128)S(1)} %copy-done.6, bf16[64,2048]{1,0:T(8,128)(2,1)S(1)} %bitcast.20, f32[1,2048]{1,0:T(1,128)S(1)} %bitcast.22, bf16[3,2048,512]{2,1,0:T(8,128)(2,1)} %bitcast.17, bf16[64,128,1024]{2,1,0:T(8,128)(2,1)} %pool.3), custom_call_target="tpu_custom_call" | custom-call | flops 2000000000 | bytes 23068672 | tf_op jit(solution)/shard_map/pallas_call | solution.py:274
  102.9 31.1 %all_gather.3.gathered = bf16[64,512]{1,0:T(8,128)(2,1)S(1)} all-gather(bf16[8,512]{1,0:T(8,128)(2,1)S(1)} %shard_map.169), channel_id=1, replica_groups=mesh['tok'=8,'head'=4] {'tok'}, dimensions={0}, use_global_device_ids=true | all-gather | bytes 73728 | tf_op jit(solution)/shard_map/all_gather | solution.py:511
  134.1 2.3 shard_map.170
  136.4 1.6 collective-permute-start.1
  137.9 0.3 collective-permute-start.2
  138.3 1.0 dynamic-slice_bitcast_fusion
  139.3 7.0 %collective-permute-done.1 = bf16[66,2048]{1,0:T(8,128)(2,1)S(1)} collective-permute-done((bf16[66,2048]{1,0:T(8,128)(2,1)S(1)}, bf16[66,2048]{1,0:T(8,128)(2,1)S(1)}, u32[]{:S(2)}, u32[]{:S(2)}) %collective-permute-start.1) | collective-permute-done | bytes 270368 | tf_op jit(solution)/shard_map/ppermute | solution.py:532
  146.3 5.4 %collective-permute-done.2 = bf16[66,2048]{1,0:T(8,128)(2,1)S(1)} collective-permute-done((bf16[66,2048]{1,0:T(8,128)(2,1)S(1)}, bf16[66,2048]{1,0:T(8,128)(2,1)S(1)}, u32[]{:S(2)}, u32[]{:S(2)}) %collective-permute-start.2) | collective-permute-done | bytes 270368 | tf_op jit(solution)/shard_map/ppermute | solution.py:532
  151.7 0.3 multiply_reduce_fusion
  152.2 9.2 %collective-permute-done.3.refs_0_ = bf16[66,2048]{1,0:T(8,128)(2,1)S(1)} collective-permute-done((bf16[66,2048]{1,0:T(8,128)(2,1)S(1)}, bf16[66,2048]{1,0:T(8,128)(2,1)S(1)}, u32[]{:S(2)}, u32[]{:S(2)}) %collective-permute-start.3) | collective-permute-done | bytes 270368 | tf_op jit(solution)/shard_map/ppermute | solution.py:540
  161.4 0.3 collective-permute-start.5
  161.7 1.7 collective-permute-start.4
  163.4 6.3 %collective-permute-done.5.refs_0_ = bf16[66,2048]{1,0:T(8,128)(2,1)S(1)} collective-permute-done((bf16[66,2048]{1,0:T(8,128)(2,1)S(1)}, bf16[66,2048]{1,0:T(8,128)(2,1)S(1)}, u32[]{:S(2)}, u32[]{:S(2)}) %collective-permute-start.5) | collective-permute-done | bytes 270368 | tf_op jit(solution)/shard_map/ppermute | solution.py:540
  169.8 0.6 collective-permute-start.7
  170.4 1.4 collective-permute-start.6
  171.8 5.4 %collective-permute-done.7.refs_0_ = bf16[66,2048]{1,0:T(8,128)(2,1)S(1)} collective-permute-done((bf16[66,2048]{1,0:T(8,128)(2,1)S(1)}, bf16[66,2048]{1,0:T(8,128)(2,1)S(1)}, u32[]{:S(2)}, u32[]{:S(2)}) %collective-permute-start.7) | collective-permute-done | bytes 270368 | tf_op jit(solution)/shard_map/ppermute | solution.py:540
  177.2 1.0 collective-permute-start.9
  178.2 1.1 collective-permute-start.8
  179.3 3.1 %copy.21 = bf16[2048,2,640]{2,0,1:T(8,128)(2,1)S(1)} copy(bf16[2048,2,640]{2,1,0:T(2,128)(2,1)} %param.22) | data formatting | bytes 10485760 | tf_op args[6]
  182.4 1.5 collective-permute-done.9.refs_0_
  184.0 4.0 %shard_map.175 = bf16[66,2048]{1,0:T(8,128)(2,1)S(1)} custom-call(bf16[66,2048]{1,0:T(8,128)(2,1)S(1)} %collective-permute-done.9.refs_0_, bf16[2,2048,640]{2,1,0:T(8,128)(2,1)S(1)} %bitcast.12, bf16[640,2048]{1,0:T(8,128)(2,1)S(1)} %copy-done), custom_call_target="tpu_custom_call" | custom-call | flops 519045120 | bytes 8388608 | tf_op jit(solution)/shard_map/pallas_call | solution.py:442
  187.9 1.4 collective-permute-start.10
  189.3 4.7 %shard_map.172 = (bf16[66,2048]{1,0:T(8,128)(2,1)S(1)}, bf16[66,2048]{1,0:T(8,128)(2,1)S(1)}) custom-call(bf16[66,2048]{1,0:T(8,128)(2,1)S(1)} %collective-permute-done.3.refs_0_, bf16[66,2048]{1,0:T(8,128)(2,1)S(1)} %collective-permute-done.4.refs_1_, bf16[2,2048,640]{2,1,0:T(8,128)(2,1)S(1)} %bitcast.13, bf16[640,2048]{1,0:T(8,128)(2,1)S(1)} %copy-done), custom_call_target="tpu_custom_call" | custom-call | flops 1038090240 | bytes 8388608 | tf_op jit(solution)/shard_map/pallas_call | solution.py:442
  194.0 4.7 %shard_map.173 = (bf16[66,2048]{1,0:T(8,128)(2,1)S(1)}, bf16[66,2048]{1,0:T(8,128)(2,1)S(1)}) custom-call(bf16[66,2048]{1,0:T(8,128)(2,1)S(1)} %collective-permute-done.5.refs_0_, bf16[66,2048]{1,0:T(8,128)(2,1)S(1)} %collective-permute-done.6.refs_1_, bf16[2,2048,640]{2,1,0:T(8,128)(2,1)S(1)} %bitcast.14, bf16[640,2048]{1,0:T(8,128)(2,1)S(1)} %copy-done), custom_call_target="tpu_custom_call" | custom-call | flops 1038090240 | bytes 8388608 | tf_op jit(solution)/shard_map/pallas_call | solution.py:442
  198.8 4.7 %shard_map.174 = (bf16[66,2048]{1,0:T(8,128)(2,1)S(1)}, bf16[66,2048]{1,0:T(8,128)(2,1)S(1)}) custom-call(bf16[66,2048]{1,0:T(8,128)(2,1)S(1)} %collective-permute-done.7.refs_0_, bf16[66,2048]{1,0:T(8,128)(2,1)S(1)} %collective-permute-done.8.refs_1_, bf16[2,2048,640]{2,1,0:T(8,128)(2,1)S(1)} %bitcast.15, bf16[640,2048]{1,0:T(8,128)(2,1)S(1)} %copy-done), custom_call_target="tpu_custom_call" | custom-call | flops 1038090240 | bytes 8388608 | tf_op jit(solution)/shard_map/pallas_call | solution.py:442
  203.6 1.0 collective-permute-start.14
  204.6 1.1 collective-permute-start.11
  205.8 6.1 %collective-permute-done.14 = bf16[66,2048]{1,0:T(8,128)(2,1)S(1)} collective-permute-done((bf16[66,2048]{1,0:T(8,128)(2,1)S(1)}, bf16[66,2048]{1,0:T(8,128)(2,1)S(1)}, u32[]{:S(2)}, u32[]{:S(2)}) %collective-permute-start.14) | collective-permute-done | bytes 270368 | tf_op jit(solution)/shard_map/ppermute | solution.py:555
  212.0 0.4 collective-permute-start.15
  212.5 1.9 collective-permute-start.12
  214.4 7.2 %collective-permute-done.15 = bf16[66,2048]{1,0:T(8,128)(2,1)S(1)} collective-permute-done((bf16[66,2048]{1,0:T(8,128)(2,1)S(1)}, bf16[66,2048]{1,0:T(8,128)(2,1)S(1)}, u32[]{:S(2)}, u32[]{:S(2)}) %collective-permute-start.15) | collective-permute-done | bytes 270368 | tf_op jit(solution)/shard_map/ppermute | solution.py:555
  221.8 2.5 %collective-permute-start.13 = (bf16[66,2048]{1,0:T(8,128)(2,1)S(1)}, bf16[66,2048]{1,0:T(8,128)(2,1)S(1)}, u32[]{:S(2)}, u32[]{:S(2)}) collective-permute-start(bf16[66,2048]{1,0:T(8,128)(2,1)S(1)} %add_convert_fusion.3), channel_id=1, source_target_pairs={{0,8},{8,16},{16,24},{24,28},{28,20},{20,12},{12,4},{4,0},{1,9},{9... | collective-permute-start | bytes 811016 | tf_op jit(solution)/shard_map/ppermute | solution.py:556
  224.3 3.9 %shard_map.171 = bf16[66,2048]{1,0:T(8,128)(2,1)S(1)} custom-call(bf16[66,2048]{1,0:T(8,128)(2,1)S(1)} %multiply_convert_fusion.refs_0_, bf16[2,2048,640]{2,1,0:T(8,128)(2,1)S(1)} %bitcast.16, bf16[640,2048]{1,0:T(8,128)(2,1)S(1)} %copy-done), custom_call_target="tpu_custom_call" | custom-call | flops 519045120 | bytes 8388608 | tf_op jit(solution)/shard_map/pallas_call | solution.py:442
  228.4 0.4 collective-permute-done.13
  228.9 0.7 slice_bitcast_fusion
  229.6 0.6 slice.9
  (53 shorter events, 1.5 us)
Async XLA Ops:
  0.6 2.8 %copy-start.1 = (bf16[2048,3,512]{2,0,1:T(8,128)(2,1)S(1)}, bf16[2048,3,512]{2,0,1:T(8,128)(2,1)}, u32[]{:S(2)}) copy-start(bf16[2048,3,512]{2,0,1:T(8,128)(2,1)} %param.19) | copy-start | bytes 18874372
  3.4 1.2 copy-start.3
  4.6 0.7 copy-start.4
  5.3 0.7 copy-start.7
  6.0 31.8 %copy-start.11 = (bf16[8,2048]{1,0:T(8,128)(2,1)S(1)}, bf16[8,2048]{1,0:T(8,128)(2,1)}, u32[]{:S(2)}) copy-start(bf16[8,2048]{1,0:T(8,128)(2,1)} %param.17) | copy-start | bytes 98308
  6.0 36.8 %copy-start.13 = (s32[64]{0:T(128)S(1)}, s32[64]{0:T(128)}, u32[]{:S(2)}) copy-start(s32[64]{0:T(128)} %param.31) | copy-start | bytes 772
  6.0 36.8 %copy-start.10 = (s32[1,48]{1,0:T(1,128)S(1)}, s32[1,48]{1,0:T(1,128)}, u32[]{:S(2)}) copy-start(s32[1,48]{1,0:T(1,128)} %param.25) | copy-start | bytes 580
  10.4 27.5 %all-to-all-start = ((bf16[8,384,128]{2,1,0:T(8,128)(2,1)}), bf16[8,384,128]{2,1,0:T(8,128)(2,1)S(1)}, u32[]{:S(2)}, u32[]{:S(2)}) async-start(bf16[8,384,128]{2,1,0:T(8,128)(2,1)} %shard_map.167), calls=%async_computation | async-start | bytes 1572864 | tf_op jit(solution)/shard_map/all_to_all | solution.py:503
  38.5 40.0 %all-to-all-start.2 = ((bf16[8,8,2048]{2,1,0:T(8,128)(2,1)}), bf16[8,8,2048]{2,1,0:T(8,128)(2,1)S(1)}, u32[]{:S(2)}, u32[]{:S(2)}) async-start(bf16[8,8,2048]{2,1,0:T(8,128)(2,1)} %broadcast_in_dim.18), calls=%async_computation.2 | async-start | bytes 524288 | tf_op jit(solution)/shard_map/all_to_all | solution.py:501
  42.9 1.4 copy-start.9
  44.3 40.3 %copy-start.8 = (s32[8]{0:T(128)S(1)}, s32[8]{0:T(128)}, u32[]{:S(2)}) copy-start(s32[8]{0:T(128)} %home.1) | copy-start | bytes 100
  44.3 40.6 %copy-start.14 = (s32[8]{0:T(128)S(1)}, s32[8]{0:T(128)}, u32[]{:S(2)}) copy-start(s32[8]{0:T(128)} %param.30) | copy-start | bytes 100
  44.3 40.7 %copy-start.5 = (f32[2048]{0:T(1024)S(1)}, f32[2048]{0:T(1024)}, u32[]{:S(2)}) copy-start(f32[2048]{0:T(1024)} %param.18) | copy-start | bytes 24580
  44.3 40.7 %copy-start.6 = (s32[8,32]{1,0:T(8,128)S(1)}, s32[8,32]{1,0:T(8,128)}, u32[]{:S(2)}) copy-start(s32[8,32]{1,0:T(8,128)} %pages.1) | copy-start | bytes 3076
  78.6 55.5 %all-to-all-start.1 = ((bf16[8,128,128]{2,1,0:T(8,128)(2,1)}), bf16[8,128,128]{2,1,0:T(8,128)(2,1)S(1)}, u32[]{:S(2)}, u32[]{:S(2)}) async-start(bf16[8,128,128]{2,1,0:T(8,128)(2,1)} %shard_map.168), calls=%async_computation.1 | async-start | bytes 524288 | tf_op jit(solution)/shard_map/all_to_all | solution.py:518
  84.9 49.1 %copy-start.2 = (bf16[512,2048]{1,0:T(8,128)(2,1)S(1)}, bf16[512,2048]{1,0:T(8,128)(2,1)}, u32[]{:S(2)}) copy-start(bf16[512,2048]{1,0:T(8,128)(2,1)} %w_out.1) | copy-start | bytes 6291460
  85.0 67.1 %copy-start.12 = (f32[2048]{0:T(1024)S(1)}, f32[2048]{0:T(1024)}, u32[]{:S(2)}) copy-start(f32[2048]{0:T(1024)} %param.21) | copy-start | bytes 24580
  136.3 2.9 %collective-permute-start = (bf16[66,2048]{1,0:T(8,128)(2,1)}, bf16[66,2048]{1,0:T(8,128)(2,1)S(1)}, u32[]{:S(2)}, u32[]{:S(2)}) collective-permute-start(bf16[66,2048]{1,0:T(8,128)(2,1)} %get-tuple-element.13), channel_id=1, source_target_pairs={{0,1},{1,0},{2,3},{3,2},{4,5},{5,4},{6,7},{7,6},{8,9},{9,8},{10,11... | collective-permute-start | bytes 811016 | tf_op jit(solution)/shard_map/ppermute | solution.py:532
  136.4 9.9 %collective-permute-start.1 = (bf16[66,2048]{1,0:T(8,128)(2,1)S(1)}, bf16[66,2048]{1,0:T(8,128)(2,1)S(1)}, u32[]{:S(2)}, u32[]{:S(2)}) collective-permute-start(bf16[66,2048]{1,0:T(8,128)(2,1)S(1)} %get-tuple-element.14), channel_id=1, source_target_pairs={{0,2},{1,3},{2,0},{3,1},{4,6},{5,7},{6,4},{7,5},{8,10},{9,11},{10,... | collective-permute-start | bytes 811016 | tf_op jit(solution)/shard_map/ppermute | solution.py:532
  137.9 13.7 %collective-permute-start.2 = (bf16[66,2048]{1,0:T(8,128)(2,1)S(1)}, bf16[66,2048]{1,0:T(8,128)(2,1)S(1)}, u32[]{:S(2)}, u32[]{:S(2)}) collective-permute-start(bf16[66,2048]{1,0:T(8,128)(2,1)S(1)} %get-tuple-element.15), channel_id=1, source_target_pairs={{0,3},{1,2},{2,1},{3,0},{4,7},{5,6},{6,5},{7,4},{8,11},{9,10},{10,... | collective-permute-start | bytes 811016 | tf_op jit(solution)/shard_map/ppermute | solution.py:532
  152.2 31.8 %copy-start = (bf16[640,2048]{1,0:T(8,128)(2,1)S(1)}, bf16[640,2048]{1,0:T(8,128)(2,1)}, u32[]{:S(2)}) copy-start(bf16[640,2048]{1,0:T(8,128)(2,1)} %refs_2_.3) | copy-start | bytes 7864324
  152.2 9.2 %collective-permute-start.3 = (bf16[66,2048]{1,0:T(8,128)(2,1)S(1)}, bf16[66,2048]{1,0:T(8,128)(2,1)S(1)}, u32[]{:S(2)}, u32[]{:S(2)}) collective-permute-start(bf16[66,2048]{1,0:T(8,128)(2,1)S(1)} %multiply_convert_fusion.refs_0_), channel_id=1, source_target_pairs={{0,8},{8,16},{16,24},{24,28},{28,20},{20,12},{12,4},{4,0},{1,9},{9... | collective-permute-start | bytes 811016 | tf_op jit(solution)/shard_map/ppermute | solution.py:540
  161.4 8.4 %collective-permute-start.5 = (bf16[66,2048]{1,0:T(8,128)(2,1)S(1)}, bf16[66,2048]{1,0:T(8,128)(2,1)S(1)}, u32[]{:S(2)}, u32[]{:S(2)}) collective-permute-start(bf16[66,2048]{1,0:T(8,128)(2,1)S(1)} %collective-permute-done.3.refs_0_), channel_id=1, source_target_pairs={{0,8},{8,16},{16,24},{24,28},{28,20},{20,12},{12,4},{4,0},{1,9},{9... | collective-permute-start | bytes 811016 | tf_op jit(solution)/shard_map/ppermute | solution.py:540
  161.7 8.7 %collective-permute-start.4 = (bf16[66,2048]{1,0:T(8,128)(2,1)S(1)}, bf16[66,2048]{1,0:T(8,128)(2,1)S(1)}, u32[]{:S(2)}, u32[]{:S(2)}) collective-permute-start(bf16[66,2048]{1,0:T(8,128)(2,1)S(1)} %multiply_convert_fusion.refs_0_), channel_id=1, source_target_pairs={{8,0},{16,8},{24,16},{28,24},{20,28},{12,20},{4,12},{0,4},{9,1},{1... | collective-permute-start | bytes 811016 | tf_op jit(solution)/shard_map/ppermute | solution.py:542
  169.8 7.5 %collective-permute-start.7 = (bf16[66,2048]{1,0:T(8,128)(2,1)S(1)}, bf16[66,2048]{1,0:T(8,128)(2,1)S(1)}, u32[]{:S(2)}, u32[]{:S(2)}) collective-permute-start(bf16[66,2048]{1,0:T(8,128)(2,1)S(1)} %collective-permute-done.5.refs_0_), channel_id=1, source_target_pairs={{0,8},{8,16},{16,24},{24,28},{28,20},{20,12},{12,4},{4,0},{1,9},{9... | collective-permute-start | bytes 811016 | tf_op jit(solution)/shard_map/ppermute | solution.py:540
  170.4 7.8 %collective-permute-start.6 = (bf16[66,2048]{1,0:T(8,128)(2,1)S(1)}, bf16[66,2048]{1,0:T(8,128)(2,1)S(1)}, u32[]{:S(2)}, u32[]{:S(2)}) collective-permute-start(bf16[66,2048]{1,0:T(8,128)(2,1)S(1)} %collective-permute-done.4.refs_1_), channel_id=1, source_target_pairs={{8,0},{16,8},{24,16},{28,24},{20,28},{12,20},{4,12},{0,4},{9,1},{1... | collective-permute-start | bytes 811016 | tf_op jit(solution)/shard_map/ppermute | solution.py:542
  177.2 6.7 %collective-permute-start.9 = (bf16[66,2048]{1,0:T(8,128)(2,1)S(1)}, bf16[66,2048]{1,0:T(8,128)(2,1)S(1)}, u32[]{:S(2)}, u32[]{:S(2)}) collective-permute-start(bf16[66,2048]{1,0:T(8,128)(2,1)S(1)} %collective-permute-done.7.refs_0_), channel_id=1, source_target_pairs={{0,8},{8,16},{16,24},{24,28},{28,20},{20,12},{12,4},{4,0},{1,9},{9... | collective-permute-start | bytes 811016 | tf_op jit(solution)/shard_map/ppermute | solution.py:540
  178.2 20.6 %collective-permute-start.8 = (bf16[66,2048]{1,0:T(8,128)(2,1)S(1)}, bf16[66,2048]{1,0:T(8,128)(2,1)S(1)}, u32[]{:S(2)}, u32[]{:S(2)}) collective-permute-start(bf16[66,2048]{1,0:T(8,128)(2,1)S(1)} %collective-permute-done.6.refs_1_), channel_id=1, source_target_pairs={{8,0},{16,8},{24,16},{28,24},{20,28},{12,20},{4,12},{0,4},{9,1},{1... | collective-permute-start | bytes 811016 | tf_op jit(solution)/shard_map/ppermute | solution.py:542
  187.9 16.6 %collective-permute-start.10 = (bf16[66,2048]{1,0:T(8,128)(2,1)S(1)}, bf16[66,2048]{1,0:T(8,128)(2,1)S(1)}, u32[]{:S(2)}, u32[]{:S(2)}) collective-permute-start(bf16[66,2048]{1,0:T(8,128)(2,1)S(1)} %shard_map.175), channel_id=1, source_target_pairs={{0,8},{8,16},{16,24},{24,28},{28,20},{20,12},{12,4},{4,0},{1,9},{9... | collective-permute-start | bytes 811016 | tf_op jit(solution)/shard_map/ppermute | solution.py:553
  203.6 8.3 %collective-permute-start.14 = (bf16[66,2048]{1,0:T(8,128)(2,1)S(1)}, bf16[66,2048]{1,0:T(8,128)(2,1)S(1)}, u32[]{:S(2)}, u32[]{:S(2)}) collective-permute-start(bf16[66,2048]{1,0:T(8,128)(2,1)S(1)} %get-tuple-element.21), channel_id=1, source_target_pairs={{8,0},{16,8},{24,16},{28,24},{20,28},{12,20},{4,12},{0,4},{9,1},{1... | collective-permute-start | bytes 811016 | tf_op jit(solution)/shard_map/ppermute | solution.py:555
  204.6 7.8 %collective-permute-start.11 = (bf16[66,2048]{1,0:T(8,128)(2,1)S(1)}, bf16[66,2048]{1,0:T(8,128)(2,1)S(1)}, u32[]{:S(2)}, u32[]{:S(2)}) collective-permute-start(bf16[66,2048]{1,0:T(8,128)(2,1)S(1)} %add_convert_fusion.5), channel_id=1, source_target_pairs={{0,8},{8,16},{16,24},{24,28},{28,20},{20,12},{12,4},{4,0},{1,9},{9... | collective-permute-start | bytes 811016 | tf_op jit(solution)/shard_map/ppermute | solution.py:553
  212.0 9.6 %collective-permute-start.15 = (bf16[66,2048]{1,0:T(8,128)(2,1)S(1)}, bf16[66,2048]{1,0:T(8,128)(2,1)S(1)}, u32[]{:S(2)}, u32[]{:S(2)}) collective-permute-start(bf16[66,2048]{1,0:T(8,128)(2,1)S(1)} %add_convert_fusion.2), channel_id=1, source_target_pairs={{8,0},{16,8},{24,16},{28,24},{20,28},{12,20},{4,12},{0,4},{9,1},{1... | collective-permute-start | bytes 811016 | tf_op jit(solution)/shard_map/ppermute | solution.py:555
  212.5 9.2 %collective-permute-start.12 = (bf16[66,2048]{1,0:T(8,128)(2,1)S(1)}, bf16[66,2048]{1,0:T(8,128)(2,1)S(1)}, u32[]{:S(2)}, u32[]{:S(2)}) collective-permute-start(bf16[66,2048]{1,0:T(8,128)(2,1)S(1)} %add_convert_fusion.4), channel_id=1, source_target_pairs={{0,8},{8,16},{16,24},{24,28},{28,20},{20,12},{12,4},{4,0},{1,9},{9... | collective-permute-start | bytes 811016 | tf_op jit(solution)/shard_map/ppermute | solution.py:553
  221.6 6.8 %collective-permute-start.16 = (bf16[66,2048]{1,0:T(8,128)(2,1)S(1)}, bf16[66,2048]{1,0:T(8,128)(2,1)S(1)}, u32[]{:S(2)}, u32[]{:S(2)}) collective-permute-start(bf16[66,2048]{1,0:T(8,128)(2,1)S(1)} %add_convert_fusion.1), channel_id=1, source_target_pairs={{8,0},{16,8},{24,16},{28,24},{20,28},{12,20},{4,12},{0,4},{9,1},{1... | collective-permute-start | bytes 811016 | tf_op jit(solution)/shard_map/ppermute | solution.py:557
  221.8 7.0 %collective-permute-start.13 = (bf16[66,2048]{1,0:T(8,128)(2,1)S(1)}, bf16[66,2048]{1,0:T(8,128)(2,1)S(1)}, u32[]{:S(2)}, u32[]{:S(2)}) collective-permute-start(bf16[66,2048]{1,0:T(8,128)(2,1)S(1)} %add_convert_fusion.3), channel_id=1, source_target_pairs={{0,8},{8,16},{16,24},{24,28},{28,20},{20,12},{12,4},{4,0},{1,9},{9... | collective-permute-start | bytes 811016 | tf_op jit(solution)/shard_map/ppermute | solution.py:556

commit v2 on v1

v2 whole, which is shorter than its diff:
```python
import functools
import jax
import jax.numpy as jnp
from jax import lax
from jax.experimental import pallas as pl
from jax.experimental.pallas import tpu as pltpu
from jax.sharding import PartitionSpec as P

HD = 64
PAGE = 128
EPSILON = 1e-06
SCALE = 0.125
MASKED = -1e30
LOG2E = 1.4426950408889634
BLOCK = 512
CHUNK = 1024
UNROLL = 2
AHEAD = 6
F32 = jnp.float32
BF16 = jnp.bfloat16
VMEM = pl.BlockSpec(memory_space=pltpu.VMEM)
SMEM = pl.BlockSpec(memory_space=pltpu.SMEM)
ANY = pl.BlockSpec(memory_space=pl.ANY)


def contract_last(left, right):
    return lax.dot_general(left, right, (((1,), (1,)), ((), ())), preferred_element_type=F32)


def cache_kernel(scal, pages, pool, flipped, values, raw, sems):
    length = scal[0]
    used = pl.cdiv(length, CHUNK)
    per_chunk = CHUNK // PAGE
    last = pages.shape[0] - 1

    def page_copy(index):
        page = pages[jnp.minimum(index, last)]
        return pltpu.make_async_copy(
            pool.at[page], raw.at[pl.ds(pl.multiple_of(index * PAGE, PAGE), PAGE), :], sems.at[index]
        )

    @pl.loop(0, used * per_chunk)
    def _(index):
        page_copy(index).start()

    @pl.loop(0, used)
    def _(c):
        for k in range(per_chunk):
            page_copy(c * per_chunk + k).wait()
        keys, mixed = doubled(raw[pl.ds(pl.multiple_of(c * CHUNK, CHUNK), CHUNK), :])
        flipped[c] = keys
        values[c] = mixed

        @pl.when(length - c * CHUNK < CHUNK)
        def _():
            valid = length - c * CHUNK
            columns = lax.broadcasted_iota(jnp.int32, keys.shape, 1) < valid
            flipped[c] = jnp.where(columns, keys, jnp.broadcast_to(keys[:, 0:1], keys.shape))
            inside = lax.broadcasted_iota(jnp.int32, mixed.shape, 0) < valid
            values[c] = jnp.where(inside, mixed, jnp.zeros_like(mixed))


def doubled(both):
    turned = both.T
    keys = jnp.concatenate([turned[:HD], turned[:HD]], axis=0)
    side = lax.broadcasted_iota(jnp.int32, both.shape, 1)
    return keys, jnp.where(side < HD, jnp.ones_like(both), both)


def prepare_cache(length, pages, pool):
    n_pages = pool.shape[0]
    chunks = pl.cdiv(n_pages * PAGE, CHUNK)
    return pl.pallas_call(
        cache_kernel,
        out_shape=[
            jax.ShapeDtypeStruct((chunks, 2 * HD, CHUNK), BF16),
            jax.ShapeDtypeStruct((chunks, CHUNK, 2 * HD), BF16),
        ],
        in_specs=[SMEM, SMEM, ANY],
        out_specs=[VMEM, VMEM],
        scratch_shapes=[
            pltpu.VMEM((chunks * CHUNK, 2 * HD), BF16),
            pltpu.SemaphoreType.DMA((chunks * (CHUNK // PAGE),)),
        ],
        compiler_params=pltpu.CompilerParams(vmem_limit_bytes=32 * 2**20),
        cost_estimate=pl.CostEstimate(flops=2 * 10**9, bytes_accessed=6 * 2**20, transcendentals=0),
    )(length, pages, pool)


def prefill_kernel(positions, scal, msg, old_flipped, old_values, decoded, out, flipped, values, queries, scores, top, total):
    blocks = msg.shape[0]
    stretch = blocks * positions
    half = positions // 2
    used = pl.cdiv(scal[0], CHUNK)
    steps = stretch // CHUNK

    @pl.loop(0, blocks)
    def _(b):
        packed = msg[b, pl.ds(positions, half), :].astype(F32) * (SCALE * LOG2E)
        high = packed.astype(BF16)
        low = (packed - high.astype(F32)).astype(BF16)
        row = pl.multiple_of(b * positions, positions)
        for part in range(2):
            lanes = slice(part * HD, (part + 1) * HD)
            queries[pl.ds(row + part * half, half), :] = jnp.concatenate([high[:, lanes], low[:, lanes]], axis=1)

    for c in range(steps):
        for k in range(CHUNK // positions):
            keys, mixed = doubled(msg[c * (CHUNK // positions) + k, 0:positions, :])
            flipped[c, :, k * positions : (k + 1) * positions] = keys
            values[c, k * positions : (k + 1) * positions, :] = mixed
    slots, features = decoded.shape
    for k in range(0, features // 128, 2):
        pair = jnp.concatenate([decoded[:, k * 128 : (k + 1) * 128], decoded[:, (k + 1) * 128 : (k + 2) * 128]], axis=0)
        pair = pair.astype(BF16)
        for b in range(blocks):
            out[b, half + k * slots : half + (k + 2) * slots, :] = pair

    def raise_top(s):
        best = top[...]
        for k in range(CHUNK // 128):
            best = jnp.maximum(best, s[:, k * 128 : (k + 1) * 128])
        top[...] = best

    def score(i, spot, keys, diagonal=False):
        q = queries[pl.ds(pl.multiple_of(i * CHUNK, CHUNK), CHUNK), :]
        s = jnp.dot(q, keys, preferred_element_type=F32)
        if diagonal:
            rows = lax.broadcasted_iota(jnp.int32, (CHUNK, CHUNK), 0)
            cols = lax.broadcasted_iota(jnp.int32, (CHUNK, CHUNK), 1)
            s = jnp.where(cols <= rows, s, MASKED)
        scores[spot] = s
        raise_top(s)

    def settle():
        best = jnp.max(top[...], axis=1, keepdims=True)
        total[1] = jnp.broadcast_to(best, (CHUNK, 128))
        top[...] = jnp.full_like(top, -jnp.inf)
        total[0] = jnp.zeros((CHUNK, 128), F32)

    def mix(spot, rows):
        best = total[1]
        s = scores[spot]
        weights = jnp.concatenate(
            [jnp.exp2(s[:, k * 128 : (k + 1) * 128] - best).astype(BF16) for k in range(CHUNK // 128)], axis=1
        )
        total[0] += jnp.dot(weights, rows, preferred_element_type=F32)

    def emit(i):
        done = total[0]
        mixed = (done[:, HD:] / done[:, :HD]).astype(BF16)
        for k in range(CHUNK // positions):
            part = mixed[k * positions : (k + 1) * positions]
            out[i * (CHUNK // positions) + k, 0:half, :] = jnp.concatenate([part[:half], part[half:]], axis=1)

    top[...] = jnp.full_like(top, -jnp.inf)

    @pl.loop(0, used)
    def _(c):
        score(0, c, old_flipped[c])

    score(0, used, flipped[0], diagonal=True)
    settle()

    @pl.loop(1, steps)
    def _(i):
        @pl.loop(0, used)
        def _(c):
            mix(c, old_values[c])
            score(i, c, old_flipped[c])

        @pl.loop(0, i)
        def _(c):
            mix(used + c, values[c])
            score(i, used + c, flipped[c])

        emit(i - 1)
        score(i, used + i, flipped[i], diagonal=True)
        settle()

    @pl.loop(0, used)
    def _(c):
        mix(c, old_values[c])

    @pl.loop(0, steps)
    def _(c):
        mix(used + c, values[c])

    emit(steps - 1)


def prefill_attention(length, msg, old_flipped, old_values, decoded):
    blocks, rows, _ = msg.shape
    positions = rows * 2 // 3
    stretch = blocks * positions
    steps = stretch // CHUNK
    chunks = old_values.shape[0] + steps
    slots, features = decoded.shape
    keys = chunks * CHUNK
    return pl.pallas_call(
        functools.partial(prefill_kernel, positions),
        out_shape=jax.ShapeDtypeStruct((blocks, positions // 2 + slots * features // 128, 2 * HD), BF16),
        in_specs=[SMEM, VMEM, VMEM, VMEM, VMEM],
        out_specs=VMEM,
        scratch_shapes=[
            pltpu.VMEM((steps, 2 * HD, CHUNK), BF16),
            pltpu.VMEM((steps, CHUNK, 2 * HD), BF16),
            pltpu.VMEM((stretch, 2 * HD), BF16),
            pltpu.VMEM((chunks, CHUNK, CHUNK), F32),
            pltpu.VMEM((CHUNK, 128), F32),
            pltpu.VMEM((2, CHUNK, 128), F32),
        ],
        compiler_params=pltpu.CompilerParams(vmem_limit_bytes=46 * 2**20),
        cost_estimate=pl.CostEstimate(flops=4 * stretch * keys * HD, bytes_accessed=4 * 2**20, transcendentals=stretch * keys),
    )(length, msg, old_flipped, old_values, decoded)


def decode_kernel(heads, scal, pages, x, gain, w, pool, out, buf, wbuf, normed, qrows, cacherows, rowout, bests, totals, mixes, owners, wsems, sems):
    slots = pages.shape[0]
    width = heads * 2 * HD
    per_group = BLOCK // PAGE
    depth = pages.shape[1]
    most = buf.shape[0] // BLOCK
    w_copies = [pltpu.make_async_copy(w.at[j], wbuf.at[j], wsems.at[j]) for j in range(3)]
    for copy in w_copies:
        copy.start()

    def page_copy(item, k):
        page = pages[owners[0, item], jnp.minimum(owners[2, item] * per_group + k, depth - 1)]
        place = item * per_group + k
        return pltpu.make_async_copy(
            pool.at[page], buf.at[pl.ds(pl.multiple_of(place * PAGE, PAGE), PAGE), :], sems.at[place]
        )

    def groups(s):
        return pl.cdiv(scal[s], BLOCK)

    @pl.loop(0, most + UNROLL)
    def _(item):
        owners[0, item] = 0
        owners[1, item] = 0
        owners[2, item] = 0

    def begin(s, start):
        @pl.loop(0, groups(s))
        def _(g):
            owners[0, start + g] = s
            owners[1, start + g] = scal[s] - g * BLOCK
            owners[2, start + g] = g

        return start + groups(s)

    items = lax.fori_loop(0, slots, begin, 0)

    def fetch(item):
        @pl.when(item < items)
        def _():
            for k in range(per_group):
                page_copy(item, k).start()

    for item in range(AHEAD):
        fetch(item)
    values = x[...].astype(F32)
    inverse = lax.rsqrt(jnp.mean(values * values, axis=-1, keepdims=True) + EPSILON)
    normed[...] = (values * inverse * gain[...]).astype(BF16)
    rows = values.shape[0]
    zero = jnp.zeros((rows, HD), F32)
    parts = []
    for j in range(3):
        w_copies[j].wait()
        parts.append(jnp.dot(normed[...], wbuf[j], preferred_element_type=F32).astype(BF16).astype(F32))
    for g in range(heads):
        cut = slice(g * HD, (g + 1) * HD)
        span = slice(g * 2 * HD, (g + 1) * 2 * HD)
        qrows[:, span] = jnp.concatenate([parts[0][:, cut] * SCALE, zero], axis=1)
        cacherows[:, span] = jnp.concatenate([parts[1][:, cut], parts[2][:, cut]], axis=1)
    owner = lax.broadcasted_iota(jnp.int32, (8, width), 1) // (2 * HD)
    diagonal = owner == lax.broadcasted_iota(jnp.int32, (8, width), 0)

    def spread(s):
        row = scal[slots + s]
        return jnp.where(diagonal, jnp.broadcast_to(qrows[pl.ds(row, 1), :], (8, width)), 0.0)

    @pl.loop(0, pl.cdiv(items, UNROLL))
    def _(turn):
        for u in range(UNROLL):
            @pl.when(turn * UNROLL + u < items)
            def _():
                for k in range(per_group):
                    page_copy(turn * UNROLL + u, k).wait()

            fetch(turn * UNROLL + u + AHEAD)
        for u in range(UNROLL):
            item = turn * UNROLL + u
            place = jnp.minimum(item, most - 1)
            cache = buf[pl.ds(pl.multiple_of(place * BLOCK, BLOCK), BLOCK), :]
            query = spread(owners[0, item]).astype(BF16)
            s = contract_last(query, cache)
            s = jnp.where(lax.broadcasted_iota(jnp.int32, (8, BLOCK), 1) < owners[1, item], s, MASKED)
            best = jnp.max(s, axis=1, keepdims=True)
            weights = jnp.exp(s - best)
            bests[item] = jnp.broadcast_to(best, (8, 128))
            totals[item] = jnp.broadcast_to(jnp.sum(weights, axis=1, keepdims=True), (8, 128))
            mixes[item] = jnp.dot(weights.astype(BF16), cache, preferred_element_type=F32)

    most_items = pl.cdiv(depth * PAGE, BLOCK)
    start = 0
    for s in range(slots):
        own = jnp.broadcast_to(cacherows[pl.ds(scal[slots + s], 1), :], (8, width))
        own_score = jnp.sum(spread(s) * own, axis=1, keepdims=True)
        count = groups(s)
        held = [jnp.where(i < count, bests[start + i], -jnp.inf) for i in range(most_items)]
        best = functools.reduce(jnp.maximum, held, jnp.broadcast_to(own_score, (8, 128)))
        own_weight = jnp.exp(own_score - best[:, 0:1])
        total = own_weight
        mixed = own_weight.astype(BF16).astype(F32) * own
        for i in range(most_items):
            share = jnp.exp(held[i] - best)[:, 0:1]
            total = total + jnp.where(i < count, totals[start + i][:, 0:1], 0.0) * share
            mixed = mixed + jnp.where(i < count, mixes[start + i], 0.0) * share
        mixed = jnp.where(diagonal, mixed / total, 0.0)
        rowout[s : s + 1, :] = jnp.sum(mixed, axis=0, keepdims=True)
        start = start + count
    done = rowout[...]
    for g in range(0, heads, 2):
        out[:, g * HD : (g + 2) * HD] = jnp.concatenate(
            [done[:, g * 2 * HD + HD : (g + 1) * 2 * HD], done[:, (g + 1) * 2 * HD + HD : (g + 2) * 2 * HD]], axis=1
        )


def decode_attention(scal, pages, x, gain, w, pool):
    slots = pages.shape[0]
    features = w.shape[2]
    heads = features // HD
    width = heads * 2 * HD
    rows = x.shape[0]
    per_group = BLOCK // PAGE
    most = pl.cdiv(pool.shape[0] + slots * (per_group - 1), per_group)
    spare = max(UNROLL, pl.cdiv(pages.shape[1], per_group))
    return pl.pallas_call(
        functools.partial(decode_kernel, heads),
        out_shape=jax.ShapeDtypeStruct((slots, features), F32),
        in_specs=[SMEM, SMEM, VMEM, VMEM, ANY, ANY],
        out_specs=VMEM,
        scratch_shapes=[
            pltpu.VMEM((most * BLOCK, width), BF16),
            pltpu.VMEM(w.shape, BF16),
            pltpu.VMEM(x.shape, BF16),
            pltpu.VMEM((rows, width), F32),
            pltpu.VMEM((rows, width), F32),
            pltpu.VMEM((slots, width), F32),
            pltpu.VMEM((most + spare, 8, 128), F32),
            pltpu.VMEM((most + spare, 8, 128), F32),
            pltpu.VMEM((most + spare, 8, width), F32),
            pltpu.SMEM((3, most + UNROLL), jnp.int32),
            pltpu.SemaphoreType.DMA((3,)),
            pltpu.SemaphoreType.DMA((most * per_group,)),
        ],
        compiler_params=pltpu.CompilerParams(vmem_limit_bytes=56 * 2**20),
        cost_estimate=pl.CostEstimate(flops=2 * 10**9, bytes_accessed=22 * 2**20, transcendentals=10**6),
    )(scal, pages, x, gain, w, pool)


def qkv_kernel(requests, heads, home, gain, x, w, out, xbuf, wbuf, normed, sems):
    rows = x.shape[0]
    positions = rows // requests
    half = positions // 2
    x_copy = pltpu.make_async_copy(x, xbuf, sems.at[3])
    x_copy.start()
    w_copies = [pltpu.make_async_copy(w.at[j], wbuf.at[j], sems.at[j]) for j in range(3)]
    for copy in w_copies:
        copy.start()
    x_copy.wait()
    values = xbuf[...].astype(F32)
    inverse = lax.rsqrt(jnp.mean(values * values, axis=-1, keepdims=True) + EPSILON)
    normed[...] = (values * inverse * gain[...]).astype(BF16)

    def project(j):
        w_copies[j].wait()
        return jnp.dot(normed[...], wbuf[j], preferred_element_type=F32).astype(BF16)

    y = project(0)
    for r in range(requests):
        for g in range(heads):
            part = y[r * positions : (r + 1) * positions, g * HD : (g + 1) * HD]
            out[home[r * heads + g], positions : positions + half, :] = jnp.concatenate([part[:half], part[half:]], axis=1)
    keys = project(1)
    y = project(2)
    for r in range(requests):
        span = slice(r * positions, (r + 1) * positions)
        for g in range(heads):
            cut = slice(g * HD, (g + 1) * HD)
            out[home[r * heads + g], 0:positions, :] = jnp.concatenate([keys[span, cut], y[span, cut]], axis=1)


def qkv_messages(home, x, gain, w, requests):
    rows, width = x.shape
    features = w.shape[2]
    heads = features // HD
    units = requests * heads
    positions = rows // requests
    return pl.pallas_call(
        functools.partial(qkv_kernel, requests, heads),
        out_shape=jax.ShapeDtypeStruct((units, positions * 3 // 2, 2 * HD), BF16),
        in_specs=[SMEM, VMEM, ANY, ANY],
        out_specs=VMEM,
        scratch_shapes=[
            pltpu.VMEM((rows, width), BF16),
            pltpu.VMEM(w.shape, BF16),
            pltpu.VMEM((rows, width), BF16),
            pltpu.SemaphoreType.DMA((4,)),
        ],
        compiler_params=pltpu.CompilerParams(vmem_limit_bytes=58 * 2**20),
        cost_estimate=pl.CostEstimate(flops=2 * rows * width * 3 * features, bytes_accessed=10 * 2**20, transcendentals=0),
    )(home, gain, x, w)


def project_kernel(requests, heads, scal, received, w_out, *rest):
    outs, rows_in, decode_in = rest[:-2], rest[-2], rest[-1]
    n_head = len(outs)
    n_tok = received.shape[0]
    units = requests * heads
    per = outs[0].shape[0]
    features = w_out.shape[0]
    slots = decode_in.shape[0] // n_tok
    half = received.shape[1] - slots * features // 128
    positions = 2 * half
    block_rows = positions // n_head
    share = per - requests * block_rows
    hosted = share * n_head
    for b in range(n_tok):
        for k in range(0, features // 128, 2):
            pair = received[b, half + k * slots : half + (k + 2) * slots, :].astype(F32)
            for j in range(2):
                decode_in[b * slots : (b + 1) * slots, (k + j) * 128 : (k + j + 1) * 128] = pair[
                    j * slots : (j + 1) * slots
                ]
    rows_in[...] = jnp.zeros_like(rows_in)
    for r in range(requests):
        for g in range(0, heads, 2):
            left = received[scal[r * heads + g], 0:half, :].astype(F32)
            right = received[scal[r * heads + g + 1], 0:half, :].astype(F32)
            both = jnp.concatenate(
                [
                    jnp.concatenate([left[:, :HD], right[:, :HD]], axis=1),
                    jnp.concatenate([left[:, HD:], right[:, HD:]], axis=1),
                ],
                axis=0,
            )
            for h in range(n_head):
                rows_in[h, r * block_rows : (r + 1) * block_rows, g * HD : (g + 2) * HD] = both[
                    h * block_rows : (h + 1) * block_rows
                ]
    for j in range(hosted):
        rows_in[j // share, requests * block_rows + j % share, :] = decode_in[pl.ds(scal[units + j], 1), :][0]
    for k in range(n_head):
        mine = rows_in[scal[units + hosted + k]].astype(BF16)
        y = jnp.dot(mine, w_out[...], preferred_element_type=F32).astype(BF16)
        outs[k][...] = y[:per]


def project_out(scal, received, w_out, requests, heads, n_head, hosted):
    features, width = w_out.shape
    positions = 2 * (received.shape[1] - hosted * features // 128)
    per = requests * (positions // n_head) + hosted // n_head
    padded = -(-per // 16) * 16
    return pl.pallas_call(
        functools.partial(project_kernel, requests, heads),
        out_shape=[jax.ShapeDtypeStruct((per, width), BF16)] * n_head,
        in_specs=[SMEM, VMEM, VMEM],
        out_specs=[VMEM] * n_head,
        scratch_shapes=[
            pltpu.VMEM((n_head, padded, features), F32),
            pltpu.VMEM((received.shape[0] * hosted, features), F32),
        ],
        compiler_params=pltpu.CompilerParams(vmem_limit_bytes=32 * 2**20),
        cost_estimate=pl.CostEstimate(flops=2 * n_head * per * features * width, bytes_accessed=4 * 2**20, transcendentals=0),
    )(scal, received, w_out)


def middle_kernel(own_pre, own_dec, gain, *rest):
    terms, (resid, normed) = rest[:-2], rest[-2:]
    split = own_pre.shape[0]
    for rows, own in ((slice(0, split), own_pre), (slice(split, resid.shape[0]), own_dec)):
        values = own[...].astype(F32)
        for term in terms:
            values = values + term[rows, :].astype(F32)
        resid[rows, :] = values
        inverse = lax.rsqrt(jnp.mean(values * values, axis=-1, keepdims=True) + EPSILON)
        normed[rows, :] = (values * inverse * gain[...]).astype(BF16)


def middle(own_pre, own_dec, gain, terms):
    shape = terms[0].shape
    return pl.pallas_call(
        middle_kernel,
        out_shape=[jax.ShapeDtypeStruct(shape, F32), jax.ShapeDtypeStruct(shape, BF16)],
        in_specs=[VMEM] * (3 + len(terms)),
        out_specs=[VMEM] * 2,
        compiler_params=pltpu.CompilerParams(vmem_limit_bytes=16 * 2**20),
        cost_estimate=pl.CostEstimate(flops=10**6, bytes_accessed=2 * 2**20, transcendentals=0),
    )(own_pre, own_dec, gain, *terms)


def feed_kernel(count, *refs):
    rows, (gate_up, down), outs = refs[:count], refs[count : count + 2], refs[count + 2 : 2 * count + 2]
    weights, down_weights, sems = refs[2 * count + 2 :]
    hidden_units = down.shape[0]
    tile = 128 if hidden_units % 128 == 0 else hidden_units
    steps = hidden_units // tile

    def load(step):
        cols = pl.ds(step * tile, tile)
        return pltpu.make_async_copy(gate_up.at[:, :, cols], weights.at[:, :, cols], sems.at[step])

    for step in range(steps):
        load(step).start()
    down_copy = pltpu.make_async_copy(down, down_weights, sems.at[steps])
    down_copy.start()
    hidden = [[] for _ in range(count)]
    for step in range(steps):
        load(step).wait()
        cols = slice(step * tile, (step + 1) * tile)
        both = jnp.concatenate([weights[0, :, cols], weights[1, :, cols]], axis=1) if tile == 128 else None
        for index in range(count):
            if tile == 128:
                y = jnp.dot(rows[index][...], both, preferred_element_type=F32)
                gate, upper = y[:, :tile], y[:, tile:]
            else:
                gate = jnp.dot(rows[index][...], weights[0], preferred_element_type=F32)
                upper = jnp.dot(rows[index][...], weights[1], preferred_element_type=F32)
            hidden[index].append((jax.nn.gelu(gate, approximate=True) * upper).astype(BF16))
    down_copy.wait()
    for index in range(count):
        full = jnp.concatenate(hidden[index], axis=1)
        outs[index][...] = jnp.dot(full, down_weights[...], preferred_element_type=F32).astype(BF16)


def feed_forward(chunks, gate_up, down):
    count = len(chunks)
    per, width = chunks[0].shape
    hidden_units = down.shape[0]
    return pl.pallas_call(
        functools.partial(feed_kernel, count),
        out_shape=[jax.ShapeDtypeStruct((per, width), BF16)] * count,
        in_specs=[VMEM] * count + [ANY, ANY],
        out_specs=[VMEM] * count,
        scratch_shapes=[
            pltpu.VMEM(gate_up.shape, BF16),
            pltpu.VMEM(down.shape, BF16),
            pltpu.SemaphoreType.DMA((hidden_units // 128 + 1,)),
        ],
        compiler_params=pltpu.CompilerParams(vmem_limit_bytes=32 * 2**20),
        cost_estimate=pl.CostEstimate(
            flops=6 * count * per * width * hidden_units, bytes_accessed=8 * 2**20, transcendentals=count * per * hidden_units
        ),
    )(*chunks, gate_up, down)


def ring_of(n_tok):
    if n_tok == 8:
        return [0, 2, 4, 6, 7, 5, 3, 1]
    return list(range(n_tok))


def shards(
    prefill_states,
    decode_states,
    attn_gain,
    w_qkv,
    w_out,
    ffn_gain,
    w_gate_up,
    w_down,
    prefill_pool,
    prefill_pages,
    prefill_lengths,
    prefill_home,
    decode_pool,
    decode_pages,
    decode_lengths,
    decode_home,
):
    n_tok = lax.axis_size("tok")
    n_head = lax.axis_size("head")
    my_tok = lax.axis_index("tok")
    my_head = lax.axis_index("head")
    requests, positions, width = prefill_states.shape
    hosted = decode_states.shape[0]
    features = w_qkv.shape[2]
    heads = features // HD
    units = requests * heads
    ring = ring_of(n_tok)
    ahead = [(ring[i], ring[(i + 1) % n_tok]) for i in range(n_tok)]
    behind = [(b, a) for a, b in ahead]
    far = n_tok // 2
    near = (n_tok - 1) // 2

    def joined(part, other):
        return (part.astype(F32) + other.astype(F32)).astype(BF16)

    gain = attn_gain.reshape(1, width)
    w_three = jnp.transpose(w_qkv, (1, 0, 2))
    unit_ids = jnp.arange(units, dtype=jnp.int32)
    my_unit = jnp.sum(jnp.where(prefill_home == my_tok, unit_ids, 0))
    length = lax.dynamic_slice_in_dim(prefill_lengths, my_unit // heads, 1, 0)
    slots = my_tok * hosted + jnp.arange(hosted, dtype=jnp.int32)
    all_requests = jnp.arange(decode_home.shape[0], dtype=jnp.int32)
    anchor = jnp.sum(jnp.where(decode_home[None, :] == slots[:, None], all_requests[None, :], 0), axis=1)
    anchor_row = ((anchor // hosted) ^ my_tok) * hosted + anchor % hosted

    first = lax.ppermute(decode_states, "tok", [(i, i ^ 1) for i in range(n_tok)])
    messages = qkv_messages(prefill_home, prefill_states.reshape(requests * positions, width), gain, w_three, requests)
    messages, first = lax.optimization_barrier((messages, first))
    pair = jnp.concatenate([decode_states, first], axis=0)
    rows = [pair] + [lax.ppermute(pair, "tok", [(i, i ^ step) for i in range(n_tok)]) for step in range(2, n_tok, 2)]
    held = lax.optimization_barrier([messages] + rows)
    messages, rows = held[0], held[1:]
    arrived = lax.all_to_all(messages, "tok", split_axis=0, concat_axis=0, tiled=True)
    rows = jnp.concatenate(rows, axis=0)
    decoded = decode_attention(
        jnp.concatenate([decode_lengths, anchor_row]), decode_pages, rows, gain, w_three, decode_pool
    )
    old_keys, old_values = prepare_cache(length, prefill_pages.reshape(-1), prefill_pool)
    arrived, decoded, old_keys, old_values = lax.optimization_barrier((arrived, decoded, old_keys, old_values))
    attn = prefill_attention(length, arrived, old_keys, old_values, decoded)
    attn, w_gate_up = lax.optimization_barrier((attn, w_gate_up))
    returned = lax.all_to_all(attn, "tok", split_axis=0, concat_axis=0, tiled=True)
    gate_up = jnp.transpose(w_gate_up, (1, 0, 2))
    returned, gate_up = lax.optimization_barrier((returned, gate_up))

    my_slots = lax.dynamic_slice_in_dim(decode_home, my_tok * hosted, hosted, 0)
    targets = my_head ^ jnp.arange(n_head, dtype=jnp.int32)
    parts = project_out(
        jnp.concatenate([prefill_home, my_slots, targets]), returned, w_out, requests, heads, n_head, hosted
    )
    block_rows = positions // n_head
    share = hosted // n_head
    own_pre = lax.dynamic_slice_in_dim(prefill_states, my_head * block_rows, block_rows, 1)
    own_dec = lax.dynamic_slice_in_dim(decode_states, my_head * share, share, 0)
    terms = [parts[0]]
    swap = [(i, i ^ 1) for i in range(n_head)]
    for k in range(2, n_head, 2):
        both = joined(parts[k], lax.ppermute(parts[k + 1], "head", swap))
        terms.append(lax.ppermute(both, "head", [(i, i ^ k) for i in range(n_head)]))
    terms.append(lax.ppermute(parts[1], "head", swap))
    resid, normed_mid = middle(own_pre.reshape(requests * block_rows, width), own_dec, ffn_gain.reshape(1, width), terms)

    plus, minus = {}, {}
    up, down = normed_mid, normed_mid
    waiting = [normed_mid]
    for k in range(1, far + 1):
        up = lax.ppermute(up, "tok", ahead)
        if k <= near:
            down = lax.ppermute(down, "tok", behind)
        done = feed_forward(waiting, gate_up, w_down)
        up, down, done = lax.optimization_barrier((up, down, done))
        if k == 1:
            (own_part,) = done
        else:
            minus[k - 1], plus[k - 1] = done
        waiting = [up, down]
    (minus[far],) = feed_forward([up], gate_up, w_down)
    plus[far] = minus[far]

    up, down = plus[far], minus[near]
    for k in range(far - 1, 0, -1):
        up = joined(plus[k], lax.ppermute(up, "tok", ahead))
        if k < near:
            down = joined(minus[k], lax.ppermute(down, "tok", behind))
    up = lax.ppermute(up, "tok", ahead).astype(F32)
    down = lax.ppermute(down, "tok", behind).astype(F32)
    result = (resid + (own_part.astype(F32) + up + down)).astype(BF16)
    prefill_out = result[: requests * block_rows].reshape(requests, block_rows, width)
    return (prefill_out, result[requests * block_rows :])


def solution(mesh):
    placed = (
        P(None, "tok", None),
        P("tok", None),
        P(),
        P(None, None, "head"),
        P("head", None),
        P(),
        P(None, None, "tok"),
        P("tok", None),
        P("tok", None, "head"),
        P("tok", None),
        P(),
        P(),
        P("tok", None, "head"),
        P("tok", None),
        P("tok"),
        P(),
    )
    return jax.shard_map(
        shards,
        mesh=mesh,
        in_specs=placed,
        out_specs=(P(None, ("tok", "head"), None), P(("tok", "head"), None)),
        check_vma=False,
    )
```

time: 231 us -> 181 us (0.78)
  blocking collectives: 31.1 us -> 0 us
  waiting for transfers between devices: 69 us -> 46.2 us
  local copies, waits for them, and re-layouts: 13.1 us -> 18.7 us
  Pallas kernels: 81 us -> 75.7 us
  other arithmetic: 1.28 us -> 3.83 us
    all_gather x1 -> x0, blocking collectives: 31.1 us -> none  [shards(): gathered = lax.all_gather(decode_attn, 'tok', axis=0, tiled=True)]
    ppermute x3, waiting for transfers between devices: 0.01 us -> 21 us  [shards(): up = joined(plus[k], lax.ppermute(up, 'tok', ahead))]
    all_to_all x1, waiting for transfers between devices: 20.2 us -> 0.01 us  [shards(): lax.all_to_all(messages, 'tok', split_axis=0, concat_axis=0, tiled=True)]
    ppermute x4, waiting for transfers between devices: 22.5 us -> 2.95 us  [shards(): up = lax.ppermute(up, 'tok', ahead)]
    ppermute x2, waiting for transfers between devices: 13.3 us -> 0.02 us  [shards(): down = joined(minus[k], lax.ppermute(down, 'tok', behind))]
    ppermute x3 -> x7, starting transfers between devices: 1.92 us -> 9.48 us  [the longest x3 4.45 us: shards(): lax.ppermute(pair, 'tok', [(i, i ^ step) for i in range(n_tok)])]
    pallas_call x2 -> x4, Pallas kernels: 38.7 us -> 33.1 us  [the longest x1 22.5 us: prefill_attention(): pl.pallas_call(functools.partial(prefill_kernel, positions), out_shape=ja...]
    optimization_barrier x0 -> x1, local copies, waits for them, and re-layouts: none -> 5.48 us  [shards(): attn, w_gate_up = lax.optimization_barrier((attn, w_gate_up))]
  transfers between devices with their start and end apart: 20 -> 23, of which waited for: 11 -> 16; matrix products, arithmetic and copies ran while one was open for 2% -> 7% of each run, Pallas kernels for 32% -> 25%
where the time goes in v2:
time: 181 us; the launch traced here: 180 us
  Pallas kernels  75.7 us (42%)
  waiting for transfers between devices  46.2 us (26%)
  starting transfers between devices  34.4 us (19%)
  local copies, waits for them, and re-layouts  18.7 us (10%)
  other arithmetic  3.83 us (2%)
    pallas_call x1, Pallas kernels, prefill_attention(): pl.pallas_call(functools.partial(prefill_kernel, positions), out_shape=ja...  22.5 us
    pallas_call x5, Pallas kernels, feed_forward(): pl.pallas_call(functools.partial(feed_kernel, count), out_shape=[jax.Shap...  22.1 us
    ppermute x3, waiting for transfers between devices, shards(): up = joined(plus[k], lax.ppermute(up, 'tok', ahead))  21 us
    pallas_call x1, Pallas kernels, decode_attention(): pl.pallas_call(functools.partial(decode_kernel, heads), out_shape=jax.Sha...  17.5 us
    unnamed x33, local copies, waits for them, and re-layouts  10.1 us
    all_to_all x1, starting transfers between devices, shards(): lax.all_to_all(attn, 'tok', split_axis=0, concat_axis=0, tiled=True)  6.85 us
    ppermute x1, waiting for transfers between devices, shards(): lax.ppermute(both, 'head', [(i, i ^ k) for i in range(n_head)])  6.02 us
    pallas_call x1, Pallas kernels, qkv_messages(): pl.pallas_call(functools.partial(qkv_kernel, requests, heads), out_shape=...  6 us
  transfers between devices with their start and end apart: 23, of which 16 were waited for; matrix products, arithmetic and copies ran while one was open for 7% of the time, Pallas kernels for 25%

profile of v2, /device:TPU:0, one launch (start us, length us, event | category | flops | bytes accessed | tf_op | source)
XLA Modules:
  0.0 180.3 jit_solution(10628588382392262754)
XLA Ops:
  0.6 3.0 %collective-permute-start = (bf16[8,2048]{1,0:T(8,128)(2,1)}, bf16[8,2048]{1,0:T(8,128)(2,1)S(1)}, u32[]{:S(2)}, u32[]{:S(2)}) collective-permute-start(bf16[8,2048]{1,0:T(8,128)(2,1)} %param.17), channel_id=1, source_target_pairs={{0,4},{4,0},{8,12},{12,8},{16,20},{20,16},{24,28},{28,24},{1,5},{5... | collective-permute-start | bytes 98312 | tf_op jit(solution)/shard_map/ppermute | solution.py:612
  3.7 0.8 constant_dynamic-update-slice_fusion.1
  4.5 6.0 %shard_map.167 = bf16[8,384,128]{2,1,0:T(8,128)(2,1)} custom-call(s32[8]{0:T(128)} %home.1, f32[1,2048]{1,0:T(1,128)} %bitcast.22, bf16[256,2048]{1,0:T(8,128)(2,1)} %bitcast.21, bf16[3,2048,512]{2,1,0:T(8,128)(2,1)} %bitcast.19), custom_call_target="tpu_custom_call" | custom-call | flops 1610612736 | bytes 10485760 | tf_op jit(solution)/shard_map/pallas_call | solution.py:402
  10.5 3.7 %collective-permute-start.3 = (bf16[16,2048]{1,0:T(8,128)(2,1)S(1)}, bf16[16,2048]{1,0:T(8,128)(2,1)S(1)}, u32[]{:S(2)}, u32[]{:S(2)}) collective-permute-start(bf16[16,2048]{1,0:T(8,128)(2,1)S(1)} %constant_dynamic-update-slice_fusion), channel_id=1, source_target_pairs={{0,24},{4,28},{8,16},{12,20},{16,8},{20,12},{24,0},{28,4},{1,25},{... | collective-permute-start | bytes 196616 | tf_op jit(solution)/shard_map/ppermute | solution.py:616
  14.2 0.8 collective-permute-start.1
  15.0 2.5 %collective-permute-done.3 = bf16[16,2048]{1,0:T(8,128)(2,1)S(1)} collective-permute-done((bf16[16,2048]{1,0:T(8,128)(2,1)S(1)}, bf16[16,2048]{1,0:T(8,128)(2,1)S(1)}, u32[]{:S(2)}, u32[]{:S(2)}) %collective-permute-start.3) | collective-permute-done | bytes 65568 | tf_op jit(solution)/shard_map/ppermute | solution.py:616
  17.4 2.1 %collective-permute-done.2 = bf16[16,2048]{1,0:T(8,128)(2,1)S(1)} collective-permute-done((bf16[16,2048]{1,0:T(8,128)(2,1)S(1)}, bf16[16,2048]{1,0:T(8,128)(2,1)S(1)}, u32[]{:S(2)}, u32[]{:S(2)}) %collective-permute-start.2) | collective-permute-done | bytes 65568 | tf_op jit(solution)/shard_map/ppermute | solution.py:616
  19.6 3.9 %all-to-all-start = ((bf16[8,384,128]{2,1,0:T(8,128)(2,1)}), bf16[8,384,128]{2,1,0:T(8,128)(2,1)S(1)}, u32[]{:S(2)}, u32[]{:S(2)}) async-start(bf16[8,384,128]{2,1,0:T(8,128)(2,1)} %shard_map.167), calls=%async_computation | async-start | bytes 1572864 | tf_op jit(solution)/shard_map/all_to_all | solution.py:619
  25.0 4.3 %shard_map.169 = (bf16[6,128,1024]{2,1,0:T(8,128)(2,1)S(1)}, bf16[6,1024,128]{2,1,0:T(8,128)(2,1)S(1)}) custom-call(s32[1]{0:T(128)S(6)} %copy.23.scal, s32[48]{0:T(128)S(1)} %bitcast.18, bf16[48,128,128]{2,1,0:T(8,128)(2,1)S(1)} %copy-done.6), custom_call_target="tpu_custom_call" | custom-call | flops 2000000000 | bytes 6291456 | tf_op jit(solution)/shard_map/pallas_call | solution.py:73
  29.3 1.1 copy-done.9
  30.5 1.2 copy-done.11
  32.3 17.5 %shard_map.168.decoded = f32[8,512]{1,0:T(8,128)} custom-call(s32[16]{0:T(128)} %pad_add_fusion.1.scal, s32[8,32]{1,0:T(8,128)} %pages.1, bf16[64,2048]{1,0:T(8,128)(2,1)} %pad_maximum_fusion.x, f32[1,2048]{1,0:T(1,128)} %bitcast.23, bf16[3,2048,512]{2,1,0:T(8,128)(2,1)} %bitcast.20, bf16[64,128,1024]{2,1,0:T(8,128)(2,1)} %pool.2), custom_call_target="tpu_custom_call" | custom-call | flops 2000000000 | bytes 23068672 | tf_op jit(solution)/shard_map/pallas_call | solution.py:340
  50.6 1.4 copy-done.12
  52.0 22.5 %shard_map.170 = bf16[8,160,128]{2,1,0:T(8,128)(2,1)} custom-call(s32[1]{0:T(128)S(6)} %copy.23.scal, bf16[8,384,128]{2,1,0:T(8,128)(2,1)S(1)} %all-to-all-done.msg, bf16[6,128,1024]{2,1,0:T(8,128)(2,1)S(1)} %copy-done.10, bf16[6,1024,128]{2,1,0:T(8,128)(2,1)S(1)} %copy-done.12, f32[8,512]{1,0:T(8,128)S(1)} %copy-done.4), custom_call_target="tpu_custom_call" | custom-call | flops 4294967296 | bytes 4194304 | tf_op jit(solution)/shard_map/pallas_call | solution.py:200
  74.5 6.9 %all-to-all-start.1 = ((bf16[8,160,128]{2,1,0:T(8,128)(2,1)}), bf16[8,160,128]{2,1,0:T(8,128)(2,1)S(1)}, u32[]{:S(2)}, u32[]{:S(2)}) async-start(bf16[8,160,128]{2,1,0:T(8,128)(2,1)} %shard_map.170), calls=%async_computation.1 | async-start | bytes 655360 | tf_op jit(solution)/shard_map/all_to_all | solution.py:628
  81.5 5.5 %copy.21 = bf16[2048,2,640]{2,0,1:T(8,128)(2,1)} copy(bf16[2048,2,640]{2,1,0:T(2,128)(2,1)} %param.22) | data formatting | bytes 10485760 | tf_op jit(solution)/shard_map/optimization_barrier | solution.py:627
  87.0 3.5 %all-to-all-done.1.received = bf16[8,160,128]{2,1,0:T(8,128)(2,1)S(1)} async-done(((bf16[8,160,128]{2,1,0:T(8,128)(2,1)}), bf16[8,160,128]{2,1,0:T(8,128)(2,1)S(1)}, u32[]{:S(2)}, u32[]{:S(2)}) %all-to-all-start.1) | async-done | bytes 327712 | tf_op jit(solution)/shard_map/all_to_all | solution.py:628
  90.5 1.6 copy-done.3
  92.1 3.0 %shard_map.171 = (bf16[66,2048]{1,0:T(8,128)(2,1)S(1)}, bf16[66,2048]{1,0:T(8,128)(2,1)S(1)}, bf16[66,2048]{1,0:T(8,128)(2,1)S(1)}, bf16[66,2048]{1,0:T(8,128)(2,1)}) custom-call(s32[20]{0:T(128)S(1)} %pad_add_fusion.scal, bf16[8,160,128]{2,1,0:T(8,128)(2,1)S(1)} %all-to-all-done.1.received, bf16[512,2048]{1,0:T(8,128)(2,1)S(1)} %copy-done.3), custom_call_target="tpu_custom_call" | custom-call | flops 553648128 | bytes 4194304 | tf_op jit(solution)/shard_map/pallas_call | solution.py:467
  96.3 1.5 collective-permute-done.4
  97.8 1.8 add_convert_fusion.6
  99.6 1.5 collective-permute-start.5
  101.0 0.8 constant_dynamic-slice_fusion.own_dec
  101.8 1.0 dynamic-slice_bitcast_fusion.own_pre
  102.8 6.0 %collective-permute-done.5.rest_1_ = bf16[66,2048]{1,0:T(8,128)(2,1)S(1)} collective-permute-done((bf16[66,2048]{1,0:T(8,128)(2,1)}, bf16[66,2048]{1,0:T(8,128)(2,1)S(1)}, u32[]{:S(2)}, u32[]{:S(2)}) %collective-permute-start.5) | collective-permute-done | bytes 270368 | tf_op jit(solution)/shard_map/ppermute | solution.py:645
  109.1 1.5 collective-permute-start.8
  111.2 2.5 %copy-done = bf16[2048,2,640]{2,0,1:T(8,128)(2,1)S(1)} copy-done((bf16[2048,2,640]{2,0,1:T(8,128)(2,1)S(1)}, bf16[2048,2,640]{2,0,1:T(8,128)(2,1)}, u32[]{:S(2)}) %copy-start) | copy-done | bytes 5242904
  113.7 4.0 %shard_map.173 = bf16[66,2048]{1,0:T(8,128)(2,1)S(1)} custom-call(bf16[66,2048]{1,0:T(8,128)(2,1)S(1)} %get-tuple-element.66.refs_0_, bf16[2,2048,640]{2,1,0:T(8,128)(2,1)S(1)} %bitcast.12, bf16[640,2048]{1,0:T(8,128)(2,1)S(1)} %copy-done.2), custom_call_target="tpu_custom_call" | custom-call | flops 519045120 | bytes 8388608 | tf_op jit(solution)/shard_map/pallas_call | solution.py:543
  117.6 0.9 collective-permute-done.7.refs_0_
  119.1 1.5 collective-permute-start.10
  120.6 4.7 %shard_map.174 = (bf16[66,2048]{1,0:T(8,128)(2,1)S(1)}, bf16[66,2048]{1,0:T(8,128)(2,1)S(1)}) custom-call(bf16[66,2048]{1,0:T(8,128)(2,1)S(1)} %collective-permute-done.7.refs_0_, bf16[66,2048]{1,0:T(8,128)(2,1)S(1)} %collective-permute-done.8.refs_1_, bf16[2,2048,640]{2,1,0:T(8,128)(2,1)S(1)} %bitcast.13, bf16[640,2048]{1,0:T(8,128)(2,1)S(1)} %copy-done.2), custom_call_target="tpu_custom_call" | custom-call | flops 1038090240 | bytes 8388608 | tf_op jit(solution)/shard_map/pallas_call | solution.py:543
  126.1 0.8 collective-permute-start.11
  126.9 1.3 collective-permute-start.12
  128.2 4.7 %shard_map.175 = (bf16[66,2048]{1,0:T(8,128)(2,1)S(1)}, bf16[66,2048]{1,0:T(8,128)(2,1)S(1)}) custom-call(bf16[66,2048]{1,0:T(8,128)(2,1)S(1)} %collective-permute-done.9.refs_0_, bf16[66,2048]{1,0:T(8,128)(2,1)S(1)} %collective-permute-done.10.refs_1_, bf16[2,2048,640]{2,1,0:T(8,128)(2,1)S(1)} %bitcast.14, bf16[640,2048]{1,0:T(8,128)(2,1)S(1)} %copy-done.2), custom_call_target="tpu_custom_call" | custom-call | flops 1038090240 | bytes 8388608 | tf_op jit(solution)/shard_map/pallas_call | solution.py:543
  133.6 0.8 collective-permute-start.13
  134.4 4.7 %shard_map.176 = (bf16[66,2048]{1,0:T(8,128)(2,1)S(1)}, bf16[66,2048]{1,0:T(8,128)(2,1)S(1)}) custom-call(bf16[66,2048]{1,0:T(8,128)(2,1)S(1)} %collective-permute-done.11.refs_0_, bf16[66,2048]{1,0:T(8,128)(2,1)S(1)} %collective-permute-done.12.refs_1_, bf16[2,2048,640]{2,1,0:T(8,128)(2,1)S(1)} %bitcast.15, bf16[640,2048]{1,0:T(8,128)(2,1)S(1)} %copy-done.2), custom_call_target="tpu_custom_call" | custom-call | flops 1038090240 | bytes 8388608 | tf_op jit(solution)/shard_map/pallas_call | solution.py:543
  139.1 1.2 collective-permute-done.13.refs_0_
  140.4 4.0 %shard_map.177 = bf16[66,2048]{1,0:T(8,128)(2,1)S(1)} custom-call(bf16[66,2048]{1,0:T(8,128)(2,1)S(1)} %collective-permute-done.13.refs_0_, bf16[2,2048,640]{2,1,0:T(8,128)(2,1)S(1)} %bitcast.16, bf16[640,2048]{1,0:T(8,128)(2,1)S(1)} %copy-done.2), custom_call_target="tpu_custom_call" | custom-call | flops 519045120 | bytes 8388608 | tf_op jit(solution)/shard_map/pallas_call | solution.py:543
  144.3 0.8 collective-permute-start.14
  145.1 1.3 collective-permute-start.18
  146.4 7.6 %collective-permute-done.14 = bf16[66,2048]{1,0:T(8,128)(2,1)S(1)} collective-permute-done((bf16[66,2048]{1,0:T(8,128)(2,1)S(1)}, bf16[66,2048]{1,0:T(8,128)(2,1)S(1)}, u32[]{:S(2)}, u32[]{:S(2)}) %collective-permute-start.14) | collective-permute-done | bytes 270368 | tf_op jit(solution)/shard_map/ppermute | solution.py:668
  154.9 1.4 collective-permute-start.19
  156.3 7.1 %collective-permute-done.15 = bf16[66,2048]{1,0:T(8,128)(2,1)S(1)} collective-permute-done((bf16[66,2048]{1,0:T(8,128)(2,1)S(1)}, bf16[66,2048]{1,0:T(8,128)(2,1)S(1)}, u32[]{:S(2)}, u32[]{:S(2)}) %collective-permute-start.15) | collective-permute-done | bytes 270368 | tf_op jit(solution)/shard_map/ppermute | solution.py:668
  163.5 0.8 collective-permute-start.16
  164.4 1.3 collective-permute-start.20
  165.7 6.3 %collective-permute-done.16 = bf16[66,2048]{1,0:T(8,128)(2,1)S(1)} collective-permute-done((bf16[66,2048]{1,0:T(8,128)(2,1)S(1)}, bf16[66,2048]{1,0:T(8,128)(2,1)S(1)}, u32[]{:S(2)}, u32[]{:S(2)}) %collective-permute-start.16) | collective-permute-done | bytes 270368 | tf_op jit(solution)/shard_map/ppermute | solution.py:668
  172.1 1.0 collective-permute-start.17
  173.0 5.8 %collective-permute-done.17 = bf16[66,2048]{1,0:T(8,128)(2,1)S(1)} collective-permute-done((bf16[66,2048]{1,0:T(8,128)(2,1)S(1)}, bf16[66,2048]{1,0:T(8,128)(2,1)S(1)}, u32[]{:S(2)}, u32[]{:S(2)}) %collective-permute-start.17) | collective-permute-done | bytes 270368 | tf_op jit(solution)/shard_map/ppermute | solution.py:671
  (63 shorter events, 9.1 us)
Async XLA Ops:
  0.6 9.9 %collective-permute-start = (bf16[8,2048]{1,0:T(8,128)(2,1)}, bf16[8,2048]{1,0:T(8,128)(2,1)S(1)}, u32[]{:S(2)}, u32[]{:S(2)}) collective-permute-start(bf16[8,2048]{1,0:T(8,128)(2,1)} %param.17), channel_id=1, source_target_pairs={{0,4},{4,0},{8,12},{12,8},{16,20},{20,16},{24,28},{28,24},{1,5},{5... | collective-permute-start | bytes 98312 | tf_op jit(solution)/shard_map/ppermute | solution.py:612
  4.5 19.7 %copy-start.15 = (s32[64]{0:T(128)S(1)}, s32[64]{0:T(128)}, u32[]{:S(2)}) copy-start(s32[64]{0:T(128)} %param.31) | copy-start | bytes 772
  4.5 19.9 %copy-start.14 = (s32[8]{0:T(128)S(1)}, s32[8]{0:T(128)}, u32[]{:S(2)}) copy-start(s32[8]{0:T(128)} %param.30) | copy-start | bytes 100
  4.5 20.5 %copy-start.6 = (bf16[48,128,128]{2,1,0:T(8,128)(2,1)S(1)}, bf16[48,128,128]{2,1,0:T(8,128)(2,1)}, u32[]{:S(2)}) copy-start(bf16[48,128,128]{2,1,0:T(8,128)(2,1)} %pool.3) | copy-start | bytes 4718596
  4.5 20.5 %copy-start.8 = (s32[1,48]{1,0:T(1,128)S(1)}, s32[1,48]{1,0:T(1,128)}, u32[]{:S(2)}) copy-start(s32[1,48]{1,0:T(1,128)} %param.25) | copy-start | bytes 580
  10.5 6.9 %collective-permute-start.3 = (bf16[16,2048]{1,0:T(8,128)(2,1)S(1)}, bf16[16,2048]{1,0:T(8,128)(2,1)S(1)}, u32[]{:S(2)}, u32[]{:S(2)}) collective-permute-start(bf16[16,2048]{1,0:T(8,128)(2,1)S(1)} %constant_dynamic-update-slice_fusion), channel_id=1, source_target_pairs={{0,24},{4,28},{8,16},{12,20},{16,8},{20,12},{24,0},{28,4},{1,25},{... | collective-permute-start | bytes 196616 | tf_op jit(solution)/shard_map/ppermute | solution.py:616
  14.2 5.4 %collective-permute-start.2 = (bf16[16,2048]{1,0:T(8,128)(2,1)S(1)}, bf16[16,2048]{1,0:T(8,128)(2,1)S(1)}, u32[]{:S(2)}, u32[]{:S(2)}) collective-permute-start(bf16[16,2048]{1,0:T(8,128)(2,1)S(1)} %constant_dynamic-update-slice_fusion), channel_id=1, source_target_pairs={{0,16},{4,20},{8,24},{12,28},{16,0},{20,4},{24,8},{28,12},{1,17},{... | collective-permute-start | bytes 196616 | tf_op jit(solution)/shard_map/ppermute | solution.py:616
  14.2 5.4 %collective-permute-start.1 = (bf16[16,2048]{1,0:T(8,128)(2,1)S(1)}, bf16[16,2048]{1,0:T(8,128)(2,1)S(1)}, u32[]{:S(2)}, u32[]{:S(2)}) collective-permute-start(bf16[16,2048]{1,0:T(8,128)(2,1)S(1)} %constant_dynamic-update-slice_fusion), channel_id=1, source_target_pairs={{0,8},{4,12},{8,0},{12,4},{16,24},{20,28},{24,16},{28,20},{1,9},{5... | collective-permute-start | bytes 196616 | tf_op jit(solution)/shard_map/ppermute | solution.py:616
  19.6 30.2 %all-to-all-start = ((bf16[8,384,128]{2,1,0:T(8,128)(2,1)}), bf16[8,384,128]{2,1,0:T(8,128)(2,1)S(1)}, u32[]{:S(2)}, u32[]{:S(2)}) async-start(bf16[8,384,128]{2,1,0:T(8,128)(2,1)} %shard_map.167), calls=%async_computation | async-start | bytes 1572864 | tf_op jit(solution)/shard_map/all_to_all | solution.py:619
  29.3 1.2 copy-start.9
  30.5 1.2 copy-start.11
  32.3 17.5 %copy-start.10 = (bf16[6,128,1024]{2,1,0:T(8,128)(2,1)S(1)}, bf16[6,128,1024]{2,1,0:T(8,128)(2,1)}, u32[]{:S(2)}) copy-start(bf16[6,128,1024]{2,1,0:T(8,128)(2,1)} %copy-done.9) | copy-start | bytes 4718596
  49.8 0.7 copy-start.4
  50.6 1.4 copy-start.12
  52.0 29.5 %copy-start.13 = (s32[8]{0:T(128)S(1)}, s32[8]{0:T(128)}, u32[]{:S(2)}) copy-start(s32[8]{0:T(128)} %home.1) | copy-start | bytes 100
  74.5 16.0 %all-to-all-start.1 = ((bf16[8,160,128]{2,1,0:T(8,128)(2,1)}), bf16[8,160,128]{2,1,0:T(8,128)(2,1)S(1)}, u32[]{:S(2)}, u32[]{:S(2)}) async-start(bf16[8,160,128]{2,1,0:T(8,128)(2,1)} %shard_map.170), calls=%async_computation.1 | async-start | bytes 655360 | tf_op jit(solution)/shard_map/all_to_all | solution.py:628
  81.5 27.3 %copy-start.5 = (f32[2048]{0:T(1024)S(1)}, f32[2048]{0:T(1024)}, u32[]{:S(2)}) copy-start(f32[2048]{0:T(1024)} %param.21) | copy-start | bytes 24580
  87.0 24.2 %copy-start.2 = (bf16[640,2048]{1,0:T(8,128)(2,1)S(1)}, bf16[640,2048]{1,0:T(8,128)(2,1)}, u32[]{:S(2)}) copy-start(bf16[640,2048]{1,0:T(8,128)(2,1)} %refs_2_.3) | copy-start | bytes 7864324
  90.5 1.6 copy-start.3
  95.1 0.7 copy-start.7
  95.8 2.0 %collective-permute-start.4 = (bf16[66,2048]{1,0:T(8,128)(2,1)}, bf16[66,2048]{1,0:T(8,128)(2,1)}, u32[]{:S(2)}, u32[]{:S(2)}) collective-permute-start(bf16[66,2048]{1,0:T(8,128)(2,1)} %get-tuple-element.63), channel_id=1, source_target_pairs={{0,1},{1,0},{2,3},{3,2},{4,5},{5,4},{6,7},{7,6},{8,9},{9,8},{10,11... | collective-permute-start | bytes 811016 | tf_op jit(solution)/shard_map/ppermute | solution.py:644
  95.8 7.0 %collective-permute-start.6 = (bf16[66,2048]{1,0:T(8,128)(2,1)}, bf16[66,2048]{1,0:T(8,128)(2,1)S(1)}, u32[]{:S(2)}, u32[]{:S(2)}) collective-permute-start(bf16[66,2048]{1,0:T(8,128)(2,1)} %copy-done.7), channel_id=1, source_target_pairs={{0,1},{1,0},{2,3},{3,2},{4,5},{5,4},{6,7},{7,6},{8,9},{9,8},{10,11... | collective-permute-start | bytes 811016 | tf_op jit(solution)/shard_map/ppermute | solution.py:646
  99.6 9.3 %collective-permute-start.5 = (bf16[66,2048]{1,0:T(8,128)(2,1)}, bf16[66,2048]{1,0:T(8,128)(2,1)S(1)}, u32[]{:S(2)}, u32[]{:S(2)}) collective-permute-start(bf16[66,2048]{1,0:T(8,128)(2,1)} %add_convert_fusion.6), channel_id=1, source_target_pairs={{0,2},{1,3},{2,0},{3,1},{4,6},{5,7},{6,4},{7,5},{8,10},{9,11},{10,... | collective-permute-start | bytes 811016 | tf_op jit(solution)/shard_map/ppermute | solution.py:645
  109.1 8.5 %collective-permute-start.8 = (bf16[66,2048]{1,0:T(8,128)(2,1)S(1)}, bf16[66,2048]{1,0:T(8,128)(2,1)S(1)}, u32[]{:S(2)}, u32[]{:S(2)}) collective-permute-start(bf16[66,2048]{1,0:T(8,128)(2,1)S(1)} %get-tuple-element.66.refs_0_), channel_id=1, source_target_pairs={{8,0},{16,8},{24,16},{28,24},{20,28},{12,20},{4,12},{0,4},{9,1},{1... | collective-permute-start | bytes 811016 | tf_op jit(solution)/shard_map/ppermute | solution.py:655
  110.6 7.9 %collective-permute-start.7 = (bf16[66,2048]{1,0:T(8,128)(2,1)S(1)}, bf16[66,2048]{1,0:T(8,128)(2,1)S(1)}, u32[]{:S(2)}, u32[]{:S(2)}) collective-permute-start(bf16[66,2048]{1,0:T(8,128)(2,1)S(1)} %get-tuple-element.66.refs_0_), channel_id=1, source_target_pairs={{0,8},{8,16},{16,24},{24,28},{28,20},{20,12},{12,4},{4,0},{1,9},{9... | collective-permute-start | bytes 811016 | tf_op jit(solution)/shard_map/ppermute | solution.py:653
  111.2 2.5 %copy-start = (bf16[2048,2,640]{2,0,1:T(8,128)(2,1)S(1)}, bf16[2048,2,640]{2,0,1:T(8,128)(2,1)}, u32[]{:S(2)}) copy-start(bf16[2048,2,640]{2,0,1:T(8,128)(2,1)} %copy.21) | copy-start | bytes 15728644
  113.7 6.9 %copy-start.1 = (bf16[2048,2,640]{2,0,1:T(8,128)(2,1)S(1)}, bf16[2048,2,640]{2,0,1:T(8,128)(2,1)}, u32[]{:S(2)}) copy-start(bf16[2048,2,640]{2,0,1:T(8,128)(2,1)} %copy.21) | copy-start | bytes 15728644
  118.6 7.0 %collective-permute-start.9 = (bf16[66,2048]{1,0:T(8,128)(2,1)S(1)}, bf16[66,2048]{1,0:T(8,128)(2,1)S(1)}, u32[]{:S(2)}, u32[]{:S(2)}) collective-permute-start(bf16[66,2048]{1,0:T(8,128)(2,1)S(1)} %collective-permute-done.7.refs_0_), channel_id=1, source_target_pairs={{0,8},{8,16},{16,24},{24,28},{28,20},{20,12},{12,4},{4,0},{1,9},{9... | collective-permute-start | bytes 811016 | tf_op jit(solution)/shard_map/ppermute | solution.py:653
  119.1 7.0 %collective-permute-start.10 = (bf16[66,2048]{1,0:T(8,128)(2,1)S(1)}, bf16[66,2048]{1,0:T(8,128)(2,1)S(1)}, u32[]{:S(2)}, u32[]{:S(2)}) collective-permute-start(bf16[66,2048]{1,0:T(8,128)(2,1)S(1)} %collective-permute-done.8.refs_1_), channel_id=1, source_target_pairs={{8,0},{16,8},{24,16},{28,24},{20,28},{12,20},{4,12},{0,4},{9,1},{1... | collective-permute-start | bytes 811016 | tf_op jit(solution)/shard_map/ppermute | solution.py:655
  126.1 7.3 %collective-permute-start.11 = (bf16[66,2048]{1,0:T(8,128)(2,1)S(1)}, bf16[66,2048]{1,0:T(8,128)(2,1)S(1)}, u32[]{:S(2)}, u32[]{:S(2)}) collective-permute-start(bf16[66,2048]{1,0:T(8,128)(2,1)S(1)} %collective-permute-done.9.refs_0_), channel_id=1, source_target_pairs={{0,8},{8,16},{16,24},{24,28},{28,20},{20,12},{12,4},{4,0},{1,9},{9... | collective-permute-start | bytes 811016 | tf_op jit(solution)/shard_map/ppermute | solution.py:653
  126.9 6.7 %collective-permute-start.12 = (bf16[66,2048]{1,0:T(8,128)(2,1)S(1)}, bf16[66,2048]{1,0:T(8,128)(2,1)S(1)}, u32[]{:S(2)}, u32[]{:S(2)}) collective-permute-start(bf16[66,2048]{1,0:T(8,128)(2,1)S(1)} %collective-permute-done.10.refs_1_), channel_id=1, source_target_pairs={{8,0},{16,8},{24,16},{28,24},{20,28},{12,20},{4,12},{0,4},{9,1},{1... | collective-permute-start | bytes 811016 | tf_op jit(solution)/shard_map/ppermute | solution.py:655
  133.6 6.7 %collective-permute-start.13 = (bf16[66,2048]{1,0:T(8,128)(2,1)S(1)}, bf16[66,2048]{1,0:T(8,128)(2,1)S(1)}, u32[]{:S(2)}, u32[]{:S(2)}) collective-permute-start(bf16[66,2048]{1,0:T(8,128)(2,1)S(1)} %collective-permute-done.11.refs_0_), channel_id=1, source_target_pairs={{0,8},{8,16},{16,24},{24,28},{28,20},{20,12},{12,4},{4,0},{1,9},{9... | collective-permute-start | bytes 811016 | tf_op jit(solution)/shard_map/ppermute | solution.py:653
  144.3 9.7 %collective-permute-start.14 = (bf16[66,2048]{1,0:T(8,128)(2,1)S(1)}, bf16[66,2048]{1,0:T(8,128)(2,1)S(1)}, u32[]{:S(2)}, u32[]{:S(2)}) collective-permute-start(bf16[66,2048]{1,0:T(8,128)(2,1)S(1)} %shard_map.177), channel_id=1, source_target_pairs={{0,8},{8,16},{16,24},{24,28},{28,20},{20,12},{12,4},{4,0},{1,9},{9... | collective-permute-start | bytes 811016 | tf_op jit(solution)/shard_map/ppermute | solution.py:668
  145.1 9.7 %collective-permute-start.18 = (bf16[66,2048]{1,0:T(8,128)(2,1)S(1)}, bf16[66,2048]{1,0:T(8,128)(2,1)S(1)}, u32[]{:S(2)}, u32[]{:S(2)}) collective-permute-start(bf16[66,2048]{1,0:T(8,128)(2,1)S(1)} %get-tuple-element.87), channel_id=1, source_target_pairs={{8,0},{16,8},{24,16},{28,24},{20,28},{12,20},{4,12},{0,4},{9,1},{1... | collective-permute-start | bytes 811016 | tf_op jit(solution)/shard_map/ppermute | solution.py:670
  154.1 9.3 %collective-permute-start.15 = (bf16[66,2048]{1,0:T(8,128)(2,1)S(1)}, bf16[66,2048]{1,0:T(8,128)(2,1)S(1)}, u32[]{:S(2)}, u32[]{:S(2)}) collective-permute-start(bf16[66,2048]{1,0:T(8,128)(2,1)S(1)} %add_convert_fusion.5), channel_id=1, source_target_pairs={{0,8},{8,16},{16,24},{24,28},{28,20},{20,12},{12,4},{4,0},{1,9},{9... | collective-permute-start | bytes 811016 | tf_op jit(solution)/shard_map/ppermute | solution.py:668
  154.9 9.4 %collective-permute-start.19 = (bf16[66,2048]{1,0:T(8,128)(2,1)S(1)}, bf16[66,2048]{1,0:T(8,128)(2,1)S(1)}, u32[]{:S(2)}, u32[]{:S(2)}) collective-permute-start(bf16[66,2048]{1,0:T(8,128)(2,1)S(1)} %add_convert_fusion.2), channel_id=1, source_target_pairs={{8,0},{16,8},{24,16},{28,24},{20,28},{12,20},{4,12},{0,4},{9,1},{1... | collective-permute-start | bytes 811016 | tf_op jit(solution)/shard_map/ppermute | solution.py:670
  163.5 8.5 %collective-permute-start.16 = (bf16[66,2048]{1,0:T(8,128)(2,1)S(1)}, bf16[66,2048]{1,0:T(8,128)(2,1)S(1)}, u32[]{:S(2)}, u32[]{:S(2)}) collective-permute-start(bf16[66,2048]{1,0:T(8,128)(2,1)S(1)} %add_convert_fusion.4), channel_id=1, source_target_pairs={{0,8},{8,16},{16,24},{24,28},{28,20},{20,12},{12,4},{4,0},{1,9},{9... | collective-permute-start | bytes 811016 | tf_op jit(solution)/shard_map/ppermute | solution.py:668
  164.4 8.6 %collective-permute-start.20 = (bf16[66,2048]{1,0:T(8,128)(2,1)S(1)}, bf16[66,2048]{1,0:T(8,128)(2,1)S(1)}, u32[]{:S(2)}, u32[]{:S(2)}) collective-permute-start(bf16[66,2048]{1,0:T(8,128)(2,1)S(1)} %add_convert_fusion.1), channel_id=1, source_target_pairs={{8,0},{16,8},{24,16},{28,24},{20,28},{12,20},{4,12},{0,4},{9,1},{1... | collective-permute-start | bytes 811016 | tf_op jit(solution)/shard_map/ppermute | solution.py:672
  172.1 6.8 %collective-permute-start.17 = (bf16[66,2048]{1,0:T(8,128)(2,1)S(1)}, bf16[66,2048]{1,0:T(8,128)(2,1)S(1)}, u32[]{:S(2)}, u32[]{:S(2)}) collective-permute-start(bf16[66,2048]{1,0:T(8,128)(2,1)S(1)} %add_convert_fusion.3), channel_id=1, source_target_pairs={{0,8},{8,16},{16,24},{24,28},{28,20},{20,12},{12,4},{4,0},{1,9},{9... | collective-permute-start | bytes 811016 | tf_op jit(solution)/shard_map/ppermute | solution.py:671

commit v3 on v2

--- a/solution.py
+++ b/solution.py
@@ -82,17 +82,26 @@
             pltpu.VMEM((chunks * CHUNK, 2 * HD), BF16),
             pltpu.SemaphoreType.DMA((chunks * (CHUNK // PAGE),)),
         ],
-        compiler_params=pltpu.CompilerParams(vmem_limit_bytes=32 * 2**20),
+        compiler_params=pltpu.CompilerParams(vmem_limit_bytes=60 * 2**20),
         cost_estimate=pl.CostEstimate(flops=2 * 10**9, bytes_accessed=6 * 2**20, transcendentals=0),
     )(length, pages, pool)
 
 
-def prefill_kernel(positions, scal, msg, old_flipped, old_values, decoded, out, flipped, values, queries, scores, top, total):
+def prefill_kernel(
+    positions, scal, msg, flipped_in, values_in, decoded, out,
+    old_flipped, old_values, flipped, values, queries, scores, top, total, sems,
+):
     blocks = msg.shape[0]
     stretch = blocks * positions
     half = positions // 2
     used = pl.cdiv(scal[0], CHUNK)
     steps = stretch // CHUNK
+    loads = [
+        pltpu.make_async_copy(flipped_in, old_flipped, sems.at[0]),
+        pltpu.make_async_copy(values_in, old_values, sems.at[1]),
+    ]
+    for load in loads:
+        load.start()
 
     @pl.loop(0, blocks)
     def _(b):
@@ -154,6 +163,8 @@
             out[i * (CHUNK // positions) + k, 0:half, :] = jnp.concatenate([part[:half], part[half:]], axis=1)
 
     top[...] = jnp.full_like(top, -jnp.inf)
+    for load in loads:
+        load.wait()
 
     @pl.loop(0, used)
     def _(c):
@@ -200,17 +211,20 @@
     return pl.pallas_call(
         functools.partial(prefill_kernel, positions),
         out_shape=jax.ShapeDtypeStruct((blocks, positions // 2 + slots * features // 128, 2 * HD), BF16),
-        in_specs=[SMEM, VMEM, VMEM, VMEM, VMEM],
+        in_specs=[SMEM, VMEM, ANY, ANY, VMEM],
         out_specs=VMEM,
         scratch_shapes=[
+            pltpu.VMEM(old_flipped.shape, BF16),
+            pltpu.VMEM(old_values.shape, BF16),
             pltpu.VMEM((steps, 2 * HD, CHUNK), BF16),
             pltpu.VMEM((steps, CHUNK, 2 * HD), BF16),
             pltpu.VMEM((stretch, 2 * HD), BF16),
             pltpu.VMEM((chunks, CHUNK, CHUNK), F32),
             pltpu.VMEM((CHUNK, 128), F32),
             pltpu.VMEM((2, CHUNK, 128), F32),
+            pltpu.SemaphoreType.DMA((2,)),
         ],
-        compiler_params=pltpu.CompilerParams(vmem_limit_bytes=46 * 2**20),
+        compiler_params=pltpu.CompilerParams(vmem_limit_bytes=58 * 2**20),
         cost_estimate=pl.CostEstimate(flops=4 * stretch * keys * HD, bytes_accessed=4 * 2**20, transcendentals=stretch * keys),
     )(length, msg, old_flipped, old_values, decoded)
 
@@ -416,7 +430,9 @@
 
 
 def project_kernel(requests, heads, scal, received, w_out, *rest):
-    outs, rows_in, decode_in = rest[:-2], rest[-2], rest[-1]
+    outs, (rows_in, decode_in, weights, sem) = rest[:-4], rest[-4:]
+    fetch = pltpu.make_async_copy(w_out, weights, sem)
+    fetch.start()
     n_head = len(outs)
     n_tok = received.shape[0]
     units = requests * heads
@@ -453,9 +469,10 @@
                 ]
     for j in range(hosted):
         rows_in[j // share, requests * block_rows + j % share, :] = decode_in[pl.ds(scal[units + j], 1), :][0]
+    fetch.wait()
     for k in range(n_head):
         mine = rows_in[scal[units + hosted + k]].astype(BF16)
-        y = jnp.dot(mine, w_out[...], preferred_element_type=F32).astype(BF16)
+        y = jnp.dot(mine, weights[...], preferred_element_type=F32).astype(BF16)
         outs[k][...] = y[:per]
 
 
@@ -467,13 +484,15 @@
     return pl.pallas_call(
         functools.partial(project_kernel, requests, heads),
         out_shape=[jax.ShapeDtypeStruct((per, width), BF16)] * n_head,
-        in_specs=[SMEM, VMEM, VMEM],
+        in_specs=[SMEM, VMEM, ANY],
         out_specs=[VMEM] * n_head,
         scratch_shapes=[
             pltpu.VMEM((n_head, padded, features), F32),
             pltpu.VMEM((received.shape[0] * hosted, features), F32),
+            pltpu.VMEM(w_out.shape, BF16),
+            pltpu.SemaphoreType.DMA,
         ],
-        compiler_params=pltpu.CompilerParams(vmem_limit_bytes=32 * 2**20),
+        compiler_params=pltpu.CompilerParams(vmem_limit_bytes=56 * 2**20),
         cost_estimate=pl.CostEstimate(flops=2 * n_head * per * features * width, bytes_accessed=4 * 2**20, transcendentals=0),
     )(scal, received, w_out)
 
@@ -502,38 +521,58 @@
     )(own_pre, own_dec, gain, *terms)
 
 
+def finish_kernel(resid, own_left, own_right, *rest):
+    sums, outs = rest[:-2], rest[-2:]
+    middle = own_left.shape[1]
+    first = 0
+    for out in outs:
+        rows = slice(first, first + out.shape[0])
+        first += out.shape[0]
+        for side, own in enumerate((own_left, own_right)):
+            cols = slice(side * middle, (side + 1) * middle)
+            added = own[rows, :].astype(F32)
+            for term in sums[2 * side : 2 * side + 2]:
+                added = added + term[rows, :].astype(F32)
+            out[:, cols] = (resid[rows, cols] + added).astype(BF16)
+
+
+def finish(resid, own, sums, split):
+    per, width = resid.shape
+    return pl.pallas_call(
+        finish_kernel,
+        out_shape=[jax.ShapeDtypeStruct((split, width), BF16), jax.ShapeDtypeStruct((per - split, width), BF16)],
+        in_specs=[VMEM] * 7,
+        out_specs=[VMEM] * 2,
+        compiler_params=pltpu.CompilerParams(vmem_limit_bytes=16 * 2**20),
+        cost_estimate=pl.CostEstimate(flops=10**6, bytes_accessed=2 * 2**20, transcendentals=0),
+    )(resid, *own, *sums)
+
+
 def feed_kernel(count, *refs):
-    rows, (gate_up, down), outs = refs[:count], refs[count : count + 2], refs[count + 2 : 2 * count + 2]
-    weights, down_weights, sems = refs[2 * count + 2 :]
+    rows, (gate_up, down), outs = refs[:count], refs[count : count + 2], refs[count + 2 :]
+    middle = down.shape[1] // 2
     hidden_units = down.shape[0]
     tile = 128 if hidden_units % 128 == 0 else hidden_units
     steps = hidden_units // tile
 
-    def load(step):
-        cols = pl.ds(step * tile, tile)
-        return pltpu.make_async_copy(gate_up.at[:, :, cols], weights.at[:, :, cols], sems.at[step])
-
-    for step in range(steps):
-        load(step).start()
-    down_copy = pltpu.make_async_copy(down, down_weights, sems.at[steps])
-    down_copy.start()
     hidden = [[] for _ in range(count)]
     for step in range(steps):
-        load(step).wait()
         cols = slice(step * tile, (step + 1) * tile)
-        both = jnp.concatenate([weights[0, :, cols], weights[1, :, cols]], axis=1) if tile == 128 else None
+        both = jnp.concatenate([gate_up[0, :, cols], gate_up[1, :, cols]], axis=1) if tile == 128 else None
         for index in range(count):
             if tile == 128:
                 y = jnp.dot(rows[index][...], both, preferred_element_type=F32)
                 gate, upper = y[:, :tile], y[:, tile:]
             else:
-                gate = jnp.dot(rows[index][...], weights[0], preferred_element_type=F32)
-                upper = jnp.dot(rows[index][...], weights[1], preferred_element_type=F32)
+                gate = jnp.dot(rows[index][...], gate_up[0], preferred_element_type=F32)
+                upper = jnp.dot(rows[index][...], gate_up[1], preferred_element_type=F32)
             hidden[index].append((jax.nn.gelu(gate, approximate=True) * upper).astype(BF16))
-    down_copy.wait()
     for index in range(count):
         full = jnp.concatenate(hidden[index], axis=1)
-        outs[index][...] = jnp.dot(full, down_weights[...], preferred_element_type=F32).astype(BF16)
+        for side in range(2):
+            cols = slice(side * middle, (side + 1) * middle)
+            y = jnp.dot(full, down[:, cols], preferred_element_type=F32)
+            outs[2 * index + side][...] = y.astype(BF16)
 
 
 def feed_forward(chunks, gate_up, down):
@@ -542,15 +581,10 @@
     hidden_units = down.shape[0]
     return pl.pallas_call(
         functools.partial(feed_kernel, count),
-        out_shape=[jax.ShapeDtypeStruct((per, width), BF16)] * count,
-        in_specs=[VMEM] * count + [ANY, ANY],
-        out_specs=[VMEM] * count,
-        scratch_shapes=[
-            pltpu.VMEM(gate_up.shape, BF16),
-            pltpu.VMEM(down.shape, BF16),
-            pltpu.SemaphoreType.DMA((hidden_units // 128 + 1,)),
-        ],
-        compiler_params=pltpu.CompilerParams(vmem_limit_bytes=32 * 2**20),
+        out_shape=[jax.ShapeDtypeStruct((per, width // 2), BF16)] * (2 * count),
+        in_specs=[VMEM] * (count + 2),
+        out_specs=[VMEM] * (2 * count),
+        compiler_params=pltpu.CompilerParams(vmem_limit_bytes=24 * 2**20),
         cost_estimate=pl.CostEstimate(
             flops=6 * count * per * width * hidden_units, bytes_accessed=8 * 2**20, transcendentals=count * per * hidden_units
         ),
@@ -607,27 +641,20 @@
     slots = my_tok * hosted + jnp.arange(hosted, dtype=jnp.int32)
     all_requests = jnp.arange(decode_home.shape[0], dtype=jnp.int32)
     anchor = jnp.sum(jnp.where(decode_home[None, :] == slots[:, None], all_requests[None, :], 0), axis=1)
-    anchor_row = ((anchor // hosted) ^ my_tok) * hosted + anchor % hosted
-
-    first = lax.ppermute(decode_states, "tok", [(i, i ^ 1) for i in range(n_tok)])
+
+    copies = jnp.broadcast_to(decode_states[None], (n_tok, hosted, width))
+    rows = lax.all_to_all(copies, "tok", split_axis=0, concat_axis=0, tiled=True).reshape(n_tok * hosted, width)
     messages = qkv_messages(prefill_home, prefill_states.reshape(requests * positions, width), gain, w_three, requests)
-    messages, first = lax.optimization_barrier((messages, first))
-    pair = jnp.concatenate([decode_states, first], axis=0)
-    rows = [pair] + [lax.ppermute(pair, "tok", [(i, i ^ step) for i in range(n_tok)]) for step in range(2, n_tok, 2)]
-    held = lax.optimization_barrier([messages] + rows)
-    messages, rows = held[0], held[1:]
+    messages, rows = lax.optimization_barrier((messages, rows))
     arrived = lax.all_to_all(messages, "tok", split_axis=0, concat_axis=0, tiled=True)
-    rows = jnp.concatenate(rows, axis=0)
     decoded = decode_attention(
-        jnp.concatenate([decode_lengths, anchor_row]), decode_pages, rows, gain, w_three, decode_pool
+        jnp.concatenate([decode_lengths, anchor]), decode_pages, rows, gain, w_three, decode_pool
     )
-    old_keys, old_values = prepare_cache(length, prefill_pages.reshape(-1), prefill_pool)
-    arrived, decoded, old_keys, old_values = lax.optimization_barrier((arrived, decoded, old_keys, old_values))
+    table, decoded = lax.optimization_barrier((prefill_pages.reshape(-1), decoded))
+    old_keys, old_values = prepare_cache(length, table, prefill_pool)
     attn = prefill_attention(length, arrived, old_keys, old_values, decoded)
-    attn, w_gate_up = lax.optimization_barrier((attn, w_gate_up))
     returned = lax.all_to_all(attn, "tok", split_axis=0, concat_axis=0, tiled=True)
     gate_up = jnp.transpose(w_gate_up, (1, 0, 2))
-    returned, gate_up = lax.optimization_barrier((returned, gate_up))
 
     my_slots = lax.dynamic_slice_in_dim(decode_home, my_tok * hosted, hosted, 0)
     targets = my_head ^ jnp.arange(n_head, dtype=jnp.int32)
@@ -656,23 +683,25 @@
         done = feed_forward(waiting, gate_up, w_down)
         up, down, done = lax.optimization_barrier((up, down, done))
         if k == 1:
-            (own_part,) = done
+            own_part = done
         else:
-            minus[k - 1], plus[k - 1] = done
+            minus[k - 1], plus[k - 1] = done[:2], done[2:]
         waiting = [up, down]
-    (minus[far],) = feed_forward([up], gate_up, w_down)
-    plus[far] = minus[far]
-
-    up, down = plus[far], minus[near]
-    for k in range(far - 1, 0, -1):
-        up = joined(plus[k], lax.ppermute(up, "tok", ahead))
-        if k < near:
-            down = joined(minus[k], lax.ppermute(down, "tok", behind))
-    up = lax.ppermute(up, "tok", ahead).astype(F32)
-    down = lax.ppermute(down, "tok", behind).astype(F32)
-    result = (resid + (own_part.astype(F32) + up + down)).astype(BF16)
-    prefill_out = result[: requests * block_rows].reshape(requests, block_rows, width)
-    return (prefill_out, result[requests * block_rows :])
+    farthest = feed_forward([up], gate_up, w_down)
+
+    def chain(part, table, side, hops, steps):
+        for k in range(hops, 0, -1):
+            part = joined(table[k][side], lax.ppermute(part, "tok", steps))
+        return lax.ppermute(part, "tok", steps)
+
+    sums = [
+        chain(minus[near][0], minus, 0, near - 1, behind),
+        chain(farthest[0], plus, 0, far - 1, ahead),
+        chain(plus[near][1], plus, 1, near - 1, ahead),
+        chain(farthest[1], minus, 1, far - 1, behind),
+    ]
+    pre, dec = finish(resid, own_part, sums, requests * block_rows)
+    return (pre.reshape(requests, block_rows, width), dec)
 
 
 def solution(mesh):

time: 181 us -> 166 us (0.917)
  local copies, waits for them, and re-layouts: 18.7 us -> 9.02 us
  starting transfers between devices: 34.4 us -> 41 us
  waiting for transfers between devices: 46.2 us -> 39.9 us
  Pallas kernels: 75.7 us -> 71.2 us
    ppermute x11 -> x14, waiting for transfers between devices: 31.5 us -> 10.8 us  [the longest x10 7.58 us: chain(): part = joined(table[k][side], lax.ppermute(part, 'tok', steps))]
    pallas_call x5, Pallas kernels: 22.1 us -> 12.1 us  [feed_forward(): pl.pallas_call(functools.partial(feed_kernel, count), out_shape=[jax.Shap...]
    all_to_all x0 -> x1, starting transfers between devices: none -> 7.28 us  [shards(): lax.all_to_all(copies, 'tok', split_axis=0, concat_axis=0, tiled=True)]
    ppermute x4, waiting for transfers between devices: 2.95 us -> 8.56 us  [shards(): up = lax.ppermute(up, 'tok', ahead)]
    optimization_barrier x1 -> x0, local copies, waits for them, and re-layouts: 5.48 us -> none  [shards(): attn, w_gate_up = lax.optimization_barrier((attn, w_gate_up))]
    all_to_all x1, waiting for transfers between devices: 3.55 us -> 8.72 us  [shards(): lax.all_to_all(attn, 'tok', split_axis=0, concat_axis=0, tiled=True)]
    unnamed x33 -> x19, local copies, waits for them, and re-layouts: 10.1 us -> 5.73 us
    all_to_all x0 -> x1, waiting for transfers between devices: none -> 2.92 us  [shards(): lax.all_to_all(copies, 'tok', split_axis=0, concat_axis=0, tiled=True)]
  transfers between devices with their start and end apart: 23 -> 27, of which waited for: 16 -> 20; matrix products, arithmetic and copies ran while one was open for 7% -> 5% of each run, Pallas kernels for 25% -> 25%
where the time goes in v3:
time: 166 us; the launch traced here: 165 us
  Pallas kernels  71.2 us (43%)
  starting transfers between devices  41 us (25%)
  waiting for transfers between devices  39.9 us (24%)
  local copies, waits for them, and re-layouts  9.02 us (5%)
  other arithmetic  2.78 us (2%)
    pallas_call x1, Pallas kernels, prefill_attention(): pl.pallas_call(functools.partial(prefill_kernel, positions), out_shape=ja...  24.5 us
    pallas_call x1, Pallas kernels, decode_attention(): pl.pallas_call(functools.partial(decode_kernel, heads), out_shape=jax.Sha...  18.1 us
    pallas_call x5, Pallas kernels, feed_forward(): pl.pallas_call(functools.partial(feed_kernel, count), out_shape=[jax.Shap...  12.1 us
    ppermute x10, starting transfers between devices, chain(): part = joined(table[k][side], lax.ppermute(part, 'tok', steps))  10.2 us
    all_to_all x1, waiting for transfers between devices, shards(): lax.all_to_all(attn, 'tok', split_axis=0, concat_axis=0, tiled=True)  8.72 us
    ppermute x4, waiting for transfers between devices, shards(): up = lax.ppermute(up, 'tok', ahead)  8.56 us
    ppermute x10, waiting for transfers between devices, chain(): part = joined(table[k][side], lax.ppermute(part, 'tok', steps))  7.58 us
    all_to_all x1, starting transfers between devices, shards(): lax.all_to_all(copies, 'tok', split_axis=0, concat_axis=0, tiled=True)  7.28 us
  transfers between devices with their start and end apart: 27, of which 20 were waited for; matrix products, arithmetic and copies ran while one was open for 5% of the time, Pallas kernels for 25%

profile of v3, /device:TPU:0, one launch (start us, length us, event | category | flops | bytes accessed | tf_op | source)
XLA Modules:
  0.0 165.4 jit_solution(4634586449167991817)
XLA Ops:
  0.6 1.5 broadcast_in_dim.16
  2.1 7.3 %all-to-all-start = ((bf16[8,8,2048]{2,1,0:T(8,128)(2,1)}), bf16[8,8,2048]{2,1,0:T(8,128)(2,1)S(1)}, u32[]{:S(2)}, u32[]{:S(2)}) async-start(bf16[8,8,2048]{2,1,0:T(8,128)(2,1)} %broadcast_in_dim.16), calls=%async_computation | async-start | bytes 524288 | tf_op jit(solution)/shard_map/all_to_all | solution.py:646
  9.4 6.0 %shard_map.167 = bf16[8,384,128]{2,1,0:T(8,128)(2,1)} custom-call(s32[8]{0:T(128)} %home.1, f32[1,2048]{1,0:T(1,128)} %bitcast.22, bf16[256,2048]{1,0:T(8,128)(2,1)} %bitcast.20, bf16[3,2048,512]{2,1,0:T(8,128)(2,1)} %bitcast.18), custom_call_target="tpu_custom_call" | custom-call | flops 1610612736 | bytes 10485760 | tf_op jit(solution)/shard_map/pallas_call | solution.py:416
  15.4 2.9 %all-to-all-done = bf16[8,8,2048]{2,1,0:T(8,128)(2,1)S(1)} async-done(((bf16[8,8,2048]{2,1,0:T(8,128)(2,1)}), bf16[8,8,2048]{2,1,0:T(8,128)(2,1)S(1)}, u32[]{:S(2)}, u32[]{:S(2)}) %all-to-all-start) | async-done | bytes 262176 | tf_op jit(solution)/shard_map/all_to_all | solution.py:646
  18.3 3.6 %all-to-all-start.1 = ((bf16[8,384,128]{2,1,0:T(8,128)(2,1)}), bf16[8,384,128]{2,1,0:T(8,128)(2,1)S(1)}, u32[]{:S(2)}, u32[]{:S(2)}) async-start(bf16[8,384,128]{2,1,0:T(8,128)(2,1)} %shard_map.167), calls=%async_computation.1 | async-start | bytes 1572864 | tf_op jit(solution)/shard_map/all_to_all | solution.py:649
  23.3 18.1 %shard_map.168.decoded = f32[8,512]{1,0:T(8,128)} custom-call(s32[16]{0:T(128)} %pad_add_fusion.1.scal, s32[8,32]{1,0:T(8,128)} %pages.1, bf16[64,2048]{1,0:T(8,128)(2,1)} %bitcast.21, f32[1,2048]{1,0:T(1,128)} %bitcast.23, bf16[3,2048,512]{2,1,0:T(8,128)(2,1)} %bitcast.19, bf16[64,128,1024]{2,1,0:T(8,128)(2,1)} %pool.2), custom_call_target="tpu_custom_call" | custom-call | flops 2000000000 | bytes 23068672 | tf_op jit(solution)/shard_map/pallas_call | solution.py:354
  41.5 4.5 %shard_map.169 = (bf16[6,128,1024]{2,1,0:T(8,128)(2,1)}, bf16[6,1024,128]{2,1,0:T(8,128)(2,1)}) custom-call(s32[1]{0:T(128)S(6)} %copy.22.scal, s32[48]{0:T(128)} %bitcast.25, bf16[48,128,128]{2,1,0:T(8,128)(2,1)} %pool.3), custom_call_target="tpu_custom_call" | custom-call | flops 2000000000 | bytes 6291456 | tf_op jit(solution)/shard_map/pallas_call | solution.py:73
  45.9 0.9 copy-done.5
  46.8 24.5 %shard_map.170 = bf16[8,160,128]{2,1,0:T(8,128)(2,1)} custom-call(s32[1]{0:T(128)S(6)} %copy.22.scal, bf16[8,384,128]{2,1,0:T(8,128)(2,1)} %copy-done.5, bf16[6,128,1024]{2,1,0:T(8,128)(2,1)} %get-tuple-element.56.flipped_in, bf16[6,1024,128]{2,1,0:T(8,128)(2,1)} %get-tuple-element.57.values_in, f32[8,512]{1,0:T(8,128)} %shard_map.168.decoded), custom_call_target="tpu_custom_call" | custom-call | flops 4294967296 | bytes 4194304 | tf_op jit(solution)/shard_map/pallas_call | solution.py:211
  71.3 5.9 %all-to-all-start.2 = ((bf16[8,160,128]{2,1,0:T(8,128)(2,1)}), bf16[8,160,128]{2,1,0:T(8,128)(2,1)S(1)}, u32[]{:S(2)}, u32[]{:S(2)}) async-start(bf16[8,160,128]{2,1,0:T(8,128)(2,1)} %shard_map.170), calls=%async_computation.2 | async-start | bytes 655360 | tf_op jit(solution)/shard_map/all_to_all | solution.py:656
  78.0 8.7 %all-to-all-done.2.received = bf16[8,160,128]{2,1,0:T(8,128)(2,1)S(1)} async-done(((bf16[8,160,128]{2,1,0:T(8,128)(2,1)}), bf16[8,160,128]{2,1,0:T(8,128)(2,1)S(1)}, u32[]{:S(2)}, u32[]{:S(2)}) %all-to-all-start.2) | async-done | bytes 327712 | tf_op jit(solution)/shard_map/all_to_all | solution.py:656
  87.4 4.9 %shard_map.171 = (bf16[66,2048]{1,0:T(8,128)(2,1)}, bf16[66,2048]{1,0:T(8,128)(2,1)}, bf16[66,2048]{1,0:T(8,128)(2,1)}, bf16[66,2048]{1,0:T(8,128)(2,1)}) custom-call(s32[20]{0:T(128)} %pad_add_fusion.scal, bf16[8,160,128]{2,1,0:T(8,128)(2,1)} %copy-done.3, bf16[512,2048]{1,0:T(8,128)(2,1)} %w_out.1), custom_call_target="tpu_custom_call" | custom-call | flops 553648128 | bytes 4194304 | tf_op jit(solution)/shard_map/pallas_call | solution.py:484
  92.9 1.3 collective-permute-done
  94.2 1.0 add_convert_fusion
  95.2 1.6 collective-permute-start.1
  96.8 0.8 constant_dynamic-slice_fusion.own_dec
  97.5 1.0 dynamic-slice_bitcast_fusion.own_pre
  98.5 5.8 %collective-permute-done.1.rest_1_ = bf16[66,2048]{1,0:T(8,128)(2,1)S(1)} collective-permute-done((bf16[66,2048]{1,0:T(8,128)(2,1)S(1)}, bf16[66,2048]{1,0:T(8,128)(2,1)S(1)}, u32[]{:S(2)}, u32[]{:S(2)}) %collective-permute-start.1) | collective-permute-done | bytes 270368 | tf_op jit(solution)/shard_map/ppermute | solution.py:672
  104.3 1.0 copy-done.1
  105.6 1.5 collective-permute-start.4
  107.7 3.1 %copy.21 = bf16[2048,2,640]{2,0,1:T(8,128)(2,1)S(1)} copy(bf16[2048,2,640]{2,1,0:T(2,128)(2,1)} %param.22) | data formatting | bytes 10485760 | tf_op args[6]
  110.8 1.7 %shard_map.173 = (bf16[66,1024]{1,0:T(8,128)(2,1)S(1)}, bf16[66,1024]{1,0:T(8,128)(2,1)S(1)}) custom-call(bf16[66,2048]{1,0:T(8,128)(2,1)S(1)} %get-tuple-element.64.refs_0_, bf16[2,2048,640]{2,1,0:T(8,128)(2,1)S(1)} %bitcast.12, bf16[640,2048]{1,0:T(8,128)(2,1)S(1)} %copy-done), custom_call_target="tpu_custom_call" | custom-call | flops 519045120 | bytes 8388608 | tf_op jit(solution)/shard_map/pallas_call | solution.py:582
  112.6 1.3 collective-permute-done.4.refs_1_
  113.9 1.2 collective-permute-done.3.refs_0_
  115.6 1.5 collective-permute-start.6
  117.1 2.9 %shard_map.174 = (bf16[66,1024]{1,0:T(8,128)(2,1)S(1)}, bf16[66,1024]{1,0:T(8,128)(2,1)S(1)}, bf16[66,1024]{1,0:T(8,128)(2,1)S(1)}, bf16[66,1024]{1,0:T(8,128)(2,1)S(1)}) custom-call(bf16[66,2048]{1,0:T(8,128)(2,1)S(1)} %collective-permute-done.3.refs_0_, bf16[66,2048]{1,0:T(8,128)(2,1)S(1)} %collective-permute-done.4.refs_1_, ...), custom_call_target="tpu_custom_call" | custom-call | flops 1038090240 | bytes 8388608 | tf_op jit(solution)/shard_map/pallas_call | solution.py:582
  120.0 2.2 %collective-permute-done.5.refs_0_ = bf16[66,2048]{1,0:T(8,128)(2,1)S(1)} collective-permute-done((bf16[66,2048]{1,0:T(8,128)(2,1)S(1)}, bf16[66,2048]{1,0:T(8,128)(2,1)S(1)}, u32[]{:S(2)}, u32[]{:S(2)}) %collective-permute-start.5) | collective-permute-done | bytes 270368 | tf_op jit(solution)/shard_map/ppermute | solution.py:680
  122.4 1.2 collective-permute-start.7
  123.5 0.8 collective-permute-start.8
  124.4 2.9 %shard_map.175 = (bf16[66,1024]{1,0:T(8,128)(2,1)S(1)}, bf16[66,1024]{1,0:T(8,128)(2,1)S(1)}, bf16[66,1024]{1,0:T(8,128)(2,1)S(1)}, bf16[66,1024]{1,0:T(8,128)(2,1)S(1)}) custom-call(bf16[66,2048]{1,0:T(8,128)(2,1)S(1)} %collective-permute-done.5.refs_0_, bf16[66,2048]{1,0:T(8,128)(2,1)S(1)} %collective-permute-done.6.refs_1_, ...), custom_call_target="tpu_custom_call" | custom-call | flops 1038090240 | bytes 8388608 | tf_op jit(solution)/shard_map/pallas_call | solution.py:582
  127.3 2.6 %collective-permute-done.7.refs_0_ = bf16[66,2048]{1,0:T(8,128)(2,1)S(1)} collective-permute-done((bf16[66,2048]{1,0:T(8,128)(2,1)S(1)}, bf16[66,2048]{1,0:T(8,128)(2,1)S(1)}, u32[]{:S(2)}, u32[]{:S(2)}) %collective-permute-start.7) | collective-permute-done | bytes 270368 | tf_op jit(solution)/shard_map/ppermute | solution.py:680
  130.3 1.2 collective-permute-start.9
  131.5 2.9 %shard_map.176 = (bf16[66,1024]{1,0:T(8,128)(2,1)S(1)}, bf16[66,1024]{1,0:T(8,128)(2,1)S(1)}, bf16[66,1024]{1,0:T(8,128)(2,1)S(1)}, bf16[66,1024]{1,0:T(8,128)(2,1)S(1)}) custom-call(bf16[66,2048]{1,0:T(8,128)(2,1)S(1)} %collective-permute-done.7.refs_0_, bf16[66,2048]{1,0:T(8,128)(2,1)S(1)} %collective-permute-done.8.refs_1_, ...), custom_call_target="tpu_custom_call" | custom-call | flops 1038090240 | bytes 8388608 | tf_op jit(solution)/shard_map/pallas_call | solution.py:582
  134.4 2.6 %collective-permute-done.9.refs_0_ = bf16[66,2048]{1,0:T(8,128)(2,1)S(1)} collective-permute-done((bf16[66,2048]{1,0:T(8,128)(2,1)S(1)}, bf16[66,2048]{1,0:T(8,128)(2,1)S(1)}, u32[]{:S(2)}, u32[]{:S(2)}) %collective-permute-start.9) | collective-permute-done | bytes 270368 | tf_op jit(solution)/shard_map/ppermute | solution.py:680
  137.0 1.9 %collective-permute-start.10 = (bf16[66,1024]{1,0:T(8,128)(2,1)S(1)}, bf16[66,1024]{1,0:T(8,128)(2,1)S(1)}, u32[]{:S(2)}, u32[]{:S(2)}) collective-permute-start(bf16[66,1024]{1,0:T(8,128)(2,1)S(1)} %get-tuple-element.89), channel_id=1, source_target_pairs={{8,0},{16,8},{24,16},{28,24},{20,28},{12,20},{4,12},{0,4},{9,1},{1... | collective-permute-start | bytes 405512 | tf_op jit(solution)/shard_map/ppermute | solution.py:694
  138.9 1.7 %shard_map.177 = (bf16[66,1024]{1,0:T(8,128)(2,1)S(1)}, bf16[66,1024]{1,0:T(8,128)(2,1)S(1)}) custom-call(bf16[66,2048]{1,0:T(8,128)(2,1)S(1)} %collective-permute-done.9.refs_0_, bf16[2,2048,640]{2,1,0:T(8,128)(2,1)S(1)} %bitcast.16, bf16[640,2048]{1,0:T(8,128)(2,1)S(1)} %copy-done), custom_call_target="tpu_custom_call" | custom-call | flops 519045120 | bytes 8388608 | tf_op jit(solution)/shard_map/pallas_call | solution.py:582
  140.8 1.9 %collective-permute-start.20 = (bf16[66,1024]{1,0:T(8,128)(2,1)S(1)}, bf16[66,1024]{1,0:T(8,128)(2,1)S(1)}, u32[]{:S(2)}, u32[]{:S(2)}) collective-permute-start(bf16[66,1024]{1,0:T(8,128)(2,1)S(1)} %get-tuple-element.101), channel_id=1, source_target_pairs={{8,0},{16,8},{24,16},{28,24},{20,28},{12,20},{4,12},{0,4},{9,1},{1... | collective-permute-start | bytes 405512 | tf_op jit(solution)/shard_map/ppermute | solution.py:694
  143.1 1.7 %collective-permute-start.11 = (bf16[66,1024]{1,0:T(8,128)(2,1)S(1)}, bf16[66,1024]{1,0:T(8,128)(2,1)S(1)}, u32[]{:S(2)}, u32[]{:S(2)}) collective-permute-start(bf16[66,1024]{1,0:T(8,128)(2,1)S(1)} %add_convert_fusion.10), channel_id=1, source_target_pairs={{8,0},{16,8},{24,16},{28,24},{20,28},{12,20},{4,12},{0,4},{9,1},{1... | collective-permute-start | bytes 405512 | tf_op jit(solution)/shard_map/ppermute | solution.py:694
  144.9 2.5 %collective-permute-done.13 = bf16[66,1024]{1,0:T(8,128)(2,1)S(1)} collective-permute-done((bf16[66,1024]{1,0:T(8,128)(2,1)S(1)}, bf16[66,1024]{1,0:T(8,128)(2,1)S(1)}, u32[]{:S(2)}, u32[]{:S(2)}) %collective-permute-start.13) | collective-permute-done | bytes 135200 | tf_op jit(solution)/shard_map/ppermute | solution.py:694
  147.6 2.0 %collective-permute-start.21 = (bf16[66,1024]{1,0:T(8,128)(2,1)S(1)}, bf16[66,1024]{1,0:T(8,128)(2,1)S(1)}, u32[]{:S(2)}, u32[]{:S(2)}) collective-permute-start(bf16[66,1024]{1,0:T(8,128)(2,1)S(1)} %add_convert_fusion.3), channel_id=1, source_target_pairs={{8,0},{16,8},{24,16},{28,24},{20,28},{12,20},{4,12},{0,4},{9,1},{1... | collective-permute-start | bytes 405512 | tf_op jit(solution)/shard_map/ppermute | solution.py:694
  149.6 0.9 collective-permute-done.17
  150.7 2.0 %collective-permute-start.12 = (bf16[66,1024]{1,0:T(8,128)(2,1)S(1)}, bf16[66,1024]{1,0:T(8,128)(2,1)S(1)}, u32[]{:S(2)}, u32[]{:S(2)}) collective-permute-start(bf16[66,1024]{1,0:T(8,128)(2,1)S(1)} %add_convert_fusion.9), channel_id=1, source_target_pairs={{8,0},{16,8},{24,16},{28,24},{20,28},{12,20},{4,12},{0,4},{9,1},{1... | collective-permute-start | bytes 405512 | tf_op jit(solution)/shard_map/ppermute | solution.py:695
  152.7 1.3 collective-permute-done.14
  154.2 2.0 %collective-permute-start.22 = (bf16[66,1024]{1,0:T(8,128)(2,1)S(1)}, bf16[66,1024]{1,0:T(8,128)(2,1)S(1)}, u32[]{:S(2)}, u32[]{:S(2)}) collective-permute-start(bf16[66,1024]{1,0:T(8,128)(2,1)S(1)} %add_convert_fusion.2), channel_id=1, source_target_pairs={{8,0},{16,8},{24,16},{28,24},{20,28},{12,20},{4,12},{0,4},{9,1},{1... | collective-permute-start | bytes 405512 | tf_op jit(solution)/shard_map/ppermute | solution.py:694
  156.7 2.5 %collective-permute-done.15 = bf16[66,1024]{1,0:T(8,128)(2,1)S(1)} collective-permute-done((bf16[66,1024]{1,0:T(8,128)(2,1)S(1)}, bf16[66,1024]{1,0:T(8,128)(2,1)S(1)}, u32[]{:S(2)}, u32[]{:S(2)}) %collective-permute-start.15) | collective-permute-done | bytes 135200 | tf_op jit(solution)/shard_map/ppermute | solution.py:694
  159.4 2.0 %collective-permute-start.23 = (bf16[66,1024]{1,0:T(8,128)(2,1)S(1)}, bf16[66,1024]{1,0:T(8,128)(2,1)S(1)}, u32[]{:S(2)}, u32[]{:S(2)}) collective-permute-start(bf16[66,1024]{1,0:T(8,128)(2,1)S(1)} %add_convert_fusion.1), channel_id=1, source_target_pairs={{8,0},{16,8},{24,16},{28,24},{20,28},{12,20},{4,12},{0,4},{9,1},{1... | collective-permute-start | bytes 405512 | tf_op jit(solution)/shard_map/ppermute | solution.py:695
  161.6 2.9 %collective-permute-done.16.rest_1_ = bf16[66,1024]{1,0:T(8,128)(2,1)S(1)} collective-permute-done((bf16[66,1024]{1,0:T(8,128)(2,1)S(1)}, bf16[66,1024]{1,0:T(8,128)(2,1)S(1)}, u32[]{:S(2)}, u32[]{:S(2)}) %collective-permute-start.16) | collective-permute-done | bytes 135200 | tf_op jit(solution)/shard_map/ppermute | solution.py:695
  164.6 0.8 shard_map.178
  (57 shorter events, 6.9 us)
Async XLA Ops:
  2.1 16.2 %all-to-all-start = ((bf16[8,8,2048]{2,1,0:T(8,128)(2,1)}), bf16[8,8,2048]{2,1,0:T(8,128)(2,1)S(1)}, u32[]{:S(2)}, u32[]{:S(2)}) async-start(bf16[8,8,2048]{2,1,0:T(8,128)(2,1)} %broadcast_in_dim.16), calls=%async_computation | async-start | bytes 524288 | tf_op jit(solution)/shard_map/all_to_all | solution.py:646
  9.4 13.2 %copy-start.8 = (s32[64]{0:T(128)S(1)}, s32[64]{0:T(128)}, u32[]{:S(2)}) copy-start(s32[64]{0:T(128)} %param.31) | copy-start | bytes 772
  9.4 13.4 %copy-start.7 = (s32[8]{0:T(128)S(1)}, s32[8]{0:T(128)}, u32[]{:S(2)}) copy-start(s32[8]{0:T(128)} %param.30) | copy-start | bytes 100
  18.3 5.0 %copy-start.4 = (bf16[8,8,2048]{2,1,0:T(8,128)(2,1)}, bf16[8,8,2048]{2,1,0:T(8,128)(2,1)S(1)}, u32[]{:S(2)}) copy-start(bf16[8,8,2048]{2,1,0:T(8,128)(2,1)S(1)} %all-to-all-done) | copy-start | bytes 786436
  18.3 27.6 %all-to-all-start.1 = ((bf16[8,384,128]{2,1,0:T(8,128)(2,1)}), bf16[8,384,128]{2,1,0:T(8,128)(2,1)S(1)}, u32[]{:S(2)}, u32[]{:S(2)}) async-start(bf16[8,384,128]{2,1,0:T(8,128)(2,1)} %shard_map.167), calls=%async_computation.1 | async-start | bytes 1572864 | tf_op jit(solution)/shard_map/all_to_all | solution.py:649
  45.9 0.9 copy-start.5
  46.8 30.6 %copy-start.6 = (s32[8]{0:T(128)S(1)}, s32[8]{0:T(128)}, u32[]{:S(2)}) copy-start(s32[8]{0:T(128)} %home.1) | copy-start | bytes 100
  71.3 33.0 %copy-start.2 = (f32[2048]{0:T(1024)S(1)}, f32[2048]{0:T(1024)}, u32[]{:S(2)}) copy-start(f32[2048]{0:T(1024)} %param.21) | copy-start | bytes 24580
  71.3 15.3 %all-to-all-start.2 = ((bf16[8,160,128]{2,1,0:T(8,128)(2,1)}), bf16[8,160,128]{2,1,0:T(8,128)(2,1)S(1)}, u32[]{:S(2)}, u32[]{:S(2)}) async-start(bf16[8,160,128]{2,1,0:T(8,128)(2,1)} %shard_map.170), calls=%async_computation.2 | async-start | bytes 655360 | tf_op jit(solution)/shard_map/all_to_all | solution.py:656
  86.7 0.7 copy-start.3
  92.3 1.9 %collective-permute-start = (bf16[66,2048]{1,0:T(8,128)(2,1)}, bf16[66,2048]{1,0:T(8,128)(2,1)S(1)}, u32[]{:S(2)}, u32[]{:S(2)}) collective-permute-start(bf16[66,2048]{1,0:T(8,128)(2,1)} %get-tuple-element.61), channel_id=1, source_target_pairs={{0,1},{1,0},{2,3},{3,2},{4,5},{5,4},{6,7},{7,6},{8,9},{9,8},{10,11... | collective-permute-start | bytes 811016 | tf_op jit(solution)/shard_map/ppermute | solution.py:671
  92.4 6.1 %collective-permute-start.2 = (bf16[66,2048]{1,0:T(8,128)(2,1)}, bf16[66,2048]{1,0:T(8,128)(2,1)S(1)}, u32[]{:S(2)}, u32[]{:S(2)}) collective-permute-start(bf16[66,2048]{1,0:T(8,128)(2,1)} %get-tuple-element.62), channel_id=1, source_target_pairs={{0,1},{1,0},{2,3},{3,2},{4,5},{5,4},{6,7},{7,6},{8,9},{9,8},{10,11... | collective-permute-start | bytes 811016 | tf_op jit(solution)/shard_map/ppermute | solution.py:673
  95.2 9.1 %collective-permute-start.1 = (bf16[66,2048]{1,0:T(8,128)(2,1)S(1)}, bf16[66,2048]{1,0:T(8,128)(2,1)S(1)}, u32[]{:S(2)}, u32[]{:S(2)}) collective-permute-start(bf16[66,2048]{1,0:T(8,128)(2,1)S(1)} %add_convert_fusion), channel_id=1, source_target_pairs={{0,2},{1,3},{2,0},{3,1},{4,6},{5,7},{6,4},{7,5},{8,10},{9,11},{10,... | collective-permute-start | bytes 811016 | tf_op jit(solution)/shard_map/ppermute | solution.py:672
  104.3 1.0 copy-start.1
  105.6 5.2 %copy-start = (bf16[640,2048]{1,0:T(8,128)(2,1)S(1)}, bf16[640,2048]{1,0:T(8,128)(2,1)}, u32[]{:S(2)}) copy-start(bf16[640,2048]{1,0:T(8,128)(2,1)} %refs_2_.3) | copy-start | bytes 7864324
  105.6 8.3 %collective-permute-start.4 = (bf16[66,2048]{1,0:T(8,128)(2,1)S(1)}, bf16[66,2048]{1,0:T(8,128)(2,1)S(1)}, u32[]{:S(2)}, u32[]{:S(2)}) collective-permute-start(bf16[66,2048]{1,0:T(8,128)(2,1)S(1)} %get-tuple-element.64.refs_0_), channel_id=1, source_target_pairs={{8,0},{16,8},{24,16},{28,24},{20,28},{12,20},{4,12},{0,4},{9,1},{1... | collective-permute-start | bytes 811016 | tf_op jit(solution)/shard_map/ppermute | solution.py:682
  107.1 7.9 %collective-permute-start.3 = (bf16[66,2048]{1,0:T(8,128)(2,1)S(1)}, bf16[66,2048]{1,0:T(8,128)(2,1)S(1)}, u32[]{:S(2)}, u32[]{:S(2)}) collective-permute-start(bf16[66,2048]{1,0:T(8,128)(2,1)S(1)} %get-tuple-element.64.refs_0_), channel_id=1, source_target_pairs={{0,8},{8,16},{16,24},{24,28},{28,20},{20,12},{12,4},{4,0},{1,9},{9... | collective-permute-start | bytes 811016 | tf_op jit(solution)/shard_map/ppermute | solution.py:680
  115.1 7.1 %collective-permute-start.5 = (bf16[66,2048]{1,0:T(8,128)(2,1)S(1)}, bf16[66,2048]{1,0:T(8,128)(2,1)S(1)}, u32[]{:S(2)}, u32[]{:S(2)}) collective-permute-start(bf16[66,2048]{1,0:T(8,128)(2,1)S(1)} %collective-permute-done.3.refs_0_), channel_id=1, source_target_pairs={{0,8},{8,16},{16,24},{24,28},{28,20},{20,12},{12,4},{4,0},{1,9},{9... | collective-permute-start | bytes 811016 | tf_op jit(solution)/shard_map/ppermute | solution.py:680
  115.6 6.7 %collective-permute-start.6 = (bf16[66,2048]{1,0:T(8,128)(2,1)S(1)}, bf16[66,2048]{1,0:T(8,128)(2,1)S(1)}, u32[]{:S(2)}, u32[]{:S(2)}) collective-permute-start(bf16[66,2048]{1,0:T(8,128)(2,1)S(1)} %collective-permute-done.4.refs_1_), channel_id=1, source_target_pairs={{8,0},{16,8},{24,16},{28,24},{20,28},{12,20},{4,12},{0,4},{9,1},{1... | collective-permute-start | bytes 811016 | tf_op jit(solution)/shard_map/ppermute | solution.py:682
  122.4 7.5 %collective-permute-start.7 = (bf16[66,2048]{1,0:T(8,128)(2,1)S(1)}, bf16[66,2048]{1,0:T(8,128)(2,1)S(1)}, u32[]{:S(2)}, u32[]{:S(2)}) collective-permute-start(bf16[66,2048]{1,0:T(8,128)(2,1)S(1)} %collective-permute-done.5.refs_0_), channel_id=1, source_target_pairs={{0,8},{8,16},{16,24},{24,28},{28,20},{20,12},{12,4},{4,0},{1,9},{9... | collective-permute-start | bytes 811016 | tf_op jit(solution)/shard_map/ppermute | solution.py:680
  123.5 6.7 %collective-permute-start.8 = (bf16[66,2048]{1,0:T(8,128)(2,1)S(1)}, bf16[66,2048]{1,0:T(8,128)(2,1)S(1)}, u32[]{:S(2)}, u32[]{:S(2)}) collective-permute-start(bf16[66,2048]{1,0:T(8,128)(2,1)S(1)} %collective-permute-done.6.refs_1_), channel_id=1, source_target_pairs={{8,0},{16,8},{24,16},{28,24},{20,28},{12,20},{4,12},{0,4},{9,1},{1... | collective-permute-start | bytes 811016 | tf_op jit(solution)/shard_map/ppermute | solution.py:682
  130.3 6.7 %collective-permute-start.9 = (bf16[66,2048]{1,0:T(8,128)(2,1)S(1)}, bf16[66,2048]{1,0:T(8,128)(2,1)S(1)}, u32[]{:S(2)}, u32[]{:S(2)}) collective-permute-start(bf16[66,2048]{1,0:T(8,128)(2,1)S(1)} %collective-permute-done.7.refs_0_), channel_id=1, source_target_pairs={{0,8},{8,16},{16,24},{24,28},{28,20},{20,12},{12,4},{4,0},{1,9},{9... | collective-permute-start | bytes 811016 | tf_op jit(solution)/shard_map/ppermute | solution.py:680
  137.0 6.1 %collective-permute-start.10 = (bf16[66,1024]{1,0:T(8,128)(2,1)S(1)}, bf16[66,1024]{1,0:T(8,128)(2,1)S(1)}, u32[]{:S(2)}, u32[]{:S(2)}) collective-permute-start(bf16[66,1024]{1,0:T(8,128)(2,1)S(1)} %get-tuple-element.89), channel_id=1, source_target_pairs={{8,0},{16,8},{24,16},{28,24},{20,28},{12,20},{4,12},{0,4},{9,1},{1... | collective-permute-start | bytes 405512 | tf_op jit(solution)/shard_map/ppermute | solution.py:694
  140.6 6.7 %collective-permute-start.13 = (bf16[66,1024]{1,0:T(8,128)(2,1)S(1)}, bf16[66,1024]{1,0:T(8,128)(2,1)S(1)}, u32[]{:S(2)}, u32[]{:S(2)}) collective-permute-start(bf16[66,1024]{1,0:T(8,128)(2,1)S(1)} %get-tuple-element.94), channel_id=1, source_target_pairs={{0,8},{8,16},{16,24},{24,28},{28,20},{20,12},{12,4},{4,0},{1,9},{9... | collective-permute-start | bytes 405512 | tf_op jit(solution)/shard_map/ppermute | solution.py:694
  140.8 6.7 %collective-permute-start.20 = (bf16[66,1024]{1,0:T(8,128)(2,1)S(1)}, bf16[66,1024]{1,0:T(8,128)(2,1)S(1)}, u32[]{:S(2)}, u32[]{:S(2)}) collective-permute-start(bf16[66,1024]{1,0:T(8,128)(2,1)S(1)} %get-tuple-element.101), channel_id=1, source_target_pairs={{8,0},{16,8},{24,16},{28,24},{20,28},{12,20},{4,12},{0,4},{9,1},{1... | collective-permute-start | bytes 405512 | tf_op jit(solution)/shard_map/ppermute | solution.py:694
  142.7 7.8 %collective-permute-start.17 = (bf16[66,1024]{1,0:T(8,128)(2,1)S(1)}, bf16[66,1024]{1,0:T(8,128)(2,1)S(1)}, u32[]{:S(2)}, u32[]{:S(2)}) collective-permute-start(bf16[66,1024]{1,0:T(8,128)(2,1)S(1)} %get-tuple-element.97), channel_id=1, source_target_pairs={{0,8},{8,16},{16,24},{24,28},{28,20},{20,12},{12,4},{4,0},{1,9},{9... | collective-permute-start | bytes 405512 | tf_op jit(solution)/shard_map/ppermute | solution.py:694
  143.1 7.6 %collective-permute-start.11 = (bf16[66,1024]{1,0:T(8,128)(2,1)S(1)}, bf16[66,1024]{1,0:T(8,128)(2,1)S(1)}, u32[]{:S(2)}, u32[]{:S(2)}) collective-permute-start(bf16[66,1024]{1,0:T(8,128)(2,1)S(1)} %add_convert_fusion.10), channel_id=1, source_target_pairs={{8,0},{16,8},{24,16},{28,24},{20,28},{12,20},{4,12},{0,4},{9,1},{1... | collective-permute-start | bytes 405512 | tf_op jit(solution)/shard_map/ppermute | solution.py:694
  147.4 6.6 %collective-permute-start.14 = (bf16[66,1024]{1,0:T(8,128)(2,1)S(1)}, bf16[66,1024]{1,0:T(8,128)(2,1)S(1)}, u32[]{:S(2)}, u32[]{:S(2)}) collective-permute-start(bf16[66,1024]{1,0:T(8,128)(2,1)S(1)} %add_convert_fusion.8), channel_id=1, source_target_pairs={{0,8},{8,16},{16,24},{24,28},{28,20},{20,12},{12,4},{4,0},{1,9},{9... | collective-permute-start | bytes 405512 | tf_op jit(solution)/shard_map/ppermute | solution.py:694
  147.6 6.6 %collective-permute-start.21 = (bf16[66,1024]{1,0:T(8,128)(2,1)S(1)}, bf16[66,1024]{1,0:T(8,128)(2,1)S(1)}, u32[]{:S(2)}, u32[]{:S(2)}) collective-permute-start(bf16[66,1024]{1,0:T(8,128)(2,1)S(1)} %add_convert_fusion.3), channel_id=1, source_target_pairs={{8,0},{16,8},{24,16},{28,24},{20,28},{12,20},{4,12},{0,4},{9,1},{1... | collective-permute-start | bytes 405512 | tf_op jit(solution)/shard_map/ppermute | solution.py:694
  150.5 5.8 %collective-permute-start.18 = (bf16[66,1024]{1,0:T(8,128)(2,1)S(1)}, bf16[66,1024]{1,0:T(8,128)(2,1)S(1)}, u32[]{:S(2)}, u32[]{:S(2)}) collective-permute-start(bf16[66,1024]{1,0:T(8,128)(2,1)S(1)} %add_convert_fusion.5), channel_id=1, source_target_pairs={{0,8},{8,16},{16,24},{24,28},{28,20},{20,12},{12,4},{4,0},{1,9},{9... | collective-permute-start | bytes 405512 | tf_op jit(solution)/shard_map/ppermute | solution.py:694
  150.7 10.7 %collective-permute-start.12 = (bf16[66,1024]{1,0:T(8,128)(2,1)S(1)}, bf16[66,1024]{1,0:T(8,128)(2,1)S(1)}, u32[]{:S(2)}, u32[]{:S(2)}) collective-permute-start(bf16[66,1024]{1,0:T(8,128)(2,1)S(1)} %add_convert_fusion.9), channel_id=1, source_target_pairs={{8,0},{16,8},{24,16},{28,24},{20,28},{12,20},{4,12},{0,4},{9,1},{1... | collective-permute-start | bytes 405512 | tf_op jit(solution)/shard_map/ppermute | solution.py:695
  154.0 5.2 %collective-permute-start.15 = (bf16[66,1024]{1,0:T(8,128)(2,1)S(1)}, bf16[66,1024]{1,0:T(8,128)(2,1)S(1)}, u32[]{:S(2)}, u32[]{:S(2)}) collective-permute-start(bf16[66,1024]{1,0:T(8,128)(2,1)S(1)} %add_convert_fusion.7), channel_id=1, source_target_pairs={{0,8},{8,16},{16,24},{24,28},{28,20},{20,12},{12,4},{4,0},{1,9},{9... | collective-permute-start | bytes 405512 | tf_op jit(solution)/shard_map/ppermute | solution.py:694
  154.2 5.2 %collective-permute-start.22 = (bf16[66,1024]{1,0:T(8,128)(2,1)S(1)}, bf16[66,1024]{1,0:T(8,128)(2,1)S(1)}, u32[]{:S(2)}, u32[]{:S(2)}) collective-permute-start(bf16[66,1024]{1,0:T(8,128)(2,1)S(1)} %add_convert_fusion.2), channel_id=1, source_target_pairs={{8,0},{16,8},{24,16},{28,24},{20,28},{12,20},{4,12},{0,4},{9,1},{1... | collective-permute-start | bytes 405512 | tf_op jit(solution)/shard_map/ppermute | solution.py:694
  156.4 5.2 %collective-permute-start.19 = (bf16[66,1024]{1,0:T(8,128)(2,1)S(1)}, bf16[66,1024]{1,0:T(8,128)(2,1)S(1)}, u32[]{:S(2)}, u32[]{:S(2)}) collective-permute-start(bf16[66,1024]{1,0:T(8,128)(2,1)S(1)} %add_convert_fusion.4), channel_id=1, source_target_pairs={{0,8},{8,16},{16,24},{24,28},{28,20},{20,12},{12,4},{4,0},{1,9},{9... | collective-permute-start | bytes 405512 | tf_op jit(solution)/shard_map/ppermute | solution.py:695
  159.2 5.2 %collective-permute-start.16 = (bf16[66,1024]{1,0:T(8,128)(2,1)S(1)}, bf16[66,1024]{1,0:T(8,128)(2,1)S(1)}, u32[]{:S(2)}, u32[]{:S(2)}) collective-permute-start(bf16[66,1024]{1,0:T(8,128)(2,1)S(1)} %add_convert_fusion.6), channel_id=1, source_target_pairs={{0,8},{8,16},{16,24},{24,28},{28,20},{20,12},{12,4},{4,0},{1,9},{9... | collective-permute-start | bytes 405512 | tf_op jit(solution)/shard_map/ppermute | solution.py:695
  159.4 5.2 %collective-permute-start.23 = (bf16[66,1024]{1,0:T(8,128)(2,1)S(1)}, bf16[66,1024]{1,0:T(8,128)(2,1)S(1)}, u32[]{:S(2)}, u32[]{:S(2)}) collective-permute-start(bf16[66,1024]{1,0:T(8,128)(2,1)S(1)} %add_convert_fusion.1), channel_id=1, source_target_pairs={{8,0},{16,8},{24,16},{28,24},{20,28},{12,20},{4,12},{0,4},{9,1},{1... | collective-permute-start | bytes 405512 | tf_op jit(solution)/shard_map/ppermute | solution.py:695

commit v4 on v3

--- a/solution.py
+++ b/solution.py
@@ -27,10 +27,16 @@
     return lax.dot_general(left, right, (((1,), (1,)), ((), ())), preferred_element_type=F32)
 
 
-def cache_kernel(scal, pages, pool, flipped, values, raw, sems):
-    length = scal[0]
-    used = pl.cdiv(length, CHUNK)
-    per_chunk = CHUNK // PAGE
+def own_length(lengths, home, ids):
+    units = home.shape[0]
+    heads = units // lengths.shape[0]
+    length = lengths[0]
+    for unit in range(units):
+        length = jnp.where(home[unit] == ids[0], lengths[unit // heads], length)
+    return length
+
+
+def start_cache(length, pages, pool, raw, sems):
     last = pages.shape[0] - 1
 
     def page_copy(index):
@@ -39,11 +45,17 @@
             pool.at[page], raw.at[pl.ds(pl.multiple_of(index * PAGE, PAGE), PAGE), :], sems.at[index]
         )
 
-    @pl.loop(0, used * per_chunk)
+    @pl.loop(0, pl.cdiv(length, CHUNK) * (CHUNK // PAGE))
     def _(index):
         page_copy(index).start()
 
-    @pl.loop(0, used)
+    return page_copy
+
+
+def turn_cache(length, page_copy, raw, flipped, values):
+    per_chunk = CHUNK // PAGE
+
+    @pl.loop(0, pl.cdiv(length, CHUNK))
     def _(c):
         for k in range(per_chunk):
             page_copy(c * per_chunk + k).wait()
@@ -67,38 +79,19 @@
     return keys, jnp.where(side < HD, jnp.ones_like(both), both)
 
 
-def prepare_cache(length, pages, pool):
-    n_pages = pool.shape[0]
-    chunks = pl.cdiv(n_pages * PAGE, CHUNK)
-    return pl.pallas_call(
-        cache_kernel,
-        out_shape=[
-            jax.ShapeDtypeStruct((chunks, 2 * HD, CHUNK), BF16),
-            jax.ShapeDtypeStruct((chunks, CHUNK, 2 * HD), BF16),
-        ],
-        in_specs=[SMEM, SMEM, ANY],
-        out_specs=[VMEM, VMEM],
-        scratch_shapes=[
-            pltpu.VMEM((chunks * CHUNK, 2 * HD), BF16),
-            pltpu.SemaphoreType.DMA((chunks * (CHUNK // PAGE),)),
-        ],
-        compiler_params=pltpu.CompilerParams(vmem_limit_bytes=60 * 2**20),
-        cost_estimate=pl.CostEstimate(flops=2 * 10**9, bytes_accessed=6 * 2**20, transcendentals=0),
-    )(length, pages, pool)
-
-
 def prefill_kernel(
-    positions, scal, msg, flipped_in, values_in, decoded, out,
-    old_flipped, old_values, flipped, values, queries, scores, top, total, sems,
+    positions, lengths, home, ids, msg, flipped_in, values_in, decoded_in, out,
+    old_flipped, old_values, decoded, flipped, values, queries, scores, top, total, sems,
 ):
     blocks = msg.shape[0]
     stretch = blocks * positions
     half = positions // 2
-    used = pl.cdiv(scal[0], CHUNK)
+    used = pl.cdiv(own_length(lengths, home, ids), CHUNK)
     steps = stretch // CHUNK
     loads = [
         pltpu.make_async_copy(flipped_in, old_flipped, sems.at[0]),
         pltpu.make_async_copy(values_in, old_values, sems.at[1]),
+        pltpu.make_async_copy(decoded_in, decoded, sems.at[2]),
     ]
     for load in loads:
         load.start()
@@ -118,13 +111,6 @@
             keys, mixed = doubled(msg[c * (CHUNK // positions) + k, 0:positions, :])
             flipped[c, :, k * positions : (k + 1) * positions] = keys
             values[c, k * positions : (k + 1) * positions, :] = mixed
-    slots, features = decoded.shape
-    for k in range(0, features // 128, 2):
-        pair = jnp.concatenate([decoded[:, k * 128 : (k + 1) * 128], decoded[:, (k + 1) * 128 : (k + 2) * 128]], axis=0)
-        pair = pair.astype(BF16)
-        for b in range(blocks):
-            out[b, half + k * slots : half + (k + 2) * slots, :] = pair
-
     def raise_top(s):
         best = top[...]
         for k in range(CHUNK // 128):
@@ -165,6 +151,12 @@
     top[...] = jnp.full_like(top, -jnp.inf)
     for load in loads:
         load.wait()
+    slots, features = decoded.shape
+    for k in range(0, features // 128, 2):
+        pair = jnp.concatenate([decoded[:, k * 128 : (k + 1) * 128], decoded[:, (k + 1) * 128 : (k + 2) * 128]], axis=0)
+        pair = pair.astype(BF16)
+        for b in range(blocks):
+            out[b, half + k * slots : half + (k + 2) * slots, :] = pair
 
     @pl.loop(0, used)
     def _(c):
@@ -200,7 +192,7 @@
     emit(steps - 1)
 
 
-def prefill_attention(length, msg, old_flipped, old_values, decoded):
+def prefill_attention(lengths, home, ids, msg, old_flipped, old_values, decoded):
     blocks, rows, _ = msg.shape
     positions = rows * 2 // 3
     stretch = blocks * positions
@@ -211,30 +203,36 @@
     return pl.pallas_call(
         functools.partial(prefill_kernel, positions),
         out_shape=jax.ShapeDtypeStruct((blocks, positions // 2 + slots * features // 128, 2 * HD), BF16),
-        in_specs=[SMEM, VMEM, ANY, ANY, VMEM],
+        in_specs=[SMEM, SMEM, SMEM, VMEM, ANY, ANY, ANY],
         out_specs=VMEM,
         scratch_shapes=[
             pltpu.VMEM(old_flipped.shape, BF16),
             pltpu.VMEM(old_values.shape, BF16),
+            pltpu.VMEM(decoded.shape, F32),
             pltpu.VMEM((steps, 2 * HD, CHUNK), BF16),
             pltpu.VMEM((steps, CHUNK, 2 * HD), BF16),
             pltpu.VMEM((stretch, 2 * HD), BF16),
             pltpu.VMEM((chunks, CHUNK, CHUNK), F32),
             pltpu.VMEM((CHUNK, 128), F32),
             pltpu.VMEM((2, CHUNK, 128), F32),
-            pltpu.SemaphoreType.DMA((2,)),
+            pltpu.SemaphoreType.DMA((3,)),
         ],
-        compiler_params=pltpu.CompilerParams(vmem_limit_bytes=58 * 2**20),
+        compiler_params=pltpu.CompilerParams(vmem_limit_bytes=48 * 2**20),
         cost_estimate=pl.CostEstimate(flops=4 * stretch * keys * HD, bytes_accessed=4 * 2**20, transcendentals=stretch * keys),
-    )(length, msg, old_flipped, old_values, decoded)
-
-
-def decode_kernel(heads, scal, pages, x, gain, w, pool, out, buf, wbuf, normed, qrows, cacherows, rowout, bests, totals, mixes, owners, wsems, sems):
+    )(lengths, home, ids, msg, old_flipped, old_values, decoded)
+
+
+def decode_kernel(
+    heads, lengths, home, ids, pages, old_lengths, old_home, old_pages, x, gain, w, pool, old_pool,
+    out, flipped, values_in, raw, old_sems, buf, wbuf, normed, qrows, cacherows, rowout, bests, totals, mixes, owners, anchors, wsems, sems,
+):
     slots = pages.shape[0]
     width = heads * 2 * HD
     per_group = BLOCK // PAGE
     depth = pages.shape[1]
     most = buf.shape[0] // BLOCK
+    old_length = own_length(old_lengths, old_home, ids)
+    old_copy = start_cache(old_length, old_pages, old_pool, raw, old_sems)
     w_copies = [pltpu.make_async_copy(w.at[j], wbuf.at[j], wsems.at[j]) for j in range(3)]
     for copy in w_copies:
         copy.start()
@@ -247,7 +245,12 @@
         )
 
     def groups(s):
-        return pl.cdiv(scal[s], BLOCK)
+        return pl.cdiv(lengths[s], BLOCK)
+
+    @pl.loop(0, home.shape[0])
+    def _(request):
+        s = home[request] - ids[0] * slots
+        anchors[jnp.where((s >= 0) & (s < slots), s, slots)] = request
 
     @pl.loop(0, most + UNROLL)
     def _(item):
@@ -259,7 +262,7 @@
         @pl.loop(0, groups(s))
         def _(g):
             owners[0, start + g] = s
-            owners[1, start + g] = scal[s] - g * BLOCK
+            owners[1, start + g] = lengths[s] - g * BLOCK
             owners[2, start + g] = g
 
         return start + groups(s)
@@ -274,6 +277,7 @@
 
     for item in range(AHEAD):
         fetch(item)
+    turn_cache(old_length, old_copy, raw, flipped, values_in)
     values = x[...].astype(F32)
     inverse = lax.rsqrt(jnp.mean(values * values, axis=-1, keepdims=True) + EPSILON)
     normed[...] = (values * inverse * gain[...]).astype(BF16)
@@ -292,7 +296,7 @@
     diagonal = owner == lax.broadcasted_iota(jnp.int32, (8, width), 0)
 
     def spread(s):
-        row = scal[slots + s]
+        row = anchors[s]
         return jnp.where(diagonal, jnp.broadcast_to(qrows[pl.ds(row, 1), :], (8, width)), 0.0)
 
     @pl.loop(0, pl.cdiv(items, UNROLL))
@@ -320,7 +324,7 @@
     most_items = pl.cdiv(depth * PAGE, BLOCK)
     start = 0
     for s in range(slots):
-        own = jnp.broadcast_to(cacherows[pl.ds(scal[slots + s], 1), :], (8, width))
+        own = jnp.broadcast_to(cacherows[pl.ds(anchors[s], 1), :], (8, width))
         own_score = jnp.sum(spread(s) * own, axis=1, keepdims=True)
         count = groups(s)
         held = [jnp.where(i < count, bests[start + i], -jnp.inf) for i in range(most_items)]
@@ -342,7 +346,7 @@
         )
 
 
-def decode_attention(scal, pages, x, gain, w, pool):
+def decode_attention(lengths, home, ids, pages, old_lengths, old_home, old_pages, x, gain, w, pool, old_pool):
     slots = pages.shape[0]
     features = w.shape[2]
     heads = features // HD
@@ -350,13 +354,21 @@
     rows = x.shape[0]
     per_group = BLOCK // PAGE
     most = pl.cdiv(pool.shape[0] + slots * (per_group - 1), per_group)
+    chunks = pl.cdiv(old_pool.shape[0] * PAGE, CHUNK)
+    flipped, values = (chunks, 2 * HD, CHUNK), (chunks, CHUNK, 2 * HD)
     spare = max(UNROLL, pl.cdiv(pages.shape[1], per_group))
     return pl.pallas_call(
         functools.partial(decode_kernel, heads),
-        out_shape=jax.ShapeDtypeStruct((slots, features), F32),
-        in_specs=[SMEM, SMEM, VMEM, VMEM, ANY, ANY],
-        out_specs=VMEM,
+        out_shape=[
+            jax.ShapeDtypeStruct((slots, features), F32),
+            jax.ShapeDtypeStruct(flipped, BF16),
+            jax.ShapeDtypeStruct(values, BF16),
+        ],
+        in_specs=[SMEM] * 7 + [VMEM, VMEM, ANY, ANY, ANY],
+        out_specs=[VMEM, VMEM, VMEM],
         scratch_shapes=[
+            pltpu.VMEM((chunks * CHUNK, 2 * HD), BF16),
+            pltpu.SemaphoreType.DMA((chunks * (CHUNK // PAGE),)),
             pltpu.VMEM((most * BLOCK, width), BF16),
             pltpu.VMEM(w.shape, BF16),
             pltpu.VMEM(x.shape, BF16),
@@ -367,12 +379,13 @@
             pltpu.VMEM((most + spare, 8, 128), F32),
             pltpu.VMEM((most + spare, 8, width), F32),
             pltpu.SMEM((3, most + UNROLL), jnp.int32),
+            pltpu.SMEM((slots + 1,), jnp.int32),
             pltpu.SemaphoreType.DMA((3,)),
             pltpu.SemaphoreType.DMA((most * per_group,)),
         ],
-        compiler_params=pltpu.CompilerParams(vmem_limit_bytes=56 * 2**20),
+        compiler_params=pltpu.CompilerParams(vmem_limit_bytes=52 * 2**20),
         cost_estimate=pl.CostEstimate(flops=2 * 10**9, bytes_accessed=22 * 2**20, transcendentals=10**6),
-    )(scal, pages, x, gain, w, pool)
+    )(lengths, home, ids, pages, old_lengths, old_home, old_pages, x, gain, w, pool, old_pool)
 
 
 def qkv_kernel(requests, heads, home, gain, x, w, out, xbuf, wbuf, normed, sems):
@@ -429,13 +442,12 @@
     )(home, gain, x, w)
 
 
-def project_kernel(requests, heads, scal, received, w_out, *rest):
-    outs, (rows_in, decode_in, weights, sem) = rest[:-4], rest[-4:]
+def project_kernel(requests, heads, home, slots_of, ids, received, w_out, *rest):
+    outs, (rows_in, decode_in, weights, products, sem) = rest[:-5], rest[-5:]
     fetch = pltpu.make_async_copy(w_out, weights, sem)
     fetch.start()
     n_head = len(outs)
     n_tok = received.shape[0]
-    units = requests * heads
     per = outs[0].shape[0]
     features = w_out.shape[0]
     slots = decode_in.shape[0] // n_tok
@@ -454,8 +466,8 @@
     rows_in[...] = jnp.zeros_like(rows_in)
     for r in range(requests):
         for g in range(0, heads, 2):
-            left = received[scal[r * heads + g], 0:half, :].astype(F32)
-            right = received[scal[r * heads + g + 1], 0:half, :].astype(F32)
+            left = received[home[r * heads + g], 0:half, :].astype(F32)
+            right = received[home[r * heads + g + 1], 0:half, :].astype(F32)
             both = jnp.concatenate(
                 [
                     jnp.concatenate([left[:, :HD], right[:, :HD]], axis=1),
@@ -468,15 +480,16 @@
                     h * block_rows : (h + 1) * block_rows
                 ]
     for j in range(hosted):
-        rows_in[j // share, requests * block_rows + j % share, :] = decode_in[pl.ds(scal[units + j], 1), :][0]
+        rows_in[j // share, requests * block_rows + j % share, :] = decode_in[pl.ds(slots_of[ids[0] * hosted + j], 1), :][0]
     fetch.wait()
+    padded = rows_in.shape[1]
+    everyone = rows_in[...].reshape(n_head * padded, features).astype(BF16)
+    products[...] = jnp.dot(everyone, weights[...], preferred_element_type=F32).astype(BF16).reshape(products.shape)
     for k in range(n_head):
-        mine = rows_in[scal[units + hosted + k]].astype(BF16)
-        y = jnp.dot(mine, weights[...], preferred_element_type=F32).astype(BF16)
-        outs[k][...] = y[:per]
-
-
-def project_out(scal, received, w_out, requests, heads, n_head, hosted):
+        outs[k][...] = products[ids[1] ^ k, 0:per, :]
+
+
+def project_out(home, slots_of, ids, received, w_out, requests, heads, n_head, hosted):
     features, width = w_out.shape
     positions = 2 * (received.shape[1] - hosted * features // 128)
     per = requests * (positions // n_head) + hosted // n_head
@@ -484,21 +497,23 @@
     return pl.pallas_call(
         functools.partial(project_kernel, requests, heads),
         out_shape=[jax.ShapeDtypeStruct((per, width), BF16)] * n_head,
-        in_specs=[SMEM, VMEM, ANY],
+        in_specs=[SMEM, SMEM, SMEM, VMEM, ANY],
         out_specs=[VMEM] * n_head,
         scratch_shapes=[
             pltpu.VMEM((n_head, padded, features), F32),
             pltpu.VMEM((received.shape[0] * hosted, features), F32),
             pltpu.VMEM(w_out.shape, BF16),
+            pltpu.VMEM((n_head, padded, width), BF16),
             pltpu.SemaphoreType.DMA,
         ],
-        compiler_params=pltpu.CompilerParams(vmem_limit_bytes=56 * 2**20),
+        compiler_params=pltpu.CompilerParams(vmem_limit_bytes=24 * 2**20),
         cost_estimate=pl.CostEstimate(flops=2 * n_head * per * features * width, bytes_accessed=4 * 2**20, transcendentals=0),
-    )(scal, received, w_out)
+    )(home, slots_of, ids, received, w_out)
 
 
 def middle_kernel(own_pre, own_dec, gain, *rest):
-    terms, (resid, normed) = rest[:-2], rest[-2:]
+    terms, (resid, normed_left, normed_right) = rest[:-3], rest[-3:]
+    middle = normed_left.shape[1]
     split = own_pre.shape[0]
     for rows, own in ((slice(0, split), own_pre), (slice(split, resid.shape[0]), own_dec)):
         values = own[...].astype(F32)
@@ -506,16 +521,18 @@
             values = values + term[rows, :].astype(F32)
         resid[rows, :] = values
         inverse = lax.rsqrt(jnp.mean(values * values, axis=-1, keepdims=True) + EPSILON)
-        normed[rows, :] = (values * inverse * gain[...]).astype(BF16)
+        normed = (values * inverse * gain[...]).astype(BF16)
+        normed_left[rows, :] = normed[:, :middle]
+        normed_right[rows, :] = normed[:, middle:]
 
 
 def middle(own_pre, own_dec, gain, terms):
     shape = terms[0].shape
     return pl.pallas_call(
         middle_kernel,
-        out_shape=[jax.ShapeDtypeStruct(shape, F32), jax.ShapeDtypeStruct(shape, BF16)],
+        out_shape=[jax.ShapeDtypeStruct(shape, F32)] + [jax.ShapeDtypeStruct((shape[0], shape[1] // 2), BF16)] * 2,
         in_specs=[VMEM] * (3 + len(terms)),
-        out_specs=[VMEM] * 2,
+        out_specs=[VMEM] * 3,
         compiler_params=pltpu.CompilerParams(vmem_limit_bytes=16 * 2**20),
         cost_estimate=pl.CostEstimate(flops=10**6, bytes_accessed=2 * 2**20, transcendentals=0),
     )(own_pre, own_dec, gain, *terms)
@@ -548,47 +565,58 @@
     )(resid, *own, *sums)
 
 
-def feed_kernel(count, *refs):
-    rows, (gate_up, down), outs = refs[:count], refs[count : count + 2], refs[count + 2 :]
+def feed_kernel(shape, *refs):
+    count, pieces = len(shape), sum(shape)
+    parts, (gate_up, down), outs = list(refs[:pieces]), refs[pieces : pieces + 2], refs[pieces + 2 :]
+    outs, rows = outs[:-1], outs[-1]
+    per = outs[0].shape[0]
+    padded = rows.shape[0] // count
+    for index, size in enumerate(shape):
+        first = 0
+        for _ in range(size):
+            part = parts.pop(0)
+            rows[index * padded : index * padded + per, first : first + part.shape[1]] = part[...]
+            first += part.shape[1]
     middle = down.shape[1] // 2
     hidden_units = down.shape[0]
     tile = 128 if hidden_units % 128 == 0 else hidden_units
     steps = hidden_units // tile
 
-    hidden = [[] for _ in range(count)]
+    hidden = []
     for step in range(steps):
         cols = slice(step * tile, (step + 1) * tile)
-        both = jnp.concatenate([gate_up[0, :, cols], gate_up[1, :, cols]], axis=1) if tile == 128 else None
+        if tile == 128:
+            both = jnp.concatenate([gate_up[0, :, cols], gate_up[1, :, cols]], axis=1)
+            y = jnp.dot(rows[...], both, preferred_element_type=F32)
+            gate, upper = y[:, :tile], y[:, tile:]
+        else:
+            gate = jnp.dot(rows[...], gate_up[0], preferred_element_type=F32)
+            upper = jnp.dot(rows[...], gate_up[1], preferred_element_type=F32)
+        hidden.append((jax.nn.gelu(gate, approximate=True) * upper).astype(BF16))
+    full = jnp.concatenate(hidden, axis=1)
+    for side in range(2):
+        cols = slice(side * middle, (side + 1) * middle)
+        y = jnp.dot(full, down[:, cols], preferred_element_type=F32).astype(BF16)
         for index in range(count):
-            if tile == 128:
-                y = jnp.dot(rows[index][...], both, preferred_element_type=F32)
-                gate, upper = y[:, :tile], y[:, tile:]
-            else:
-                gate = jnp.dot(rows[index][...], gate_up[0], preferred_element_type=F32)
-                upper = jnp.dot(rows[index][...], gate_up[1], preferred_element_type=F32)
-            hidden[index].append((jax.nn.gelu(gate, approximate=True) * upper).astype(BF16))
-    for index in range(count):
-        full = jnp.concatenate(hidden[index], axis=1)
-        for side in range(2):
-            cols = slice(side * middle, (side + 1) * middle)
-            y = jnp.dot(full, down[:, cols], preferred_element_type=F32)
-            outs[2 * index + side][...] = y.astype(BF16)
+            outs[2 * index + side][...] = y[index * padded : index * padded + per]
 
 
 def feed_forward(chunks, gate_up, down):
     count = len(chunks)
-    per, width = chunks[0].shape
+    pieces = [piece for chunk in chunks for piece in chunk]
+    per, width = pieces[0].shape[0], down.shape[1]
     hidden_units = down.shape[0]
     return pl.pallas_call(
-        functools.partial(feed_kernel, count),
+        functools.partial(feed_kernel, [len(chunk) for chunk in chunks]),
         out_shape=[jax.ShapeDtypeStruct((per, width // 2), BF16)] * (2 * count),
-        in_specs=[VMEM] * (count + 2),
+        in_specs=[VMEM] * (len(pieces) + 2),
         out_specs=[VMEM] * (2 * count),
+        scratch_shapes=[pltpu.VMEM((count * (-(-per // 16) * 16), width), BF16)],
         compiler_params=pltpu.CompilerParams(vmem_limit_bytes=24 * 2**20),
         cost_estimate=pl.CostEstimate(
             flops=6 * count * per * width * hidden_units, bytes_accessed=8 * 2**20, transcendentals=count * per * hidden_units
         ),
-    )(*chunks, gate_up, down)
+    )(*pieces, gate_up, down)
 
 
 def ring_of(n_tok):
@@ -635,32 +663,21 @@
 
     gain = attn_gain.reshape(1, width)
     w_three = jnp.transpose(w_qkv, (1, 0, 2))
-    unit_ids = jnp.arange(units, dtype=jnp.int32)
-    my_unit = jnp.sum(jnp.where(prefill_home == my_tok, unit_ids, 0))
-    length = lax.dynamic_slice_in_dim(prefill_lengths, my_unit // heads, 1, 0)
-    slots = my_tok * hosted + jnp.arange(hosted, dtype=jnp.int32)
-    all_requests = jnp.arange(decode_home.shape[0], dtype=jnp.int32)
-    anchor = jnp.sum(jnp.where(decode_home[None, :] == slots[:, None], all_requests[None, :], 0), axis=1)
-
+    ids = jnp.stack([my_tok, my_head]).astype(jnp.int32)
     copies = jnp.broadcast_to(decode_states[None], (n_tok, hosted, width))
     rows = lax.all_to_all(copies, "tok", split_axis=0, concat_axis=0, tiled=True).reshape(n_tok * hosted, width)
     messages = qkv_messages(prefill_home, prefill_states.reshape(requests * positions, width), gain, w_three, requests)
     messages, rows = lax.optimization_barrier((messages, rows))
     arrived = lax.all_to_all(messages, "tok", split_axis=0, concat_axis=0, tiled=True)
-    decoded = decode_attention(
-        jnp.concatenate([decode_lengths, anchor]), decode_pages, rows, gain, w_three, decode_pool
+    decoded, old_keys, old_values = decode_attention(
+        decode_lengths, decode_home, ids, decode_pages, prefill_lengths, prefill_home, prefill_pages.reshape(-1),
+        rows, gain, w_three, decode_pool, prefill_pool,
     )
-    table, decoded = lax.optimization_barrier((prefill_pages.reshape(-1), decoded))
-    old_keys, old_values = prepare_cache(length, table, prefill_pool)
-    attn = prefill_attention(length, arrived, old_keys, old_values, decoded)
+    attn = prefill_attention(prefill_lengths, prefill_home, ids, arrived, old_keys, old_values, decoded)
     returned = lax.all_to_all(attn, "tok", split_axis=0, concat_axis=0, tiled=True)
     gate_up = jnp.transpose(w_gate_up, (1, 0, 2))
 
-    my_slots = lax.dynamic_slice_in_dim(decode_home, my_tok * hosted, hosted, 0)
-    targets = my_head ^ jnp.arange(n_head, dtype=jnp.int32)
-    parts = project_out(
-        jnp.concatenate([prefill_home, my_slots, targets]), returned, w_out, requests, heads, n_head, hosted
-    )
+    parts = project_out(prefill_home, decode_home, ids, returned, w_out, requests, heads, n_head, hosted)
     block_rows = positions // n_head
     share = hosted // n_head
     own_pre = lax.dynamic_slice_in_dim(prefill_states, my_head * block_rows, block_rows, 1)
@@ -671,23 +688,26 @@
         both = joined(parts[k], lax.ppermute(parts[k + 1], "head", swap))
         terms.append(lax.ppermute(both, "head", [(i, i ^ k) for i in range(n_head)]))
     terms.append(lax.ppermute(parts[1], "head", swap))
-    resid, normed_mid = middle(own_pre.reshape(requests * block_rows, width), own_dec, ffn_gain.reshape(1, width), terms)
+    terms[1], gate_up = lax.optimization_barrier((terms[1], gate_up))
+    resid, left, right = middle(own_pre.reshape(requests * block_rows, width), own_dec, ffn_gain.reshape(1, width), terms)
 
     plus, minus = {}, {}
-    up, down = normed_mid, normed_mid
-    waiting = [normed_mid]
+    up_left, up_right, down_left, down_right = left, right, left, right
+    waiting = None
     for k in range(1, far + 1):
-        up = lax.ppermute(up, "tok", ahead)
+        up_left = lax.ppermute(up_left, "tok", ahead)
+        down_right = lax.ppermute(down_right, "tok", behind)
         if k <= near:
-            down = lax.ppermute(down, "tok", behind)
-        done = feed_forward(waiting, gate_up, w_down)
-        up, down, done = lax.optimization_barrier((up, down, done))
-        if k == 1:
-            own_part = done
-        else:
+            down_left = lax.ppermute(down_left, "tok", behind)
+            up_right = lax.ppermute(up_right, "tok", ahead)
+        if waiting is not None:
+            done = feed_forward(waiting, gate_up, w_down)
+            up_left, down_right, done = lax.optimization_barrier((up_left, down_right, done))
             minus[k - 1], plus[k - 1] = done[:2], done[2:]
-        waiting = [up, down]
-    farthest = feed_forward([up], gate_up, w_down)
+        waiting = [(up_left, up_right), (down_left, down_right)]
+    farthest = feed_forward([(up_left, down_right)], gate_up, w_down)
+    left, right, farthest = lax.optimization_barrier((left, right, farthest))
+    own_part = feed_forward([(left, right)], gate_up, w_down)
 
     def chain(part, table, side, hops, steps):
         for k in range(hops, 0, -1):

time: 166 us -> 157 us (0.946)
  blocking collectives: 0 us -> 15.5 us
  waiting for transfers between devices: 39.9 us -> 25 us
  Pallas kernels: 71.2 us -> 59.6 us
  local copies, waits for them, and re-layouts: 9.02 us -> 12.8 us
    all_to_all x0 -> x1, blocking collectives: none -> 15.5 us  [shards(): lax.all_to_all(attn, 'tok', split_axis=0, concat_axis=0, tiled=True)]
    all_to_all x1 -> x0, waiting for transfers between devices: 8.72 us -> none  [shards(): lax.all_to_all(attn, 'tok', split_axis=0, concat_axis=0, tiled=True)]
    pallas_call x7 -> x6, Pallas kernels: 34.7 us -> 27.3 us  [the longest x1 18.4 us: decode_attention(): pl.pallas_call(functools.partial(decode_kernel, heads), out_shape=[jax.Sh...]
    ppermute x7 -> x14, starting transfers between devices: 7.36 us -> 14.3 us  [the longest x4 4.59 us: shards(): down_right = lax.ppermute(down_right, 'tok', behind)]
    all_to_all x1 -> x0, starting transfers between devices: 5.95 us -> none  [shards(): lax.all_to_all(attn, 'tok', split_axis=0, concat_axis=0, tiled=True)]
    ppermute x1, waiting for transfers between devices: 5.8 us -> 0.42 us  [shards(): lax.ppermute(both, 'head', [(i, i ^ k) for i in range(n_head)])]
    unnamed x19 -> x27, local copies, waits for them, and re-layouts: 5.73 us -> 9.59 us
    pallas_call x1, Pallas kernels: 4.91 us -> 2.49 us  [project_out(): pl.pallas_call(functools.partial(project_kernel, requests, heads), out_sh...]
  transfers between devices with their start and end apart: 27 -> 33, of which waited for: 20 -> 15; matrix products, arithmetic and copies ran while one was open for 5% -> 5% of each run, Pallas kernels for 25% -> 20%
where the time goes in v4:
time: 157 us
  Pallas kernels  59.6 us (38%)
  starting transfers between devices  41.2 us (26%)
  waiting for transfers between devices  25 us (16%)
  blocking collectives  15.5 us (10%)
  local copies, waits for them, and re-layouts  12.8 us (8%)
  between operations  1.57 us (1%)
    pallas_call x1, Pallas kernels, prefill_attention(): pl.pallas_call(functools.partial(prefill_kernel, positions), out_shape=ja...  22.6 us
    pallas_call x1, Pallas kernels, decode_attention(): pl.pallas_call(functools.partial(decode_kernel, heads), out_shape=[jax.Sh...  18.4 us
    all_to_all x1, blocking collectives, shards(): lax.all_to_all(attn, 'tok', split_axis=0, concat_axis=0, tiled=True)  15.5 us
    ppermute x10, starting transfers between devices, chain(): part = joined(table[k][side], lax.ppermute(part, 'tok', steps))  10.2 us
    unnamed x27, local copies, waits for them, and re-layouts  9.59 us
    pallas_call x5, Pallas kernels, feed_forward(): pl.pallas_call(functools.partial(feed_kernel, [len(chunk) for chunk in ch...  8.93 us
    ppermute x10, waiting for transfers between devices, chain(): part = joined(table[k][side], lax.ppermute(part, 'tok', steps))  8.42 us
    all_to_all x1, starting transfers between devices, shards(): lax.all_to_all(copies, 'tok', split_axis=0, concat_axis=0, tiled=True)  7.28 us
  transfers between devices with their start and end apart: 33, of which 15 were waited for; matrix products, arithmetic and copies ran while one was open for 5% of the time, Pallas kernels for 20%

profile of v4, /device:TPU:0, one launch (start us, length us, event | category | flops | bytes accessed | tf_op | source)
XLA Modules:
  0.0 156.9 jit_solution(6274318888556667722)
XLA Ops:
  0.6 1.5 broadcast_in_dim.2
  2.1 7.3 %all-to-all-start = ((bf16[8,8,2048]{2,1,0:T(8,128)(2,1)}), bf16[8,8,2048]{2,1,0:T(8,128)(2,1)S(1)}, u32[]{:S(2)}, u32[]{:S(2)}) async-start(bf16[8,8,2048]{2,1,0:T(8,128)(2,1)} %broadcast_in_dim.2), calls=%async_computation | async-start | bytes 524288 | tf_op jit(solution)/shard_map/all_to_all | solution.py:668
  9.5 6.0 %shard_map.167 = bf16[8,384,128]{2,1,0:T(8,128)(2,1)} custom-call(s32[8]{0:T(128)} %home.7, f32[1,2048]{1,0:T(1,128)} %bitcast.22, bf16[256,2048]{1,0:T(8,128)(2,1)} %bitcast.28, bf16[3,2048,512]{2,1,0:T(8,128)(2,1)} %bitcast.26), custom_call_target="tpu_custom_call" | custom-call | flops 1610612736 | bytes 10485760 | tf_op jit(solution)/shard_map/pallas_call | solution.py:429
  15.5 2.9 %all-to-all-done = bf16[8,8,2048]{2,1,0:T(8,128)(2,1)S(1)} async-done(((bf16[8,8,2048]{2,1,0:T(8,128)(2,1)}), bf16[8,8,2048]{2,1,0:T(8,128)(2,1)S(1)}, u32[]{:S(2)}, u32[]{:S(2)}) %all-to-all-start) | async-done | bytes 262176 | tf_op jit(solution)/shard_map/all_to_all | solution.py:668
  18.3 3.6 %all-to-all-start.1 = ((bf16[8,384,128]{2,1,0:T(8,128)(2,1)}), bf16[8,384,128]{2,1,0:T(8,128)(2,1)S(1)}, u32[]{:S(2)}, u32[]{:S(2)}) async-start(bf16[8,384,128]{2,1,0:T(8,128)(2,1)} %shard_map.167), calls=%async_computation.1 | async-start | bytes 1572864 | tf_op jit(solution)/shard_map/all_to_all | solution.py:671
  22.7 18.4 %shard_map.168 = (f32[8,512]{1,0:T(8,128)S(1)}, bf16[6,128,1024]{2,1,0:T(8,128)(2,1)S(1)}, bf16[6,1024,128]{2,1,0:T(8,128)(2,1)}) custom-call(s32[8]{0:T(128)S(1)} %copy-done.8, s32[64]{0:T(128)S(1)} %copy-done.7, s32[2]{0:T(128)S(1)} %pad_add_fusion.ids, s32[8,32]{1,0:T(8,128)S(1)} %copy-done.6, s32[1]{0:T(128)S(6)} %copy.21.old_lengths.lengths, ...), custom_call_target="tpu_custom_call" | custom-call | flops 2000000000 | bytes 23068672 | tf_op jit(solution)/shard_map/pallas_call | solution.py:360
  41.8 1.4 copy-done.10
  43.2 22.6 %shard_map.169 = bf16[8,160,128]{2,1,0:T(8,128)(2,1)S(1)} custom-call(s32[1]{0:T(128)S(6)} %copy.21.old_lengths.lengths, s32[8]{0:T(128)S(1)} %copy-done.5, s32[2]{0:T(128)S(1)} %pad_add_fusion.ids, bf16[8,384,128]{2,1,0:T(8,128)(2,1)S(1)} %all-to-all-done.1.msg, bf16[6,128,1024]{2,1,0:T(8,128)(2,1)S(1)} %get-tuple-element.58.flipped_in, ...), custom_call_target="tpu_custom_call" | custom-call | flops 4294967296 | bytes 4194304 | tf_op jit(solution)/shard_map/pallas_call | solution.py:203
  65.9 15.5 %all_to_all.15.received = bf16[8,160,128]{2,1,0:T(8,128)(2,1)S(1)} all-to-all(bf16[8,160,128]{2,1,0:T(8,128)(2,1)S(1)} %shard_map.169), channel_id=1, replica_groups=mesh['tok'=8,'head'=4] {'tok'}, dimensions={0} | all-to-all | bytes 655360 | tf_op jit(solution)/shard_map/all_to_all | solution.py:677
  81.4 2.5 %shard_map.170 = (bf16[66,2048]{1,0:T(8,128)(2,1)S(1)}, bf16[66,2048]{1,0:T(8,128)(2,1)}, bf16[66,2048]{1,0:T(8,128)(2,1)S(1)}, bf16[66,2048]{1,0:T(8,128)(2,1)S(1)}) custom-call(s32[8]{0:T(128)S(1)} %copy-done.5, s32[64]{0:T(128)S(1)} %copy-done.7, s32[2]{0:T(128)S(1)} %pad_add_fusion.ids, bf16[8,160,128]{2,1,0:T(8,128)(2,1)S(1)} %all_to_all.15.received, ...), custom_call_target="tpu_custom_call" | custom-call | flops 553648128 | bytes 4194304 | tf_op jit(solution)/shard_map/pallas_call | solution.py:497
  84.4 1.1 collective-permute-done
  86.3 1.4 collective-permute-start.1
  88.5 5.6 %copy.20 = bf16[2048,2,640]{2,0,1:T(8,128)(2,1)} copy(bf16[2048,2,640]{2,1,0:T(2,128)(2,1)} %param.22) | data formatting | bytes 10485760 | tf_op args[6]
  94.2 1.0 dynamic-slice_bitcast_fusion.own_pre
  96.6 1.3 collective-permute-start.5
  98.7 1.3 collective-permute-start.8
  100.0 2.7 %collective-permute-done.3.refs_0_ = bf16[66,1024]{1,0:T(8,128)(2,1)S(1)} collective-permute-done((bf16[66,1024]{1,0:T(8,128)(2,1)S(1)}, bf16[66,1024]{1,0:T(8,128)(2,1)S(1)}, u32[]{:S(2)}, u32[]{:S(2)}) %collective-permute-start.3) | collective-permute-done | bytes 135200 | tf_op jit(solution)/shard_map/ppermute | solution.py:698
  103.4 1.3 collective-permute-start.6
  104.7 1.1 collective-permute-done.7.refs_1_
  106.6 1.3 collective-permute-start.12
  107.9 2.5 %copy-done = bf16[2048,2,640]{2,0,1:T(8,128)(2,1)S(1)} copy-done((bf16[2048,2,640]{2,0,1:T(8,128)(2,1)S(1)}, bf16[2048,2,640]{2,0,1:T(8,128)(2,1)}, u32[]{:S(2)}) %copy-start) | copy-done | bytes 5242904
  110.4 1.8 %shard_map.172 = (bf16[66,1024]{1,0:T(8,128)(2,1)S(1)}, bf16[66,1024]{1,0:T(8,128)(2,1)S(1)}, bf16[66,1024]{1,0:T(8,128)(2,1)S(1)}, bf16[66,1024]{1,0:T(8,128)(2,1)S(1)}) custom-call(bf16[66,1024]{1,0:T(8,128)(2,1)S(1)} %collective-permute-done.3.refs_0_, bf16[66,1024]{1,0:T(8,128)(2,1)S(1)} %collective-permute-done.7.refs_1_, ...), custom_call_target="tpu_custom_call" | custom-call | flops 1038090240 | bytes 8388608 | tf_op jit(solution)/shard_map/pallas_call | solution.py:609
  112.2 0.9 collective-permute-start.10
  113.1 1.2 collective-permute-start.9
  115.0 1.3 collective-permute-start.16
  116.3 1.8 %shard_map.173 = (bf16[66,1024]{1,0:T(8,128)(2,1)S(1)}, bf16[66,1024]{1,0:T(8,128)(2,1)S(1)}, bf16[66,1024]{1,0:T(8,128)(2,1)S(1)}, bf16[66,1024]{1,0:T(8,128)(2,1)S(1)}) custom-call(bf16[66,1024]{1,0:T(8,128)(2,1)S(1)} %collective-permute-done.4.refs_0_, bf16[66,1024]{1,0:T(8,128)(2,1)S(1)} %collective-permute-done.11.refs_1_, ...), custom_call_target="tpu_custom_call" | custom-call | flops 1038090240 | bytes 8388608 | tf_op jit(solution)/shard_map/pallas_call | solution.py:609
  118.2 1.1 collective-permute-done.9.refs_0_
  119.3 0.9 collective-permute-start.13
  120.2 1.1 collective-permute-start.14
  121.3 1.8 %shard_map.174 = (bf16[66,1024]{1,0:T(8,128)(2,1)S(1)}, bf16[66,1024]{1,0:T(8,128)(2,1)S(1)}, bf16[66,1024]{1,0:T(8,128)(2,1)S(1)}, bf16[66,1024]{1,0:T(8,128)(2,1)S(1)}) custom-call(bf16[66,1024]{1,0:T(8,128)(2,1)S(1)} %collective-permute-done.9.refs_0_, bf16[66,1024]{1,0:T(8,128)(2,1)S(1)} %collective-permute-done.15.refs_1_, ...), custom_call_target="tpu_custom_call" | custom-call | flops 1038090240 | bytes 8388608 | tf_op jit(solution)/shard_map/pallas_call | solution.py:609
  123.2 1.3 collective-permute-done.13.refs_0_
  124.4 2.4 %collective-permute-done.14.refs_1_ = bf16[66,1024]{1,0:T(8,128)(2,1)S(1)} collective-permute-done((bf16[66,1024]{1,0:T(8,128)(2,1)S(1)}, bf16[66,1024]{1,0:T(8,128)(2,1)S(1)}, u32[]{:S(2)}, u32[]{:S(2)}) %collective-permute-start.14) | collective-permute-done | bytes 135200 | tf_op jit(solution)/shard_map/ppermute | solution.py:699
  126.9 1.7 %shard_map.175 = (bf16[66,1024]{1,0:T(8,128)(2,1)S(1)}, bf16[66,1024]{1,0:T(8,128)(2,1)S(1)}) custom-call(bf16[66,1024]{1,0:T(8,128)(2,1)S(1)} %collective-permute-done.13.refs_0_, bf16[66,1024]{1,0:T(8,128)(2,1)S(1)} %collective-permute-done.14.refs_1_, bf16[2,2048,640]{2,1,0:T(8,128)(2,1)S(1)} %bitcast.17, bf16[640,2048]{1,0:T(8,128)(2,1)S(1)} %copy-done.1), custom_call_target="tpu_custom_call" | custom-call | flops 519045120 | bytes 8388608 | tf_op jit(solution)/shard_map/pallas_call | solution.py:609
  128.6 1.2 collective-permute-start.27
  129.8 0.8 collective-permute-start.24
  131.2 1.5 collective-permute-start.17
  132.7 2.6 %collective-permute-done.27 = bf16[66,1024]{1,0:T(8,128)(2,1)S(1)} collective-permute-done((bf16[66,1024]{1,0:T(8,128)(2,1)S(1)}, bf16[66,1024]{1,0:T(8,128)(2,1)S(1)}, u32[]{:S(2)}, u32[]{:S(2)}) %collective-permute-start.27) | collective-permute-done | bytes 135200 | tf_op jit(solution)/shard_map/ppermute | solution.py:714
  135.3 1.3 collective-permute-start.28
  137.5 1.3 collective-permute-done.20
  138.9 0.9 collective-permute-start.21
  139.8 1.2 collective-permute-start.18
  141.1 0.9 collective-permute-done.28
  142.0 1.3 collective-permute-start.29
  144.1 1.5 collective-permute-done.21
  146.3 1.6 collective-permute-start.19
  148.8 2.1 %collective-permute-done.22 = bf16[66,1024]{1,0:T(8,128)(2,1)S(1)} collective-permute-done((bf16[66,1024]{1,0:T(8,128)(2,1)S(1)}, bf16[66,1024]{1,0:T(8,128)(2,1)S(1)}, u32[]{:S(2)}, u32[]{:S(2)}) %collective-permute-start.22) | collective-permute-done | bytes 135200 | tf_op jit(solution)/shard_map/ppermute | solution.py:714
  151.5 1.7 %shard_map.176 = (bf16[66,1024]{1,0:T(8,128)(2,1)S(1)}, bf16[66,1024]{1,0:T(8,128)(2,1)S(1)}) custom-call(bf16[66,1024]{1,0:T(8,128)(2,1)S(1)} %get-tuple-element.90.refs_0_, bf16[66,1024]{1,0:T(8,128)(2,1)S(1)} %get-tuple-element.91.refs_1_, bf16[2,2048,640]{2,1,0:T(8,128)(2,1)S(1)} %bitcast.20, bf16[640,2048]{1,0:T(8,128)(2,1)S(1)} %copy-done.1), custom_call_target="tpu_custom_call" | custom-call | flops 519045120 | bytes 8388608 | tf_op jit(solution)/shard_map/pallas_call | solution.py:609
  153.3 2.8 %collective-permute-done.23.rest_1_ = bf16[66,1024]{1,0:T(8,128)(2,1)S(1)} collective-permute-done((bf16[66,1024]{1,0:T(8,128)(2,1)S(1)}, bf16[66,1024]{1,0:T(8,128)(2,1)S(1)}, u32[]{:S(2)}, u32[]{:S(2)}) %collective-permute-start.23) | collective-permute-done | bytes 135200 | tf_op jit(solution)/shard_map/ppermute | solution.py:715
  (73 shorter events, 12.9 us)
Async XLA Ops:
  2.1 16.2 %all-to-all-start = ((bf16[8,8,2048]{2,1,0:T(8,128)(2,1)}), bf16[8,8,2048]{2,1,0:T(8,128)(2,1)S(1)}, u32[]{:S(2)}, u32[]{:S(2)}) async-start(bf16[8,8,2048]{2,1,0:T(8,128)(2,1)} %broadcast_in_dim.2), calls=%async_computation | async-start | bytes 524288 | tf_op jit(solution)/shard_map/all_to_all | solution.py:668
  9.4 13.2 %copy-start.3 = (f32[2048]{0:T(1024)S(1)}, f32[2048]{0:T(1024)}, u32[]{:S(2)}) copy-start(f32[2048]{0:T(1024)} %param.18) | copy-start | bytes 24580
  9.4 13.2 %copy-start.5 = (s32[8]{0:T(128)S(1)}, s32[8]{0:T(128)}, u32[]{:S(2)}) copy-start(s32[8]{0:T(128)} %home.7) | copy-start | bytes 100
  9.4 13.2 %copy-start.6 = (s32[8,32]{1,0:T(8,128)S(1)}, s32[8,32]{1,0:T(8,128)}, u32[]{:S(2)}) copy-start(s32[8,32]{1,0:T(8,128)} %pages.1) | copy-start | bytes 3076
  9.4 13.2 %copy-start.7 = (s32[64]{0:T(128)S(1)}, s32[64]{0:T(128)}, u32[]{:S(2)}) copy-start(s32[64]{0:T(128)} %slots_of.1) | copy-start | bytes 772
  9.4 13.2 %copy-start.8 = (s32[8]{0:T(128)S(1)}, s32[8]{0:T(128)}, u32[]{:S(2)}) copy-start(s32[8]{0:T(128)} %lengths.2) | copy-start | bytes 100
  9.4 13.2 %copy-start.9 = (s32[1,48]{1,0:T(1,128)S(1)}, s32[1,48]{1,0:T(1,128)}, u32[]{:S(2)}) copy-start(s32[1,48]{1,0:T(1,128)} %param.25) | copy-start | bytes 580
  18.3 23.5 %all-to-all-start.1 = ((bf16[8,384,128]{2,1,0:T(8,128)(2,1)}), bf16[8,384,128]{2,1,0:T(8,128)(2,1)S(1)}, u32[]{:S(2)}, u32[]{:S(2)}) async-start(bf16[8,384,128]{2,1,0:T(8,128)(2,1)} %shard_map.167), calls=%async_computation.1 | async-start | bytes 1572864 | tf_op jit(solution)/shard_map/all_to_all | solution.py:671
  41.8 1.4 copy-start.10
  43.2 38.2 %copy-start.2 = (bf16[512,2048]{1,0:T(8,128)(2,1)S(1)}, bf16[512,2048]{1,0:T(8,128)(2,1)}, u32[]{:S(2)}) copy-start(bf16[512,2048]{1,0:T(8,128)(2,1)} %w_out.1) | copy-start | bytes 6291460
  83.9 1.6 %collective-permute-start = (bf16[66,2048]{1,0:T(8,128)(2,1)S(1)}, bf16[66,2048]{1,0:T(8,128)(2,1)S(1)}, u32[]{:S(2)}, u32[]{:S(2)}) collective-permute-start(bf16[66,2048]{1,0:T(8,128)(2,1)S(1)} %get-tuple-element.63), channel_id=1, source_target_pairs={{0,1},{1,0},{2,3},{3,2},{4,5},{5,4},{6,7},{7,6},{8,9},{9,8},{10,11... | collective-permute-start | bytes 811016 | tf_op jit(solution)/shard_map/ppermute | solution.py:688
  83.9 11.6 %collective-permute-start.2 = (bf16[66,2048]{1,0:T(8,128)(2,1)}, bf16[66,2048]{1,0:T(8,128)(2,1)S(1)}, u32[]{:S(2)}, u32[]{:S(2)}) collective-permute-start(bf16[66,2048]{1,0:T(8,128)(2,1)} %get-tuple-element.65), channel_id=1, source_target_pairs={{0,1},{1,0},{2,3},{3,2},{4,5},{5,4},{6,7},{7,6},{8,9},{9,8},{10,11... | collective-permute-start | bytes 811016 | tf_op jit(solution)/shard_map/ppermute | solution.py:690
  86.3 9.3 %collective-permute-start.1 = (bf16[66,2048]{1,0:T(8,128)(2,1)}, bf16[66,2048]{1,0:T(8,128)(2,1)S(1)}, u32[]{:S(2)}, u32[]{:S(2)}) collective-permute-start(bf16[66,2048]{1,0:T(8,128)(2,1)} %add_convert_fusion), channel_id=1, source_target_pairs={{0,2},{1,3},{2,0},{3,1},{4,6},{5,7},{6,4},{7,5},{8,10},{9,11},{10,... | collective-permute-start | bytes 811016 | tf_op jit(solution)/shard_map/ppermute | solution.py:689
  88.5 7.1 %copy-start.4 = (f32[2048]{0:T(1024)S(1)}, f32[2048]{0:T(1024)}, u32[]{:S(2)}) copy-start(f32[2048]{0:T(1024)} %param.21) | copy-start | bytes 24580
  88.5 19.4 %copy-start.1 = (bf16[640,2048]{1,0:T(8,128)(2,1)S(1)}, bf16[640,2048]{1,0:T(8,128)(2,1)}, u32[]{:S(2)}) copy-start(bf16[640,2048]{1,0:T(8,128)(2,1)} %refs_3_.3) | copy-start | bytes 7864324
  95.8 6.8 %collective-permute-start.3 = (bf16[66,1024]{1,0:T(8,128)(2,1)S(1)}, bf16[66,1024]{1,0:T(8,128)(2,1)S(1)}, u32[]{:S(2)}, u32[]{:S(2)}) collective-permute-start(bf16[66,1024]{1,0:T(8,128)(2,1)S(1)} %get-tuple-element.90.refs_0_), channel_id=1, source_target_pairs={{0,8},{8,16},{16,24},{24,28},{28,20},{20,12},{12,4},{4,0},{1,9},{9... | collective-permute-start | bytes 405512 | tf_op jit(solution)/shard_map/ppermute | solution.py:698
  96.6 6.8 %collective-permute-start.5 = (bf16[66,1024]{1,0:T(8,128)(2,1)S(1)}, bf16[66,1024]{1,0:T(8,128)(2,1)S(1)}, u32[]{:S(2)}, u32[]{:S(2)}) collective-permute-start(bf16[66,1024]{1,0:T(8,128)(2,1)S(1)} %get-tuple-element.91.refs_1_), channel_id=1, source_target_pairs={{8,0},{16,8},{24,16},{28,24},{20,28},{12,20},{4,12},{0,4},{9,1},{1... | collective-permute-start | bytes 405512 | tf_op jit(solution)/shard_map/ppermute | solution.py:699
  97.9 7.9 %collective-permute-start.7 = (bf16[66,1024]{1,0:T(8,128)(2,1)S(1)}, bf16[66,1024]{1,0:T(8,128)(2,1)S(1)}, u32[]{:S(2)}, u32[]{:S(2)}) collective-permute-start(bf16[66,1024]{1,0:T(8,128)(2,1)S(1)} %get-tuple-element.91.refs_1_), channel_id=1, source_target_pairs={{0,8},{8,16},{16,24},{24,28},{28,20},{20,12},{12,4},{4,0},{1,9},{9... | collective-permute-start | bytes 405512 | tf_op jit(solution)/shard_map/ppermute | solution.py:702
  98.7 7.9 %collective-permute-start.8 = (bf16[66,1024]{1,0:T(8,128)(2,1)S(1)}, bf16[66,1024]{1,0:T(8,128)(2,1)S(1)}, u32[]{:S(2)}, u32[]{:S(2)}) collective-permute-start(bf16[66,1024]{1,0:T(8,128)(2,1)S(1)} %get-tuple-element.90.refs_0_), channel_id=1, source_target_pairs={{8,0},{16,8},{24,16},{28,24},{20,28},{12,20},{4,12},{0,4},{9,1},{1... | collective-permute-start | bytes 405512 | tf_op jit(solution)/shard_map/ppermute | solution.py:701
  102.7 9.5 %collective-permute-start.4 = (bf16[66,1024]{1,0:T(8,128)(2,1)S(1)}, bf16[66,1024]{1,0:T(8,128)(2,1)S(1)}, u32[]{:S(2)}, u32[]{:S(2)}) collective-permute-start(bf16[66,1024]{1,0:T(8,128)(2,1)S(1)} %collective-permute-done.3.refs_0_), channel_id=1, source_target_pairs={{0,8},{8,16},{16,24},{24,28},{28,20},{20,12},{12,4},{4,0},{1,9},{9... | collective-permute-start | bytes 405512 | tf_op jit(solution)/shard_map/ppermute | solution.py:698
  103.4 8.8 %collective-permute-start.6 = (bf16[66,1024]{1,0:T(8,128)(2,1)S(1)}, bf16[66,1024]{1,0:T(8,128)(2,1)S(1)}, u32[]{:S(2)}, u32[]{:S(2)}) collective-permute-start(bf16[66,1024]{1,0:T(8,128)(2,1)S(1)} %collective-permute-done.5.refs_3_), channel_id=1, source_target_pairs={{8,0},{16,8},{24,16},{28,24},{20,28},{12,20},{4,12},{0,4},{9,1},{1... | collective-permute-start | bytes 405512 | tf_op jit(solution)/shard_map/ppermute | solution.py:699
  105.8 8.5 %collective-permute-start.11 = (bf16[66,1024]{1,0:T(8,128)(2,1)S(1)}, bf16[66,1024]{1,0:T(8,128)(2,1)S(1)}, u32[]{:S(2)}, u32[]{:S(2)}) collective-permute-start(bf16[66,1024]{1,0:T(8,128)(2,1)S(1)} %collective-permute-done.7.refs_1_), channel_id=1, source_target_pairs={{0,8},{8,16},{16,24},{24,28},{28,20},{20,12},{12,4},{4,0},{1,9},{9... | collective-permute-start | bytes 405512 | tf_op jit(solution)/shard_map/ppermute | solution.py:702
  106.6 8.5 %collective-permute-start.12 = (bf16[66,1024]{1,0:T(8,128)(2,1)S(1)}, bf16[66,1024]{1,0:T(8,128)(2,1)S(1)}, u32[]{:S(2)}, u32[]{:S(2)}) collective-permute-start(bf16[66,1024]{1,0:T(8,128)(2,1)S(1)} %collective-permute-done.8.refs_2_), channel_id=1, source_target_pairs={{8,0},{16,8},{24,16},{28,24},{20,28},{12,20},{4,12},{0,4},{9,1},{1... | collective-permute-start | bytes 405512 | tf_op jit(solution)/shard_map/ppermute | solution.py:701
  107.9 2.5 %copy-start = (bf16[2048,2,640]{2,0,1:T(8,128)(2,1)S(1)}, bf16[2048,2,640]{2,0,1:T(8,128)(2,1)}, u32[]{:S(2)}) copy-start(bf16[2048,2,640]{2,0,1:T(8,128)(2,1)} %copy.20) | copy-start | bytes 15728644
  112.2 5.9 %collective-permute-start.10 = (bf16[66,1024]{1,0:T(8,128)(2,1)S(1)}, bf16[66,1024]{1,0:T(8,128)(2,1)S(1)}, u32[]{:S(2)}, u32[]{:S(2)}) collective-permute-start(bf16[66,1024]{1,0:T(8,128)(2,1)S(1)} %collective-permute-done.6.refs_3_), channel_id=1, source_target_pairs={{8,0},{16,8},{24,16},{28,24},{20,28},{12,20},{4,12},{0,4},{9,1},{1... | collective-permute-start | bytes 405512 | tf_op jit(solution)/shard_map/ppermute | solution.py:699
  113.1 6.2 %collective-permute-start.9 = (bf16[66,1024]{1,0:T(8,128)(2,1)S(1)}, bf16[66,1024]{1,0:T(8,128)(2,1)S(1)}, u32[]{:S(2)}, u32[]{:S(2)}) collective-permute-start(bf16[66,1024]{1,0:T(8,128)(2,1)S(1)} %collective-permute-done.4.refs_0_), channel_id=1, source_target_pairs={{0,8},{8,16},{16,24},{24,28},{28,20},{20,12},{12,4},{4,0},{1,9},{9... | collective-permute-start | bytes 405512 | tf_op jit(solution)/shard_map/ppermute | solution.py:698
  114.3 7.0 %collective-permute-start.15 = (bf16[66,1024]{1,0:T(8,128)(2,1)S(1)}, bf16[66,1024]{1,0:T(8,128)(2,1)S(1)}, u32[]{:S(2)}, u32[]{:S(2)}) collective-permute-start(bf16[66,1024]{1,0:T(8,128)(2,1)S(1)} %collective-permute-done.11.refs_1_), channel_id=1, source_target_pairs={{0,8},{8,16},{16,24},{24,28},{28,20},{20,12},{12,4},{4,0},{1,9},{9... | collective-permute-start | bytes 405512 | tf_op jit(solution)/shard_map/ppermute | solution.py:702
  115.0 6.3 %collective-permute-start.16 = (bf16[66,1024]{1,0:T(8,128)(2,1)S(1)}, bf16[66,1024]{1,0:T(8,128)(2,1)S(1)}, u32[]{:S(2)}, u32[]{:S(2)}) collective-permute-start(bf16[66,1024]{1,0:T(8,128)(2,1)S(1)} %collective-permute-done.12.refs_2_), channel_id=1, source_target_pairs={{8,0},{16,8},{24,16},{28,24},{20,28},{12,20},{4,12},{0,4},{9,1},{1... | collective-permute-start | bytes 405512 | tf_op jit(solution)/shard_map/ppermute | solution.py:701
  119.3 5.2 %collective-permute-start.13 = (bf16[66,1024]{1,0:T(8,128)(2,1)S(1)}, bf16[66,1024]{1,0:T(8,128)(2,1)S(1)}, u32[]{:S(2)}, u32[]{:S(2)}) collective-permute-start(bf16[66,1024]{1,0:T(8,128)(2,1)S(1)} %collective-permute-done.9.refs_0_), channel_id=1, source_target_pairs={{0,8},{8,16},{16,24},{24,28},{28,20},{20,12},{12,4},{4,0},{1,9},{9... | collective-permute-start | bytes 405512 | tf_op jit(solution)/shard_map/ppermute | solution.py:698
  120.2 6.7 %collective-permute-start.14 = (bf16[66,1024]{1,0:T(8,128)(2,1)S(1)}, bf16[66,1024]{1,0:T(8,128)(2,1)S(1)}, u32[]{:S(2)}, u32[]{:S(2)}) collective-permute-start(bf16[66,1024]{1,0:T(8,128)(2,1)S(1)} %collective-permute-done.10.refs_3_), channel_id=1, source_target_pairs={{8,0},{16,8},{24,16},{28,24},{20,28},{12,20},{4,12},{0,4},{9,1},{1... | collective-permute-start | bytes 405512 | tf_op jit(solution)/shard_map/ppermute | solution.py:699
  126.9 24.6 %slice-start = ((s8[5242880]{0:T(1024)(128)(4,1)}), s8[4194304]{0:T(1024)(128)(4,1)S(1)}, s32[]{:S(2)}) async-start(s8[5242880]{0:T(1024)(128)(4,1)} %bitcast.18), calls=%async_computation.3 | async-start | bytes 8388608
  126.9 24.6 %slice-start.1 = ((s8[5242880]{0:T(1024)(128)(4,1)}), s8[1048576]{0:T(1024)(128)(4,1)S(1)}, s32[]{:S(2)}) async-start(s8[5242880]{0:T(1024)(128)(4,1)} %bitcast.18), calls=%async_computation.4 | async-start | bytes 2097152
  128.6 6.7 %collective-permute-start.27 = (bf16[66,1024]{1,0:T(8,128)(2,1)S(1)}, bf16[66,1024]{1,0:T(8,128)(2,1)S(1)}, u32[]{:S(2)}, u32[]{:S(2)}) collective-permute-start(bf16[66,1024]{1,0:T(8,128)(2,1)S(1)} %get-tuple-element.107), channel_id=1, source_target_pairs={{8,0},{16,8},{24,16},{28,24},{20,28},{12,20},{4,12},{0,4},{9,1},{1... | collective-permute-start | bytes 405512 | tf_op jit(solution)/shard_map/ppermute | solution.py:714
  129.8 6.8 %collective-permute-start.24 = (bf16[66,1024]{1,0:T(8,128)(2,1)S(1)}, bf16[66,1024]{1,0:T(8,128)(2,1)S(1)}, u32[]{:S(2)}, u32[]{:S(2)}) collective-permute-start(bf16[66,1024]{1,0:T(8,128)(2,1)S(1)} %get-tuple-element.103), channel_id=1, source_target_pairs={{0,8},{8,16},{16,24},{24,28},{28,20},{20,12},{12,4},{4,0},{1,9},{9... | collective-permute-start | bytes 405512 | tf_op jit(solution)/shard_map/ppermute | solution.py:714
  130.7 8.2 %collective-permute-start.20 = (bf16[66,1024]{1,0:T(8,128)(2,1)S(1)}, bf16[66,1024]{1,0:T(8,128)(2,1)S(1)}, u32[]{:S(2)}, u32[]{:S(2)}) collective-permute-start(bf16[66,1024]{1,0:T(8,128)(2,1)S(1)} %get-tuple-element.100), channel_id=1, source_target_pairs={{0,8},{8,16},{16,24},{24,28},{28,20},{20,12},{12,4},{4,0},{1,9},{9... | collective-permute-start | bytes 405512 | tf_op jit(solution)/shard_map/ppermute | solution.py:714
  131.2 8.6 %collective-permute-start.17 = (bf16[66,1024]{1,0:T(8,128)(2,1)S(1)}, bf16[66,1024]{1,0:T(8,128)(2,1)S(1)}, u32[]{:S(2)}, u32[]{:S(2)}) collective-permute-start(bf16[66,1024]{1,0:T(8,128)(2,1)S(1)} %get-tuple-element.96), channel_id=1, source_target_pairs={{8,0},{16,8},{24,16},{28,24},{20,28},{12,20},{4,12},{0,4},{9,1},{1... | collective-permute-start | bytes 405512 | tf_op jit(solution)/shard_map/ppermute | solution.py:714
  135.3 6.6 %collective-permute-start.28 = (bf16[66,1024]{1,0:T(8,128)(2,1)S(1)}, bf16[66,1024]{1,0:T(8,128)(2,1)S(1)}, u32[]{:S(2)}, u32[]{:S(2)}) collective-permute-start(bf16[66,1024]{1,0:T(8,128)(2,1)S(1)} %add_convert_fusion.3), channel_id=1, source_target_pairs={{8,0},{16,8},{24,16},{28,24},{20,28},{12,20},{4,12},{0,4},{9,1},{1... | collective-permute-start | bytes 405512 | tf_op jit(solution)/shard_map/ppermute | solution.py:714
  136.7 6.6 %collective-permute-start.25 = (bf16[66,1024]{1,0:T(8,128)(2,1)S(1)}, bf16[66,1024]{1,0:T(8,128)(2,1)S(1)}, u32[]{:S(2)}, u32[]{:S(2)}) collective-permute-start(bf16[66,1024]{1,0:T(8,128)(2,1)S(1)} %add_convert_fusion.5), channel_id=1, source_target_pairs={{0,8},{8,16},{16,24},{24,28},{28,20},{20,12},{12,4},{4,0},{1,9},{9... | collective-permute-start | bytes 405512 | tf_op jit(solution)/shard_map/ppermute | solution.py:714
  138.9 6.8 %collective-permute-start.21 = (bf16[66,1024]{1,0:T(8,128)(2,1)S(1)}, bf16[66,1024]{1,0:T(8,128)(2,1)S(1)}, u32[]{:S(2)}, u32[]{:S(2)}) collective-permute-start(bf16[66,1024]{1,0:T(8,128)(2,1)S(1)} %add_convert_fusion.8), channel_id=1, source_target_pairs={{0,8},{8,16},{16,24},{24,28},{28,20},{20,12},{12,4},{4,0},{1,9},{9... | collective-permute-start | bytes 405512 | tf_op jit(solution)/shard_map/ppermute | solution.py:714
  139.8 6.4 %collective-permute-start.18 = (bf16[66,1024]{1,0:T(8,128)(2,1)S(1)}, bf16[66,1024]{1,0:T(8,128)(2,1)S(1)}, u32[]{:S(2)}, u32[]{:S(2)}) collective-permute-start(bf16[66,1024]{1,0:T(8,128)(2,1)S(1)} %add_convert_fusion.10), channel_id=1, source_target_pairs={{8,0},{16,8},{24,16},{28,24},{20,28},{12,20},{4,12},{0,4},{9,1},{1... | collective-permute-start | bytes 405512 | tf_op jit(solution)/shard_map/ppermute | solution.py:714
  142.0 5.9 %collective-permute-start.29 = (bf16[66,1024]{1,0:T(8,128)(2,1)S(1)}, bf16[66,1024]{1,0:T(8,128)(2,1)S(1)}, u32[]{:S(2)}, u32[]{:S(2)}) collective-permute-start(bf16[66,1024]{1,0:T(8,128)(2,1)S(1)} %add_convert_fusion.2), channel_id=1, source_target_pairs={{8,0},{16,8},{24,16},{28,24},{20,28},{12,20},{4,12},{0,4},{9,1},{1... | collective-permute-start | bytes 405512 | tf_op jit(solution)/shard_map/ppermute | solution.py:714
  143.3 9.9 %collective-permute-start.26 = (bf16[66,1024]{1,0:T(8,128)(2,1)S(1)}, bf16[66,1024]{1,0:T(8,128)(2,1)S(1)}, u32[]{:S(2)}, u32[]{:S(2)}) collective-permute-start(bf16[66,1024]{1,0:T(8,128)(2,1)S(1)} %add_convert_fusion.4), channel_id=1, source_target_pairs={{0,8},{8,16},{16,24},{24,28},{28,20},{20,12},{12,4},{4,0},{1,9},{9... | collective-permute-start | bytes 405512 | tf_op jit(solution)/shard_map/ppermute | solution.py:715
  145.7 5.2 %collective-permute-start.22 = (bf16[66,1024]{1,0:T(8,128)(2,1)S(1)}, bf16[66,1024]{1,0:T(8,128)(2,1)S(1)}, u32[]{:S(2)}, u32[]{:S(2)}) collective-permute-start(bf16[66,1024]{1,0:T(8,128)(2,1)S(1)} %add_convert_fusion.7), channel_id=1, source_target_pairs={{0,8},{8,16},{16,24},{24,28},{28,20},{20,12},{12,4},{4,0},{1,9},{9... | collective-permute-start | bytes 405512 | tf_op jit(solution)/shard_map/ppermute | solution.py:714
  146.3 6.9 %collective-permute-start.19 = (bf16[66,1024]{1,0:T(8,128)(2,1)S(1)}, bf16[66,1024]{1,0:T(8,128)(2,1)S(1)}, u32[]{:S(2)}, u32[]{:S(2)}) collective-permute-start(bf16[66,1024]{1,0:T(8,128)(2,1)S(1)} %add_convert_fusion.9), channel_id=1, source_target_pairs={{8,0},{16,8},{24,16},{28,24},{20,28},{12,20},{4,12},{0,4},{9,1},{1... | collective-permute-start | bytes 405512 | tf_op jit(solution)/shard_map/ppermute | solution.py:715
  147.9 5.4 %collective-permute-start.30 = (bf16[66,1024]{1,0:T(8,128)(2,1)S(1)}, bf16[66,1024]{1,0:T(8,128)(2,1)S(1)}, u32[]{:S(2)}, u32[]{:S(2)}) collective-permute-start(bf16[66,1024]{1,0:T(8,128)(2,1)S(1)} %add_convert_fusion.1), channel_id=1, source_target_pairs={{8,0},{16,8},{24,16},{28,24},{20,28},{12,20},{4,12},{0,4},{9,1},{1... | collective-permute-start | bytes 405512 | tf_op jit(solution)/shard_map/ppermute | solution.py:715
  150.9 5.2 %collective-permute-start.23 = (bf16[66,1024]{1,0:T(8,128)(2,1)S(1)}, bf16[66,1024]{1,0:T(8,128)(2,1)S(1)}, u32[]{:S(2)}, u32[]{:S(2)}) collective-permute-start(bf16[66,1024]{1,0:T(8,128)(2,1)S(1)} %add_convert_fusion.6), channel_id=1, source_target_pairs={{0,8},{8,16},{16,24},{24,28},{28,20},{20,12},{12,4},{4,0},{1,9},{9... | collective-permute-start | bytes 405512 | tf_op jit(solution)/shard_map/ppermute | solution.py:715

commit v5 on v4

--- a/solution.py
+++ b/solution.py
@@ -538,6 +538,24 @@
     )(own_pre, own_dec, gain, *terms)
 
 
+def hold_kernel(source, out, sem):
+    copy = pltpu.make_async_copy(source, out, sem)
+    copy.start()
+    copy.wait()
+
+
+def hold(array):
+    return pl.pallas_call(
+        hold_kernel,
+        out_shape=jax.ShapeDtypeStruct(array.shape, array.dtype),
+        in_specs=[ANY],
+        out_specs=VMEM,
+        scratch_shapes=[pltpu.SemaphoreType.DMA],
+        compiler_params=pltpu.CompilerParams(vmem_limit_bytes=24 * 2**20),
+        cost_estimate=pl.CostEstimate(flops=0, bytes_accessed=2 * array.size * 2, transcendentals=0),
+    )(array)
+
+
 def finish_kernel(resid, own_left, own_right, *rest):
     sums, outs = rest[:-2], rest[-2:]
     middle = own_left.shape[1]
@@ -674,8 +692,10 @@
         rows, gain, w_three, decode_pool, prefill_pool,
     )
     attn = prefill_attention(prefill_lengths, prefill_home, ids, arrived, old_keys, old_values, decoded)
+    attn, w_gate_up = lax.optimization_barrier((attn, w_gate_up))
     returned = lax.all_to_all(attn, "tok", split_axis=0, concat_axis=0, tiled=True)
     gate_up = jnp.transpose(w_gate_up, (1, 0, 2))
+    returned, gate_up = lax.optimization_barrier((returned, gate_up))
 
     parts = project_out(prefill_home, decode_home, ids, returned, w_out, requests, heads, n_head, hosted)
     block_rows = positions // n_head
@@ -688,6 +708,7 @@
         both = joined(parts[k], lax.ppermute(parts[k + 1], "head", swap))
         terms.append(lax.ppermute(both, "head", [(i, i ^ k) for i in range(n_head)]))
     terms.append(lax.ppermute(parts[1], "head", swap))
+    gate_up = hold(gate_up)
     terms[1], gate_up = lax.optimization_barrier((terms[1], gate_up))
     resid, left, right = middle(own_pre.reshape(requests * block_rows, width), own_dec, ffn_gain.reshape(1, width), terms)
 

time: 157 us -> 155 us (0.987)
  blocking collectives: 15.5 us -> 0 us
  starting transfers between devices: 41.2 us -> 48.6 us
  waiting for transfers between devices: 25 us -> 30.6 us
    all_to_all x1 -> x0, blocking collectives: 15.5 us -> none  [shards(): lax.all_to_all(attn, 'tok', split_axis=0, concat_axis=0, tiled=True)]
    unnamed x27 -> x22, local copies, waits for them, and re-layouts: 9.59 us -> 3.93 us
    all_to_all x0 -> x1, starting transfers between devices: none -> 5.65 us  [shards(): lax.all_to_all(attn, 'tok', split_axis=0, concat_axis=0, tiled=True)]
    optimization_barrier x0 -> x1, local copies, waits for them, and re-layouts: none -> 5.63 us  [shards(): attn, w_gate_up = lax.optimization_barrier((attn, w_gate_up))]
    all_to_all x0 -> x1, waiting for transfers between devices: none -> 3.7 us  [shards(): lax.all_to_all(attn, 'tok', split_axis=0, concat_axis=0, tiled=True)]
    ppermute x1, waiting for transfers between devices: 0.42 us -> 2.9 us  [shards(): lax.ppermute(both, 'head', [(i, i ^ k) for i in range(n_head)])]
    ppermute x4, starting transfers between devices: 3.82 us -> 5.43 us  [chain(): return lax.ppermute(part, 'tok', steps)]
    ppermute x10, waiting for transfers between devices: 8.42 us -> 6.8 us  [chain(): part = joined(table[k][side], lax.ppermute(part, 'tok', steps))]
  transfers between devices with their start and end apart: 33 -> 34, of which waited for: 15 -> 18; matrix products, arithmetic and copies ran while one was open for 5% -> 5% of each run, Pallas kernels for 20% -> 20%
where the time goes in v5:
time: 155 us; the launch traced here: 154 us
  Pallas kernels  60.3 us (39%)
  starting transfers between devices  48.6 us (31%)
  waiting for transfers between devices  30.6 us (20%)
  local copies, waits for them, and re-layouts  12.8 us (8%)
  between operations  1.58 us (1%)
    pallas_call x1, Pallas kernels, prefill_attention(): pl.pallas_call(functools.partial(prefill_kernel, positions), out_shape=ja...  23.4 us
    pallas_call x1, Pallas kernels, decode_attention(): pl.pallas_call(functools.partial(decode_kernel, heads), out_shape=[jax.Sh...  18.2 us
    ppermute x10, starting transfers between devices, chain(): part = joined(table[k][side], lax.ppermute(part, 'tok', steps))  10.2 us
    pallas_call x5, Pallas kernels, feed_forward(): pl.pallas_call(functools.partial(feed_kernel, [len(chunk) for chunk in ch...  8.93 us
    all_to_all x1, starting transfers between devices, shards(): lax.all_to_all(copies, 'tok', split_axis=0, concat_axis=0, tiled=True)  7.28 us
    ppermute x10, waiting for transfers between devices, chain(): part = joined(table[k][side], lax.ppermute(part, 'tok', steps))  6.8 us
    pallas_call x1, Pallas kernels, qkv_messages(): pl.pallas_call(functools.partial(qkv_kernel, requests, heads), out_shape=...  5.89 us
    all_to_all x1, starting transfers between devices, shards(): lax.all_to_all(attn, 'tok', split_axis=0, concat_axis=0, tiled=True)  5.65 us
  transfers between devices with their start and end apart: 34, of which 18 were waited for; matrix products, arithmetic and copies ran while one was open for 5% of the time, Pallas kernels for 20%

profile of v5, /device:TPU:0, one launch (start us, length us, event | category | flops | bytes accessed | tf_op | source)
XLA Modules:
  0.0 154.5 jit_solution(6603722872712217305)
XLA Ops:
  0.7 1.5 broadcast_in_dim.2
  2.2 7.3 %all-to-all-start = ((bf16[8,8,2048]{2,1,0:T(8,128)(2,1)}), bf16[8,8,2048]{2,1,0:T(8,128)(2,1)S(1)}, u32[]{:S(2)}, u32[]{:S(2)}) async-start(bf16[8,8,2048]{2,1,0:T(8,128)(2,1)} %broadcast_in_dim.2), calls=%async_computation | async-start | bytes 524288 | tf_op jit(solution)/shard_map/all_to_all | solution.py:686
  9.5 5.9 %shard_map.167 = bf16[8,384,128]{2,1,0:T(8,128)(2,1)} custom-call(s32[8]{0:T(128)} %home.7, f32[1,2048]{1,0:T(1,128)} %bitcast.16, bf16[256,2048]{1,0:T(8,128)(2,1)} %bitcast.22, bf16[3,2048,512]{2,1,0:T(8,128)(2,1)} %bitcast.20), custom_call_target="tpu_custom_call" | custom-call | flops 1610612736 | bytes 10485760 | tf_op jit(solution)/shard_map/pallas_call | solution.py:429
  15.4 3.0 %all-to-all-done = bf16[8,8,2048]{2,1,0:T(8,128)(2,1)S(1)} async-done(((bf16[8,8,2048]{2,1,0:T(8,128)(2,1)}), bf16[8,8,2048]{2,1,0:T(8,128)(2,1)S(1)}, u32[]{:S(2)}, u32[]{:S(2)}) %all-to-all-start) | async-done | bytes 262176 | tf_op jit(solution)/shard_map/all_to_all | solution.py:686
  18.4 3.6 %all-to-all-start.1 = ((bf16[8,384,128]{2,1,0:T(8,128)(2,1)}), bf16[8,384,128]{2,1,0:T(8,128)(2,1)S(1)}, u32[]{:S(2)}, u32[]{:S(2)}) async-start(bf16[8,384,128]{2,1,0:T(8,128)(2,1)} %shard_map.167), calls=%async_computation.1 | async-start | bytes 1572864 | tf_op jit(solution)/shard_map/all_to_all | solution.py:689
  22.8 18.2 %shard_map.168 = (f32[8,512]{1,0:T(8,128)S(1)}, bf16[6,128,1024]{2,1,0:T(8,128)(2,1)S(1)}, bf16[6,1024,128]{2,1,0:T(8,128)(2,1)}) custom-call(s32[8]{0:T(128)S(1)} %copy-done.8, s32[64]{0:T(128)S(1)} %copy-done.7, s32[2]{0:T(128)S(1)} %pad_add_fusion.ids, s32[8,32]{1,0:T(8,128)S(1)} %copy-done.6, s32[1]{0:T(128)S(6)} %copy.21.old_lengths.lengths, ...), custom_call_target="tpu_custom_call" | custom-call | flops 2000000000 | bytes 23068672 | tf_op jit(solution)/shard_map/pallas_call | solution.py:360
  41.9 1.4 copy-done.10
  43.3 23.4 %shard_map.169 = bf16[8,160,128]{2,1,0:T(8,128)(2,1)} custom-call(s32[1]{0:T(128)S(6)} %copy.21.old_lengths.lengths, s32[8]{0:T(128)S(1)} %copy-done.5, s32[2]{0:T(128)S(1)} %pad_add_fusion.ids, bf16[8,384,128]{2,1,0:T(8,128)(2,1)S(1)} %all-to-all-done.1.msg, bf16[6,128,1024]{2,1,0:T(8,128)(2,1)S(1)} %get-tuple-element.62.flipped_in, ...), custom_call_target="tpu_custom_call" | custom-call | flops 4294967296 | bytes 4194304 | tf_op jit(solution)/shard_map/pallas_call | solution.py:203
  66.7 5.7 %all-to-all-start.2 = ((bf16[8,160,128]{2,1,0:T(8,128)(2,1)}), bf16[8,160,128]{2,1,0:T(8,128)(2,1)S(1)}, u32[]{:S(2)}, u32[]{:S(2)}) async-start(bf16[8,160,128]{2,1,0:T(8,128)(2,1)} %shard_map.169), calls=%async_computation.2 | async-start | bytes 655360 | tf_op jit(solution)/shard_map/all_to_all | solution.py:696
  72.3 5.6 %copy.20 = bf16[2048,2,640]{2,0,1:T(8,128)(2,1)} copy(bf16[2048,2,640]{2,1,0:T(2,128)(2,1)} %param.22) | data formatting | bytes 10485760 | tf_op jit(solution)/shard_map/optimization_barrier | solution.py:695
  77.9 3.7 %all-to-all-done.2.received = bf16[8,160,128]{2,1,0:T(8,128)(2,1)S(1)} async-done(((bf16[8,160,128]{2,1,0:T(8,128)(2,1)}), bf16[8,160,128]{2,1,0:T(8,128)(2,1)S(1)}, u32[]{:S(2)}, u32[]{:S(2)}) %all-to-all-start.2) | async-done | bytes 327712 | tf_op jit(solution)/shard_map/all_to_all | solution.py:696
  81.7 2.5 %shard_map.170 = (bf16[66,2048]{1,0:T(8,128)(2,1)S(1)}, bf16[66,2048]{1,0:T(8,128)(2,1)S(1)}, bf16[66,2048]{1,0:T(8,128)(2,1)S(1)}, bf16[66,2048]{1,0:T(8,128)(2,1)}) custom-call(s32[8]{0:T(128)S(1)} %copy-done.5, s32[64]{0:T(128)S(1)} %copy-done.7, s32[2]{0:T(128)S(1)} %pad_add_fusion.ids, bf16[8,160,128]{2,1,0:T(8,128)(2,1)S(1)} %all-to-all-done.2.received, ...), custom_call_target="tpu_custom_call" | custom-call | flops 553648128 | bytes 4194304 | tf_op jit(solution)/shard_map/pallas_call | solution.py:497
  84.7 1.3 collective-permute-done
  86.1 1.6 %collective-permute-start.1 = (bf16[66,2048]{1,0:T(8,128)(2,1)S(1)}, bf16[66,2048]{1,0:T(8,128)(2,1)S(1)}, u32[]{:S(2)}, u32[]{:S(2)}) collective-permute-start(bf16[66,2048]{1,0:T(8,128)(2,1)S(1)} %add_convert_fusion), channel_id=1, source_target_pairs={{0,2},{1,3},{2,0},{3,1},{4,6},{5,7},{6,4},{7,5},{8,10},{9,11},{10,... | collective-permute-start | bytes 811016 | tf_op jit(solution)/shard_map/ppermute | solution.py:709
  89.5 2.5 %copy-done.1 = bf16[2048,2,640]{2,0,1:T(8,128)(2,1)S(1)} copy-done((bf16[2048,2,640]{2,0,1:T(8,128)(2,1)S(1)}, bf16[2048,2,640]{2,0,1:T(8,128)(2,1)}, u32[]{:S(2)}) %copy-start.1) | copy-done | bytes 5242904
  92.3 2.9 %collective-permute-done.1.rest_1_ = bf16[66,2048]{1,0:T(8,128)(2,1)S(1)} collective-permute-done((bf16[66,2048]{1,0:T(8,128)(2,1)S(1)}, bf16[66,2048]{1,0:T(8,128)(2,1)S(1)}, u32[]{:S(2)}, u32[]{:S(2)}) %collective-permute-start.1) | collective-permute-done | bytes 270368 | tf_op jit(solution)/shard_map/ppermute | solution.py:709
  95.5 1.1 collective-permute-start.3
  97.6 1.0 collective-permute-start.7
  99.6 2.7 %collective-permute-done.3.refs_0_ = bf16[66,1024]{1,0:T(8,128)(2,1)S(1)} collective-permute-done((bf16[66,1024]{1,0:T(8,128)(2,1)S(1)}, bf16[66,1024]{1,0:T(8,128)(2,1)S(1)}, u32[]{:S(2)}, u32[]{:S(2)}) %collective-permute-start.3) | collective-permute-done | bytes 135200 | tf_op jit(solution)/shard_map/ppermute | solution.py:719
  102.3 1.0 collective-permute-start.4
  103.4 1.0 collective-permute-start.6
  104.4 1.1 collective-permute-done.7.refs_1_
  105.5 1.0 collective-permute-start.11
  107.5 1.8 %shard_map.173 = (bf16[66,1024]{1,0:T(8,128)(2,1)S(1)}, bf16[66,1024]{1,0:T(8,128)(2,1)S(1)}, bf16[66,1024]{1,0:T(8,128)(2,1)S(1)}, bf16[66,1024]{1,0:T(8,128)(2,1)S(1)}) custom-call(bf16[66,1024]{1,0:T(8,128)(2,1)S(1)} %collective-permute-done.3.refs_0_, bf16[66,1024]{1,0:T(8,128)(2,1)S(1)} %collective-permute-done.7.refs_1_, ...), custom_call_target="tpu_custom_call" | custom-call | flops 1038090240 | bytes 8388608 | tf_op jit(solution)/shard_map/pallas_call | solution.py:627
  110.9 1.2 collective-permute-start.9
  112.1 1.1 collective-permute-start.15
  114.3 1.8 %shard_map.174 = (bf16[66,1024]{1,0:T(8,128)(2,1)S(1)}, bf16[66,1024]{1,0:T(8,128)(2,1)S(1)}, bf16[66,1024]{1,0:T(8,128)(2,1)S(1)}, bf16[66,1024]{1,0:T(8,128)(2,1)S(1)}) custom-call(bf16[66,1024]{1,0:T(8,128)(2,1)S(1)} %collective-permute-done.4.refs_0_, bf16[66,1024]{1,0:T(8,128)(2,1)S(1)} %collective-permute-done.11.refs_1_, ...), custom_call_target="tpu_custom_call" | custom-call | flops 1038090240 | bytes 8388608 | tf_op jit(solution)/shard_map/pallas_call | solution.py:627
  116.2 1.1 collective-permute-done.9.refs_0_
  117.3 1.3 collective-permute-start.13
  119.3 1.8 %shard_map.175 = (bf16[66,1024]{1,0:T(8,128)(2,1)S(1)}, bf16[66,1024]{1,0:T(8,128)(2,1)S(1)}, bf16[66,1024]{1,0:T(8,128)(2,1)S(1)}, bf16[66,1024]{1,0:T(8,128)(2,1)S(1)}) custom-call(bf16[66,1024]{1,0:T(8,128)(2,1)S(1)} %collective-permute-done.9.refs_0_, bf16[66,1024]{1,0:T(8,128)(2,1)S(1)} %collective-permute-done.15.refs_1_, ...), custom_call_target="tpu_custom_call" | custom-call | flops 1038090240 | bytes 8388608 | tf_op jit(solution)/shard_map/pallas_call | solution.py:627
  121.2 1.3 collective-permute-done.13.refs_0_
  122.4 2.6 %collective-permute-done.14.refs_1_ = bf16[66,1024]{1,0:T(8,128)(2,1)S(1)} collective-permute-done((bf16[66,1024]{1,0:T(8,128)(2,1)S(1)}, bf16[66,1024]{1,0:T(8,128)(2,1)S(1)}, u32[]{:S(2)}, u32[]{:S(2)}) %collective-permute-start.14) | collective-permute-done | bytes 135200 | tf_op jit(solution)/shard_map/ppermute | solution.py:720
  125.0 1.7 %shard_map.176 = (bf16[66,1024]{1,0:T(8,128)(2,1)S(1)}, bf16[66,1024]{1,0:T(8,128)(2,1)S(1)}) custom-call(bf16[66,1024]{1,0:T(8,128)(2,1)S(1)} %collective-permute-done.13.refs_0_, bf16[66,1024]{1,0:T(8,128)(2,1)S(1)} %collective-permute-done.14.refs_1_, bf16[2,2048,640]{2,1,0:T(8,128)(2,1)S(1)} %shard_map.171.refs_4_.refs_2_, bf16[640,2048]{1,0:T(8,128)(2,1)S(1)} %copy-done), custom_call_target="tpu_custom_call" | custom-call | flops 519045120 | bytes 8388608 | tf_op jit(solution)/shard_map/pallas_call | solution.py:627
  127.0 1.8 %collective-permute-start.24 = (bf16[66,1024]{1,0:T(8,128)(2,1)S(1)}, bf16[66,1024]{1,0:T(8,128)(2,1)S(1)}, u32[]{:S(2)}, u32[]{:S(2)}) collective-permute-start(bf16[66,1024]{1,0:T(8,128)(2,1)S(1)} %get-tuple-element.111), channel_id=1, source_target_pairs={{0,8},{8,16},{16,24},{24,28},{28,20},{20,12},{12,4},{4,0},{1,9},{9... | collective-permute-start | bytes 405512 | tf_op jit(solution)/shard_map/ppermute | solution.py:735
  128.8 2.0 %collective-permute-start.17 = (bf16[66,1024]{1,0:T(8,128)(2,1)S(1)}, bf16[66,1024]{1,0:T(8,128)(2,1)S(1)}, u32[]{:S(2)}, u32[]{:S(2)}) collective-permute-start(bf16[66,1024]{1,0:T(8,128)(2,1)S(1)} %get-tuple-element.104), channel_id=1, source_target_pairs={{8,0},{16,8},{24,16},{28,24},{20,28},{12,20},{4,12},{0,4},{9,1},{1... | collective-permute-start | bytes 405512 | tf_op jit(solution)/shard_map/ppermute | solution.py:735
  130.8 2.6 %collective-permute-done.27 = bf16[66,1024]{1,0:T(8,128)(2,1)S(1)} collective-permute-done((bf16[66,1024]{1,0:T(8,128)(2,1)S(1)}, bf16[66,1024]{1,0:T(8,128)(2,1)S(1)}, u32[]{:S(2)}, u32[]{:S(2)}) %collective-permute-start.27) | collective-permute-done | bytes 135200 | tf_op jit(solution)/shard_map/ppermute | solution.py:735
  133.9 1.8 %collective-permute-start.25 = (bf16[66,1024]{1,0:T(8,128)(2,1)S(1)}, bf16[66,1024]{1,0:T(8,128)(2,1)S(1)}, u32[]{:S(2)}, u32[]{:S(2)}) collective-permute-start(bf16[66,1024]{1,0:T(8,128)(2,1)S(1)} %add_convert_fusion.5), channel_id=1, source_target_pairs={{0,8},{8,16},{16,24},{24,28},{28,20},{20,12},{12,4},{4,0},{1,9},{9... | collective-permute-start | bytes 405512 | tf_op jit(solution)/shard_map/ppermute | solution.py:735
  135.7 1.1 collective-permute-done.20
  136.8 1.1 collective-permute-start.21
  138.0 1.0 collective-permute-start.18
  139.0 1.1 collective-permute-done.28
  140.9 1.4 collective-permute-start.26
  143.2 1.2 collective-permute-start.22
  145.4 1.9 %collective-permute-start.30 = (bf16[66,1024]{1,0:T(8,128)(2,1)S(1)}, bf16[66,1024]{1,0:T(8,128)(2,1)S(1)}, u32[]{:S(2)}, u32[]{:S(2)}) collective-permute-start(bf16[66,1024]{1,0:T(8,128)(2,1)S(1)} %add_convert_fusion.1), channel_id=1, source_target_pairs={{8,0},{16,8},{24,16},{28,24},{20,28},{12,20},{4,12},{0,4},{9,1},{1... | collective-permute-start | bytes 405512 | tf_op jit(solution)/shard_map/ppermute | solution.py:736
  147.3 1.1 collective-permute-done.22
  148.5 1.2 collective-permute-start.23
  149.6 1.7 %shard_map.177 = (bf16[66,1024]{1,0:T(8,128)(2,1)S(1)}, bf16[66,1024]{1,0:T(8,128)(2,1)S(1)}) custom-call(bf16[66,1024]{1,0:T(8,128)(2,1)S(1)} %get-tuple-element.98.refs_0_, bf16[66,1024]{1,0:T(8,128)(2,1)S(1)} %get-tuple-element.99.refs_1_, bf16[2,2048,640]{2,1,0:T(8,128)(2,1)S(1)} %shard_map.171.refs_4_.refs_2_, bf16[640,2048]{1,0:T(8,128)(2,1)S(1)} %copy-done), custom_call_target="tpu_custom_call" | custom-call | flops 519045120 | bytes 8388608 | tf_op jit(solution)/shard_map/pallas_call | solution.py:627
  151.4 2.3 %collective-permute-done.23.rest_1_ = bf16[66,1024]{1,0:T(8,128)(2,1)S(1)} collective-permute-done((bf16[66,1024]{1,0:T(8,128)(2,1)S(1)}, bf16[66,1024]{1,0:T(8,128)(2,1)S(1)}, u32[]{:S(2)}, u32[]{:S(2)}) %collective-permute-start.23) | collective-permute-done | bytes 135200 | tf_op jit(solution)/shard_map/ppermute | solution.py:736
  (70 shorter events, 14.8 us)
Async XLA Ops:
  0.6 22.1 %copy-start.3 = (f32[2048]{0:T(1024)S(1)}, f32[2048]{0:T(1024)}, u32[]{:S(2)}) copy-start(f32[2048]{0:T(1024)} %param.18) | copy-start | bytes 24580
  0.6 22.1 %copy-start.5 = (s32[8]{0:T(128)S(1)}, s32[8]{0:T(128)}, u32[]{:S(2)}) copy-start(s32[8]{0:T(128)} %home.7) | copy-start | bytes 100
  0.7 22.1 %copy-start.9 = (s32[1,48]{1,0:T(1,128)S(1)}, s32[1,48]{1,0:T(1,128)}, u32[]{:S(2)}) copy-start(s32[1,48]{1,0:T(1,128)} %param.25) | copy-start | bytes 580
  0.7 22.1 %copy-start.6 = (s32[8,32]{1,0:T(8,128)S(1)}, s32[8,32]{1,0:T(8,128)}, u32[]{:S(2)}) copy-start(s32[8,32]{1,0:T(8,128)} %pages.1) | copy-start | bytes 3076
  0.7 22.1 %copy-start.8 = (s32[8]{0:T(128)S(1)}, s32[8]{0:T(128)}, u32[]{:S(2)}) copy-start(s32[8]{0:T(128)} %lengths.2) | copy-start | bytes 100
  0.7 22.1 %copy-start.7 = (s32[64]{0:T(128)S(1)}, s32[64]{0:T(128)}, u32[]{:S(2)}) copy-start(s32[64]{0:T(128)} %slots_of.1) | copy-start | bytes 772
  2.2 16.2 %all-to-all-start = ((bf16[8,8,2048]{2,1,0:T(8,128)(2,1)}), bf16[8,8,2048]{2,1,0:T(8,128)(2,1)S(1)}, u32[]{:S(2)}, u32[]{:S(2)}) async-start(bf16[8,8,2048]{2,1,0:T(8,128)(2,1)} %broadcast_in_dim.2), calls=%async_computation | async-start | bytes 524288 | tf_op jit(solution)/shard_map/all_to_all | solution.py:686
  18.4 23.5 %all-to-all-start.1 = ((bf16[8,384,128]{2,1,0:T(8,128)(2,1)}), bf16[8,384,128]{2,1,0:T(8,128)(2,1)S(1)}, u32[]{:S(2)}, u32[]{:S(2)}) async-start(bf16[8,384,128]{2,1,0:T(8,128)(2,1)} %shard_map.167), calls=%async_computation.1 | async-start | bytes 1572864 | tf_op jit(solution)/shard_map/all_to_all | solution.py:689
  41.9 1.4 copy-start.10
  66.7 15.0 %all-to-all-start.2 = ((bf16[8,160,128]{2,1,0:T(8,128)(2,1)}), bf16[8,160,128]{2,1,0:T(8,128)(2,1)S(1)}, u32[]{:S(2)}, u32[]{:S(2)}) async-start(bf16[8,160,128]{2,1,0:T(8,128)(2,1)} %shard_map.169), calls=%async_computation.2 | async-start | bytes 655360 | tf_op jit(solution)/shard_map/all_to_all | solution.py:696
  72.3 9.3 %copy-start.2 = (bf16[512,2048]{1,0:T(8,128)(2,1)S(1)}, bf16[512,2048]{1,0:T(8,128)(2,1)}, u32[]{:S(2)}) copy-start(bf16[512,2048]{1,0:T(8,128)(2,1)} %w_out.1) | copy-start | bytes 6291460
  84.2 1.9 %collective-permute-start = (bf16[66,2048]{1,0:T(8,128)(2,1)}, bf16[66,2048]{1,0:T(8,128)(2,1)S(1)}, u32[]{:S(2)}, u32[]{:S(2)}) collective-permute-start(bf16[66,2048]{1,0:T(8,128)(2,1)} %get-tuple-element.70), channel_id=1, source_target_pairs={{0,1},{1,0},{2,3},{3,2},{4,5},{5,4},{6,7},{7,6},{8,9},{9,8},{10,11... | collective-permute-start | bytes 811016 | tf_op jit(solution)/shard_map/ppermute | solution.py:708
  84.2 11.0 %collective-permute-start.2 = (bf16[66,2048]{1,0:T(8,128)(2,1)S(1)}, bf16[66,2048]{1,0:T(8,128)(2,1)S(1)}, u32[]{:S(2)}, u32[]{:S(2)}) collective-permute-start(bf16[66,2048]{1,0:T(8,128)(2,1)S(1)} %get-tuple-element.73), channel_id=1, source_target_pairs={{0,1},{1,0},{2,3},{3,2},{4,5},{5,4},{6,7},{7,6},{8,9},{9,8},{10,11... | collective-permute-start | bytes 811016 | tf_op jit(solution)/shard_map/ppermute | solution.py:710
  86.1 9.1 %collective-permute-start.1 = (bf16[66,2048]{1,0:T(8,128)(2,1)S(1)}, bf16[66,2048]{1,0:T(8,128)(2,1)S(1)}, u32[]{:S(2)}, u32[]{:S(2)}) collective-permute-start(bf16[66,2048]{1,0:T(8,128)(2,1)S(1)} %add_convert_fusion), channel_id=1, source_target_pairs={{0,2},{1,3},{2,0},{3,1},{4,6},{5,7},{6,4},{7,5},{8,10},{9,11},{10,... | collective-permute-start | bytes 811016 | tf_op jit(solution)/shard_map/ppermute | solution.py:709
  89.4 2.5 %copy-start.1 = (bf16[2048,2,640]{2,0,1:T(8,128)(2,1)S(1)}, bf16[2048,2,640]{2,0,1:T(8,128)(2,1)}, u32[]{:S(2)}) copy-start(bf16[2048,2,640]{2,0,1:T(8,128)(2,1)} %copy.20) | copy-start | bytes 15728644
  91.9 3.3 %copy-start.4 = (f32[2048]{0:T(1024)S(1)}, f32[2048]{0:T(1024)}, u32[]{:S(2)}) copy-start(f32[2048]{0:T(1024)} %param.21) | copy-start | bytes 24580
  91.9 15.6 %copy-start = (bf16[640,2048]{1,0:T(8,128)(2,1)S(1)}, bf16[640,2048]{1,0:T(8,128)(2,1)}, u32[]{:S(2)}) copy-start(bf16[640,2048]{1,0:T(8,128)(2,1)} %refs_3_.3) | copy-start | bytes 7864324
  95.5 6.8 %collective-permute-start.3 = (bf16[66,1024]{1,0:T(8,128)(2,1)S(1)}, bf16[66,1024]{1,0:T(8,128)(2,1)S(1)}, u32[]{:S(2)}, u32[]{:S(2)}) collective-permute-start(bf16[66,1024]{1,0:T(8,128)(2,1)S(1)} %get-tuple-element.98.refs_0_), channel_id=1, source_target_pairs={{0,8},{8,16},{16,24},{24,28},{28,20},{20,12},{12,4},{4,0},{1,9},{9... | collective-permute-start | bytes 405512 | tf_op jit(solution)/shard_map/ppermute | solution.py:719
  96.6 6.8 %collective-permute-start.5 = (bf16[66,1024]{1,0:T(8,128)(2,1)S(1)}, bf16[66,1024]{1,0:T(8,128)(2,1)S(1)}, u32[]{:S(2)}, u32[]{:S(2)}) collective-permute-start(bf16[66,1024]{1,0:T(8,128)(2,1)S(1)} %get-tuple-element.99.refs_1_), channel_id=1, source_target_pairs={{8,0},{16,8},{24,16},{28,24},{20,28},{12,20},{4,12},{0,4},{9,1},{1... | collective-permute-start | bytes 405512 | tf_op jit(solution)/shard_map/ppermute | solution.py:720
  97.6 7.9 %collective-permute-start.7 = (bf16[66,1024]{1,0:T(8,128)(2,1)S(1)}, bf16[66,1024]{1,0:T(8,128)(2,1)S(1)}, u32[]{:S(2)}, u32[]{:S(2)}) collective-permute-start(bf16[66,1024]{1,0:T(8,128)(2,1)S(1)} %get-tuple-element.99.refs_1_), channel_id=1, source_target_pairs={{0,8},{8,16},{16,24},{24,28},{28,20},{20,12},{12,4},{4,0},{1,9},{9... | collective-permute-start | bytes 405512 | tf_op jit(solution)/shard_map/ppermute | solution.py:723
  98.6 7.9 %collective-permute-start.8 = (bf16[66,1024]{1,0:T(8,128)(2,1)S(1)}, bf16[66,1024]{1,0:T(8,128)(2,1)S(1)}, u32[]{:S(2)}, u32[]{:S(2)}) collective-permute-start(bf16[66,1024]{1,0:T(8,128)(2,1)S(1)} %get-tuple-element.98.refs_0_), channel_id=1, source_target_pairs={{8,0},{16,8},{24,16},{28,24},{20,28},{12,20},{4,12},{0,4},{9,1},{1... | collective-permute-start | bytes 405512 | tf_op jit(solution)/shard_map/ppermute | solution.py:722
  102.3 7.0 %collective-permute-start.4 = (bf16[66,1024]{1,0:T(8,128)(2,1)S(1)}, bf16[66,1024]{1,0:T(8,128)(2,1)S(1)}, u32[]{:S(2)}, u32[]{:S(2)}) collective-permute-start(bf16[66,1024]{1,0:T(8,128)(2,1)S(1)} %collective-permute-done.3.refs_0_), channel_id=1, source_target_pairs={{0,8},{8,16},{16,24},{24,28},{28,20},{20,12},{12,4},{4,0},{1,9},{9... | collective-permute-start | bytes 405512 | tf_op jit(solution)/shard_map/ppermute | solution.py:719
  103.4 6.7 %collective-permute-start.6 = (bf16[66,1024]{1,0:T(8,128)(2,1)S(1)}, bf16[66,1024]{1,0:T(8,128)(2,1)S(1)}, u32[]{:S(2)}, u32[]{:S(2)}) collective-permute-start(bf16[66,1024]{1,0:T(8,128)(2,1)S(1)} %collective-permute-done.5.refs_3_), channel_id=1, source_target_pairs={{8,0},{16,8},{24,16},{28,24},{20,28},{12,20},{4,12},{0,4},{9,1},{1... | collective-permute-start | bytes 405512 | tf_op jit(solution)/shard_map/ppermute | solution.py:720
  105.5 6.6 %collective-permute-start.11 = (bf16[66,1024]{1,0:T(8,128)(2,1)S(1)}, bf16[66,1024]{1,0:T(8,128)(2,1)S(1)}, u32[]{:S(2)}, u32[]{:S(2)}) collective-permute-start(bf16[66,1024]{1,0:T(8,128)(2,1)S(1)} %collective-permute-done.7.refs_1_), channel_id=1, source_target_pairs={{0,8},{8,16},{16,24},{24,28},{28,20},{20,12},{12,4},{4,0},{1,9},{9... | collective-permute-start | bytes 405512 | tf_op jit(solution)/shard_map/ppermute | solution.py:723
  106.5 6.8 %collective-permute-start.12 = (bf16[66,1024]{1,0:T(8,128)(2,1)S(1)}, bf16[66,1024]{1,0:T(8,128)(2,1)S(1)}, u32[]{:S(2)}, u32[]{:S(2)}) collective-permute-start(bf16[66,1024]{1,0:T(8,128)(2,1)S(1)} %collective-permute-done.8.refs_2_), channel_id=1, source_target_pairs={{8,0},{16,8},{24,16},{28,24},{20,28},{12,20},{4,12},{0,4},{9,1},{1... | collective-permute-start | bytes 405512 | tf_op jit(solution)/shard_map/ppermute | solution.py:722
  110.1 6.1 %collective-permute-start.10 = (bf16[66,1024]{1,0:T(8,128)(2,1)S(1)}, bf16[66,1024]{1,0:T(8,128)(2,1)S(1)}, u32[]{:S(2)}, u32[]{:S(2)}) collective-permute-start(bf16[66,1024]{1,0:T(8,128)(2,1)S(1)} %collective-permute-done.6.refs_3_), channel_id=1, source_target_pairs={{8,0},{16,8},{24,16},{28,24},{20,28},{12,20},{4,12},{0,4},{9,1},{1... | collective-permute-start | bytes 405512 | tf_op jit(solution)/shard_map/ppermute | solution.py:720
  110.9 6.4 %collective-permute-start.9 = (bf16[66,1024]{1,0:T(8,128)(2,1)S(1)}, bf16[66,1024]{1,0:T(8,128)(2,1)S(1)}, u32[]{:S(2)}, u32[]{:S(2)}) collective-permute-start(bf16[66,1024]{1,0:T(8,128)(2,1)S(1)} %collective-permute-done.4.refs_0_), channel_id=1, source_target_pairs={{0,8},{8,16},{16,24},{24,28},{28,20},{20,12},{12,4},{4,0},{1,9},{9... | collective-permute-start | bytes 405512 | tf_op jit(solution)/shard_map/ppermute | solution.py:719
  112.1 7.2 %collective-permute-start.15 = (bf16[66,1024]{1,0:T(8,128)(2,1)S(1)}, bf16[66,1024]{1,0:T(8,128)(2,1)S(1)}, u32[]{:S(2)}, u32[]{:S(2)}) collective-permute-start(bf16[66,1024]{1,0:T(8,128)(2,1)S(1)} %collective-permute-done.11.refs_1_), channel_id=1, source_target_pairs={{0,8},{8,16},{16,24},{24,28},{28,20},{20,12},{12,4},{4,0},{1,9},{9... | collective-permute-start | bytes 405512 | tf_op jit(solution)/shard_map/ppermute | solution.py:723
  113.3 6.0 %collective-permute-start.16 = (bf16[66,1024]{1,0:T(8,128)(2,1)S(1)}, bf16[66,1024]{1,0:T(8,128)(2,1)S(1)}, u32[]{:S(2)}, u32[]{:S(2)}) collective-permute-start(bf16[66,1024]{1,0:T(8,128)(2,1)S(1)} %collective-permute-done.12.refs_2_), channel_id=1, source_target_pairs={{8,0},{16,8},{24,16},{28,24},{20,28},{12,20},{4,12},{0,4},{9,1},{1... | collective-permute-start | bytes 405512 | tf_op jit(solution)/shard_map/ppermute | solution.py:722
  117.3 5.1 %collective-permute-start.13 = (bf16[66,1024]{1,0:T(8,128)(2,1)S(1)}, bf16[66,1024]{1,0:T(8,128)(2,1)S(1)}, u32[]{:S(2)}, u32[]{:S(2)}) collective-permute-start(bf16[66,1024]{1,0:T(8,128)(2,1)S(1)} %collective-permute-done.9.refs_0_), channel_id=1, source_target_pairs={{0,8},{8,16},{16,24},{24,28},{28,20},{20,12},{12,4},{4,0},{1,9},{9... | collective-permute-start | bytes 405512 | tf_op jit(solution)/shard_map/ppermute | solution.py:719
  118.6 6.4 %collective-permute-start.14 = (bf16[66,1024]{1,0:T(8,128)(2,1)S(1)}, bf16[66,1024]{1,0:T(8,128)(2,1)S(1)}, u32[]{:S(2)}, u32[]{:S(2)}) collective-permute-start(bf16[66,1024]{1,0:T(8,128)(2,1)S(1)} %collective-permute-done.10.refs_3_), channel_id=1, source_target_pairs={{8,0},{16,8},{24,16},{28,24},{20,28},{12,20},{4,12},{0,4},{9,1},{1... | collective-permute-start | bytes 405512 | tf_op jit(solution)/shard_map/ppermute | solution.py:720
  126.7 6.7 %collective-permute-start.27 = (bf16[66,1024]{1,0:T(8,128)(2,1)S(1)}, bf16[66,1024]{1,0:T(8,128)(2,1)S(1)}, u32[]{:S(2)}, u32[]{:S(2)}) collective-permute-start(bf16[66,1024]{1,0:T(8,128)(2,1)S(1)} %get-tuple-element.115), channel_id=1, source_target_pairs={{8,0},{16,8},{24,16},{28,24},{20,28},{12,20},{4,12},{0,4},{9,1},{1... | collective-permute-start | bytes 405512 | tf_op jit(solution)/shard_map/ppermute | solution.py:735
  127.0 6.8 %collective-permute-start.24 = (bf16[66,1024]{1,0:T(8,128)(2,1)S(1)}, bf16[66,1024]{1,0:T(8,128)(2,1)S(1)}, u32[]{:S(2)}, u32[]{:S(2)}) collective-permute-start(bf16[66,1024]{1,0:T(8,128)(2,1)S(1)} %get-tuple-element.111), channel_id=1, source_target_pairs={{0,8},{8,16},{16,24},{24,28},{28,20},{20,12},{12,4},{4,0},{1,9},{9... | collective-permute-start | bytes 405512 | tf_op jit(solution)/shard_map/ppermute | solution.py:735
  128.8 8.0 %collective-permute-start.20 = (bf16[66,1024]{1,0:T(8,128)(2,1)S(1)}, bf16[66,1024]{1,0:T(8,128)(2,1)S(1)}, u32[]{:S(2)}, u32[]{:S(2)}) collective-permute-start(bf16[66,1024]{1,0:T(8,128)(2,1)S(1)} %get-tuple-element.108), channel_id=1, source_target_pairs={{0,8},{8,16},{16,24},{24,28},{28,20},{20,12},{12,4},{4,0},{1,9},{9... | collective-permute-start | bytes 405512 | tf_op jit(solution)/shard_map/ppermute | solution.py:735
  128.8 9.1 %collective-permute-start.17 = (bf16[66,1024]{1,0:T(8,128)(2,1)S(1)}, bf16[66,1024]{1,0:T(8,128)(2,1)S(1)}, u32[]{:S(2)}, u32[]{:S(2)}) collective-permute-start(bf16[66,1024]{1,0:T(8,128)(2,1)S(1)} %get-tuple-element.104), channel_id=1, source_target_pairs={{8,0},{16,8},{24,16},{28,24},{20,28},{12,20},{4,12},{0,4},{9,1},{1... | collective-permute-start | bytes 405512 | tf_op jit(solution)/shard_map/ppermute | solution.py:735
  133.5 6.6 %collective-permute-start.28 = (bf16[66,1024]{1,0:T(8,128)(2,1)S(1)}, bf16[66,1024]{1,0:T(8,128)(2,1)S(1)}, u32[]{:S(2)}, u32[]{:S(2)}) collective-permute-start(bf16[66,1024]{1,0:T(8,128)(2,1)S(1)} %add_convert_fusion.3), channel_id=1, source_target_pairs={{8,0},{16,8},{24,16},{28,24},{20,28},{12,20},{4,12},{0,4},{9,1},{1... | collective-permute-start | bytes 405512 | tf_op jit(solution)/shard_map/ppermute | solution.py:735
  133.9 7.0 %collective-permute-start.25 = (bf16[66,1024]{1,0:T(8,128)(2,1)S(1)}, bf16[66,1024]{1,0:T(8,128)(2,1)S(1)}, u32[]{:S(2)}, u32[]{:S(2)}) collective-permute-start(bf16[66,1024]{1,0:T(8,128)(2,1)S(1)} %add_convert_fusion.5), channel_id=1, source_target_pairs={{0,8},{8,16},{16,24},{24,28},{28,20},{20,12},{12,4},{4,0},{1,9},{9... | collective-permute-start | bytes 405512 | tf_op jit(solution)/shard_map/ppermute | solution.py:735
  136.8 6.3 %collective-permute-start.21 = (bf16[66,1024]{1,0:T(8,128)(2,1)S(1)}, bf16[66,1024]{1,0:T(8,128)(2,1)S(1)}, u32[]{:S(2)}, u32[]{:S(2)}) collective-permute-start(bf16[66,1024]{1,0:T(8,128)(2,1)S(1)} %add_convert_fusion.8), channel_id=1, source_target_pairs={{0,8},{8,16},{16,24},{24,28},{28,20},{20,12},{12,4},{4,0},{1,9},{9... | collective-permute-start | bytes 405512 | tf_op jit(solution)/shard_map/ppermute | solution.py:735
  138.0 6.4 %collective-permute-start.18 = (bf16[66,1024]{1,0:T(8,128)(2,1)S(1)}, bf16[66,1024]{1,0:T(8,128)(2,1)S(1)}, u32[]{:S(2)}, u32[]{:S(2)}) collective-permute-start(bf16[66,1024]{1,0:T(8,128)(2,1)S(1)} %add_convert_fusion.10), channel_id=1, source_target_pairs={{8,0},{16,8},{24,16},{28,24},{20,28},{12,20},{4,12},{0,4},{9,1},{1... | collective-permute-start | bytes 405512 | tf_op jit(solution)/shard_map/ppermute | solution.py:735
  140.2 5.2 %collective-permute-start.29 = (bf16[66,1024]{1,0:T(8,128)(2,1)S(1)}, bf16[66,1024]{1,0:T(8,128)(2,1)S(1)}, u32[]{:S(2)}, u32[]{:S(2)}) collective-permute-start(bf16[66,1024]{1,0:T(8,128)(2,1)S(1)} %add_convert_fusion.2), channel_id=1, source_target_pairs={{8,0},{16,8},{24,16},{28,24},{20,28},{12,20},{4,12},{0,4},{9,1},{1... | collective-permute-start | bytes 405512 | tf_op jit(solution)/shard_map/ppermute | solution.py:735
  140.9 10.5 %collective-permute-start.26 = (bf16[66,1024]{1,0:T(8,128)(2,1)S(1)}, bf16[66,1024]{1,0:T(8,128)(2,1)S(1)}, u32[]{:S(2)}, u32[]{:S(2)}) collective-permute-start(bf16[66,1024]{1,0:T(8,128)(2,1)S(1)} %add_convert_fusion.4), channel_id=1, source_target_pairs={{0,8},{8,16},{16,24},{24,28},{28,20},{20,12},{12,4},{4,0},{1,9},{9... | collective-permute-start | bytes 405512 | tf_op jit(solution)/shard_map/ppermute | solution.py:736
  143.2 5.2 %collective-permute-start.22 = (bf16[66,1024]{1,0:T(8,128)(2,1)S(1)}, bf16[66,1024]{1,0:T(8,128)(2,1)S(1)}, u32[]{:S(2)}, u32[]{:S(2)}) collective-permute-start(bf16[66,1024]{1,0:T(8,128)(2,1)S(1)} %add_convert_fusion.7), channel_id=1, source_target_pairs={{0,8},{8,16},{16,24},{24,28},{28,20},{20,12},{12,4},{4,0},{1,9},{9... | collective-permute-start | bytes 405512 | tf_op jit(solution)/shard_map/ppermute | solution.py:735
  144.4 6.9 %collective-permute-start.19 = (bf16[66,1024]{1,0:T(8,128)(2,1)S(1)}, bf16[66,1024]{1,0:T(8,128)(2,1)S(1)}, u32[]{:S(2)}, u32[]{:S(2)}) collective-permute-start(bf16[66,1024]{1,0:T(8,128)(2,1)S(1)} %add_convert_fusion.9), channel_id=1, source_target_pairs={{8,0},{16,8},{24,16},{28,24},{20,28},{12,20},{4,12},{0,4},{9,1},{1... | collective-permute-start | bytes 405512 | tf_op jit(solution)/shard_map/ppermute | solution.py:736
  145.4 5.9 %collective-permute-start.30 = (bf16[66,1024]{1,0:T(8,128)(2,1)S(1)}, bf16[66,1024]{1,0:T(8,128)(2,1)S(1)}, u32[]{:S(2)}, u32[]{:S(2)}) collective-permute-start(bf16[66,1024]{1,0:T(8,128)(2,1)S(1)} %add_convert_fusion.1), channel_id=1, source_target_pairs={{8,0},{16,8},{24,16},{28,24},{20,28},{12,20},{4,12},{0,4},{9,1},{1... | collective-permute-start | bytes 405512 | tf_op jit(solution)/shard_map/ppermute | solution.py:736
  148.5 5.2 %collective-permute-start.23 = (bf16[66,1024]{1,0:T(8,128)(2,1)S(1)}, bf16[66,1024]{1,0:T(8,128)(2,1)S(1)}, u32[]{:S(2)}, u32[]{:S(2)}) collective-permute-start(bf16[66,1024]{1,0:T(8,128)(2,1)S(1)} %add_convert_fusion.6), channel_id=1, source_target_pairs={{0,8},{8,16},{16,24},{24,28},{28,20},{20,12},{12,4},{4,0},{1,9},{9... | collective-permute-start | bytes 405512 | tf_op jit(solution)/shard_map/ppermute | solution.py:736

commit v6 on v5

--- a/solution.py
+++ b/solution.py
@@ -685,7 +685,7 @@
     copies = jnp.broadcast_to(decode_states[None], (n_tok, hosted, width))
     rows = lax.all_to_all(copies, "tok", split_axis=0, concat_axis=0, tiled=True).reshape(n_tok * hosted, width)
     messages = qkv_messages(prefill_home, prefill_states.reshape(requests * positions, width), gain, w_three, requests)
-    messages, rows = lax.optimization_barrier((messages, rows))
+    messages, rows, ids = lax.optimization_barrier((messages, rows, ids))
     arrived = lax.all_to_all(messages, "tok", split_axis=0, concat_axis=0, tiled=True)
     decoded, old_keys, old_values = decode_attention(
         decode_lengths, decode_home, ids, decode_pages, prefill_lengths, prefill_home, prefill_pages.reshape(-1),
@@ -723,7 +723,8 @@
             up_right = lax.ppermute(up_right, "tok", ahead)
         if waiting is not None:
             done = feed_forward(waiting, gate_up, w_down)
-            up_left, down_right, done = lax.optimization_barrier((up_left, down_right, done))
+            if k < far:
+                up_left, down_right, done = lax.optimization_barrier((up_left, down_right, done))
             minus[k - 1], plus[k - 1] = done[:2], done[2:]
         waiting = [(up_left, up_right), (down_left, down_right)]
     farthest = feed_forward([(up_left, down_right)], gate_up, w_down)
@@ -735,12 +736,11 @@
             part = joined(table[k][side], lax.ppermute(part, "tok", steps))
         return lax.ppermute(part, "tok", steps)
 
-    sums = [
-        chain(minus[near][0], minus, 0, near - 1, behind),
-        chain(farthest[0], plus, 0, far - 1, ahead),
-        chain(plus[near][1], plus, 1, near - 1, ahead),
-        chain(farthest[1], minus, 1, far - 1, behind),
-    ]
+    near_left = chain(minus[near][0], minus, 0, near - 1, behind)
+    near_right = chain(plus[near][1], plus, 1, near - 1, ahead)
+    far_left = chain(farthest[0], plus, 0, far - 1, ahead)
+    far_right = chain(farthest[1], minus, 1, far - 1, behind)
+    sums = [near_left, far_left, near_right, far_right]
     pre, dec = finish(resid, own_part, sums, requests * block_rows)
     return (pre.reshape(requests, block_rows, width), dec)
 

time: 155 us -> 154 us (level)
  starting transfers between devices: 48.6 us -> 45.4 us
    ppermute x10, waiting for transfers between devices: 6.8 us -> 10.1 us  [chain(): part = joined(table[k][side], lax.ppermute(part, 'tok', steps))]
    ppermute x10, starting transfers between devices: 10.2 us -> 8.48 us  [chain(): part = joined(table[k][side], lax.ppermute(part, 'tok', steps))]
    ppermute x4, starting transfers between devices: 5.43 us -> 3.84 us  [chain(): return lax.ppermute(part, 'tok', steps)]
  transfers between devices with their start and end apart: 34 -> 34, of which waited for: 18 -> 21; matrix products, arithmetic and copies ran while one was open for 5% -> 5% of each run, Pallas kernels for 20% -> 22%
where the time goes in v6:
time: 154 us; the launch traced here: 153 us
  Pallas kernels  61.1 us (40%)
  starting transfers between devices  45.4 us (29%)
  waiting for transfers between devices  31.8 us (21%)
  local copies, waits for them, and re-layouts  12.8 us (8%)
  between operations  1.6 us (1%)
    pallas_call x1, Pallas kernels, prefill_attention(): pl.pallas_call(functools.partial(prefill_kernel, positions), out_shape=ja...  23.4 us
    pallas_call x1, Pallas kernels, decode_attention(): pl.pallas_call(functools.partial(decode_kernel, heads), out_shape=[jax.Sh...  19 us
    ppermute x10, waiting for transfers between devices, chain(): part = joined(table[k][side], lax.ppermute(part, 'tok', steps))  10.1 us
    pallas_call x5, Pallas kernels, feed_forward(): pl.pallas_call(functools.partial(feed_kernel, [len(chunk) for chunk in ch...  8.93 us
    ppermute x10, starting transfers between devices, chain(): part = joined(table[k][side], lax.ppermute(part, 'tok', steps))  8.48 us
    all_to_all x1, starting transfers between devices, shards(): lax.all_to_all(copies, 'tok', split_axis=0, concat_axis=0, tiled=True)  7.28 us
    pallas_call x1, Pallas kernels, qkv_messages(): pl.pallas_call(functools.partial(qkv_kernel, requests, heads), out_shape=...  5.89 us
    all_to_all x1, starting transfers between devices, shards(): lax.all_to_all(attn, 'tok', split_axis=0, concat_axis=0, tiled=True)  5.81 us
  transfers between devices with their start and end apart: 34, of which 21 were waited for; matrix products, arithmetic and copies ran while one was open for 5% of the time, Pallas kernels for 22%

profile of v6, /device:TPU:0, one launch (start us, length us, event | category | flops | bytes accessed | tf_op | source)
XLA Modules:
  0.0 153.2 jit_solution(15894524721373442711)
XLA Ops:
  0.7 1.5 broadcast_in_dim.2
  2.2 7.3 %all-to-all-start = ((bf16[8,8,2048]{2,1,0:T(8,128)(2,1)}), bf16[8,8,2048]{2,1,0:T(8,128)(2,1)S(1)}, u32[]{:S(2)}, u32[]{:S(2)}) async-start(bf16[8,8,2048]{2,1,0:T(8,128)(2,1)} %broadcast_in_dim.2), calls=%async_computation | async-start | bytes 524288 | tf_op jit(solution)/shard_map/all_to_all | solution.py:686
  9.6 5.9 %shard_map.167 = bf16[8,384,128]{2,1,0:T(8,128)(2,1)} custom-call(s32[8]{0:T(128)} %home.7, f32[1,2048]{1,0:T(1,128)} %bitcast.16, bf16[256,2048]{1,0:T(8,128)(2,1)} %bitcast.22, bf16[3,2048,512]{2,1,0:T(8,128)(2,1)} %bitcast.20), custom_call_target="tpu_custom_call" | custom-call | flops 1610612736 | bytes 10485760 | tf_op jit(solution)/shard_map/pallas_call | solution.py:429
  15.5 2.9 %all-to-all-done = bf16[8,8,2048]{2,1,0:T(8,128)(2,1)S(1)} async-done(((bf16[8,8,2048]{2,1,0:T(8,128)(2,1)}), bf16[8,8,2048]{2,1,0:T(8,128)(2,1)S(1)}, u32[]{:S(2)}, u32[]{:S(2)}) %all-to-all-start) | async-done | bytes 262176 | tf_op jit(solution)/shard_map/all_to_all | solution.py:686
  18.4 3.6 %all-to-all-start.1 = ((bf16[8,384,128]{2,1,0:T(8,128)(2,1)}), bf16[8,384,128]{2,1,0:T(8,128)(2,1)S(1)}, u32[]{:S(2)}, u32[]{:S(2)}) async-start(bf16[8,384,128]{2,1,0:T(8,128)(2,1)} %shard_map.167), calls=%async_computation.1 | async-start | bytes 1572864 | tf_op jit(solution)/shard_map/all_to_all | solution.py:689
  22.7 19.0 %shard_map.168 = (f32[8,512]{1,0:T(8,128)S(1)}, bf16[6,128,1024]{2,1,0:T(8,128)(2,1)S(1)}, bf16[6,1024,128]{2,1,0:T(8,128)(2,1)}) custom-call(s32[8]{0:T(128)S(1)} %copy-done.8, s32[64]{0:T(128)S(1)} %copy-done.7, s32[2]{0:T(128)S(1)} %pad_add_fusion.ids, s32[8,32]{1,0:T(8,128)S(1)} %copy-done.6, s32[1]{0:T(128)S(6)} %copy.21.old_lengths.lengths, ...), custom_call_target="tpu_custom_call" | custom-call | flops 2000000000 | bytes 23068672 | tf_op jit(solution)/shard_map/pallas_call | solution.py:360
  41.9 1.4 copy-done.10
  43.3 23.4 %shard_map.169 = bf16[8,160,128]{2,1,0:T(8,128)(2,1)} custom-call(s32[1]{0:T(128)S(6)} %copy.21.old_lengths.lengths, s32[8]{0:T(128)S(1)} %copy-done.5, s32[2]{0:T(128)S(1)} %pad_add_fusion.ids, bf16[8,384,128]{2,1,0:T(8,128)(2,1)S(1)} %all-to-all-done.1.msg, bf16[6,128,1024]{2,1,0:T(8,128)(2,1)S(1)} %get-tuple-element.58.flipped_in, ...), custom_call_target="tpu_custom_call" | custom-call | flops 4294967296 | bytes 4194304 | tf_op jit(solution)/shard_map/pallas_call | solution.py:203
  66.7 5.8 %all-to-all-start.2 = ((bf16[8,160,128]{2,1,0:T(8,128)(2,1)}), bf16[8,160,128]{2,1,0:T(8,128)(2,1)S(1)}, u32[]{:S(2)}, u32[]{:S(2)}) async-start(bf16[8,160,128]{2,1,0:T(8,128)(2,1)} %shard_map.169), calls=%async_computation.2 | async-start | bytes 655360 | tf_op jit(solution)/shard_map/all_to_all | solution.py:696
  72.5 5.6 %copy.20 = bf16[2048,2,640]{2,0,1:T(8,128)(2,1)} copy(bf16[2048,2,640]{2,1,0:T(2,128)(2,1)} %param.22) | data formatting | bytes 10485760 | tf_op jit(solution)/shard_map/optimization_barrier | solution.py:695
  78.1 3.7 %all-to-all-done.2.received = bf16[8,160,128]{2,1,0:T(8,128)(2,1)S(1)} async-done(((bf16[8,160,128]{2,1,0:T(8,128)(2,1)}), bf16[8,160,128]{2,1,0:T(8,128)(2,1)S(1)}, u32[]{:S(2)}, u32[]{:S(2)}) %all-to-all-start.2) | async-done | bytes 327712 | tf_op jit(solution)/shard_map/all_to_all | solution.py:696
  81.8 2.5 %shard_map.170 = (bf16[66,2048]{1,0:T(8,128)(2,1)S(1)}, bf16[66,2048]{1,0:T(8,128)(2,1)S(1)}, bf16[66,2048]{1,0:T(8,128)(2,1)S(1)}, bf16[66,2048]{1,0:T(8,128)(2,1)}) custom-call(s32[8]{0:T(128)S(1)} %copy-done.5, s32[64]{0:T(128)S(1)} %copy-done.7, s32[2]{0:T(128)S(1)} %pad_add_fusion.ids, bf16[8,160,128]{2,1,0:T(8,128)(2,1)S(1)} %all-to-all-done.2.received, ...), custom_call_target="tpu_custom_call" | custom-call | flops 553648128 | bytes 4194304 | tf_op jit(solution)/shard_map/pallas_call | solution.py:497
  84.9 1.3 collective-permute-done
  86.3 1.6 %collective-permute-start.1 = (bf16[66,2048]{1,0:T(8,128)(2,1)S(1)}, bf16[66,2048]{1,0:T(8,128)(2,1)S(1)}, u32[]{:S(2)}, u32[]{:S(2)}) collective-permute-start(bf16[66,2048]{1,0:T(8,128)(2,1)S(1)} %add_convert_fusion), channel_id=1, source_target_pairs={{0,2},{1,3},{2,0},{3,1},{4,6},{5,7},{6,4},{7,5},{8,10},{9,11},{10,... | collective-permute-start | bytes 811016 | tf_op jit(solution)/shard_map/ppermute | solution.py:709
  89.6 2.5 %copy-done.1 = bf16[2048,2,640]{2,0,1:T(8,128)(2,1)S(1)} copy-done((bf16[2048,2,640]{2,0,1:T(8,128)(2,1)S(1)}, bf16[2048,2,640]{2,0,1:T(8,128)(2,1)}, u32[]{:S(2)}) %copy-start.1) | copy-done | bytes 5242904
  92.4 3.0 %collective-permute-done.1.rest_1_ = bf16[66,2048]{1,0:T(8,128)(2,1)S(1)} collective-permute-done((bf16[66,2048]{1,0:T(8,128)(2,1)S(1)}, bf16[66,2048]{1,0:T(8,128)(2,1)S(1)}, u32[]{:S(2)}, u32[]{:S(2)}) %collective-permute-start.1) | collective-permute-done | bytes 270368 | tf_op jit(solution)/shard_map/ppermute | solution.py:709
  95.7 1.1 collective-permute-start.3
  96.8 1.0 collective-permute-start.5
  97.8 1.0 collective-permute-start.7
  98.8 1.0 collective-permute-start.8
  99.8 2.7 %collective-permute-done.3.refs_0_ = bf16[66,1024]{1,0:T(8,128)(2,1)S(1)} collective-permute-done((bf16[66,1024]{1,0:T(8,128)(2,1)S(1)}, bf16[66,1024]{1,0:T(8,128)(2,1)S(1)}, u32[]{:S(2)}, u32[]{:S(2)}) %collective-permute-start.3) | collective-permute-done | bytes 135200 | tf_op jit(solution)/shard_map/ppermute | solution.py:719
  102.5 1.0 collective-permute-start.4
  103.6 1.0 collective-permute-start.6
  104.6 1.1 collective-permute-done.7.refs_1_
  105.7 1.0 collective-permute-start.11
  106.7 1.0 collective-permute-start.12
  107.7 1.8 %shard_map.173 = (bf16[66,1024]{1,0:T(8,128)(2,1)S(1)}, bf16[66,1024]{1,0:T(8,128)(2,1)S(1)}, bf16[66,1024]{1,0:T(8,128)(2,1)S(1)}, bf16[66,1024]{1,0:T(8,128)(2,1)S(1)}) custom-call(bf16[66,1024]{1,0:T(8,128)(2,1)S(1)} %collective-permute-done.3.refs_0_, bf16[66,1024]{1,0:T(8,128)(2,1)S(1)} %collective-permute-done.7.refs_1_, ...), custom_call_target="tpu_custom_call" | custom-call | flops 1038090240 | bytes 8388608 | tf_op jit(solution)/shard_map/pallas_call | solution.py:627
  111.1 1.2 collective-permute-start.9
  112.3 1.1 collective-permute-start.15
  114.5 1.8 %shard_map.174 = (bf16[66,1024]{1,0:T(8,128)(2,1)S(1)}, bf16[66,1024]{1,0:T(8,128)(2,1)S(1)}, bf16[66,1024]{1,0:T(8,128)(2,1)S(1)}, bf16[66,1024]{1,0:T(8,128)(2,1)S(1)}) custom-call(bf16[66,1024]{1,0:T(8,128)(2,1)S(1)} %collective-permute-done.4.refs_0_, bf16[66,1024]{1,0:T(8,128)(2,1)S(1)} %collective-permute-done.11.refs_1_, ...), custom_call_target="tpu_custom_call" | custom-call | flops 1038090240 | bytes 8388608 | tf_op jit(solution)/shard_map/pallas_call | solution.py:627
  116.4 1.1 collective-permute-done.9.refs_0_
  117.5 1.3 collective-permute-start.13
  119.7 1.8 %shard_map.177 = (bf16[66,1024]{1,0:T(8,128)(2,1)S(1)}, bf16[66,1024]{1,0:T(8,128)(2,1)S(1)}, bf16[66,1024]{1,0:T(8,128)(2,1)S(1)}, bf16[66,1024]{1,0:T(8,128)(2,1)S(1)}) custom-call(bf16[66,1024]{1,0:T(8,128)(2,1)S(1)} %collective-permute-done.9.refs_0_, bf16[66,1024]{1,0:T(8,128)(2,1)S(1)} %collective-permute-done.15.refs_1_, ...), custom_call_target="tpu_custom_call" | custom-call | flops 1038090240 | bytes 8388608 | tf_op jit(solution)/shard_map/pallas_call | solution.py:627
  121.5 1.8 %collective-permute-start.24 = (bf16[66,1024]{1,0:T(8,128)(2,1)S(1)}, bf16[66,1024]{1,0:T(8,128)(2,1)S(1)}, u32[]{:S(2)}, u32[]{:S(2)}) collective-permute-start(bf16[66,1024]{1,0:T(8,128)(2,1)S(1)} %get-tuple-element.101), channel_id=1, source_target_pairs={{0,8},{8,16},{16,24},{24,28},{28,20},{20,12},{12,4},{4,0},{1,9},{9... | collective-permute-start | bytes 405512 | tf_op jit(solution)/shard_map/ppermute | solution.py:736
  123.8 1.4 collective-permute-done.14.refs_1_
  125.2 1.7 %shard_map.175 = (bf16[66,1024]{1,0:T(8,128)(2,1)S(1)}, bf16[66,1024]{1,0:T(8,128)(2,1)S(1)}) custom-call(bf16[66,1024]{1,0:T(8,128)(2,1)S(1)} %collective-permute-done.13.refs_0_, bf16[66,1024]{1,0:T(8,128)(2,1)S(1)} %collective-permute-done.14.refs_1_, bf16[2,2048,640]{2,1,0:T(8,128)(2,1)S(1)} %shard_map.171.refs_4_.refs_2_, bf16[640,2048]{1,0:T(8,128)(2,1)S(1)} %copy-done), custom_call_target="tpu_custom_call" | custom-call | flops 519045120 | bytes 8388608 | tf_op jit(solution)/shard_map/pallas_call | solution.py:627
  128.5 1.1 collective-permute-start.25
  130.3 1.3 collective-permute-start.18
  133.0 1.8 %collective-permute-done.25 = bf16[66,1024]{1,0:T(8,128)(2,1)S(1)} collective-permute-done((bf16[66,1024]{1,0:T(8,128)(2,1)S(1)}, bf16[66,1024]{1,0:T(8,128)(2,1)S(1)}, u32[]{:S(2)}, u32[]{:S(2)}) %collective-permute-start.25) | collective-permute-done | bytes 135200 | tf_op jit(solution)/shard_map/ppermute | solution.py:736
  135.2 1.2 collective-permute-done.20
  136.9 1.7 %collective-permute-start.19 = (bf16[66,1024]{1,0:T(8,128)(2,1)S(1)}, bf16[66,1024]{1,0:T(8,128)(2,1)S(1)}, u32[]{:S(2)}, u32[]{:S(2)}) collective-permute-start(bf16[66,1024]{1,0:T(8,128)(2,1)S(1)} %add_convert_fusion.9), channel_id=1, source_target_pairs={{8,0},{16,8},{24,16},{28,24},{20,28},{12,20},{4,12},{0,4},{9,1},{1... | collective-permute-start | bytes 405512 | tf_op jit(solution)/shard_map/ppermute | solution.py:737
  138.6 1.3 collective-permute-start.29
  139.9 2.1 %collective-permute-done.21 = bf16[66,1024]{1,0:T(8,128)(2,1)S(1)} collective-permute-done((bf16[66,1024]{1,0:T(8,128)(2,1)S(1)}, bf16[66,1024]{1,0:T(8,128)(2,1)S(1)}, u32[]{:S(2)}, u32[]{:S(2)}) %collective-permute-start.21) | collective-permute-done | bytes 135200 | tf_op jit(solution)/shard_map/ppermute | solution.py:736
  142.3 1.7 %collective-permute-done.29 = bf16[66,1024]{1,0:T(8,128)(2,1)S(1)} collective-permute-done((bf16[66,1024]{1,0:T(8,128)(2,1)S(1)}, bf16[66,1024]{1,0:T(8,128)(2,1)S(1)}, u32[]{:S(2)}, u32[]{:S(2)}) %collective-permute-start.29) | collective-permute-done | bytes 135200 | tf_op jit(solution)/shard_map/ppermute | solution.py:736
  144.1 1.5 collective-permute-start.30
  145.6 1.6 %collective-permute-done.22 = bf16[66,1024]{1,0:T(8,128)(2,1)S(1)} collective-permute-done((bf16[66,1024]{1,0:T(8,128)(2,1)S(1)}, bf16[66,1024]{1,0:T(8,128)(2,1)S(1)}, u32[]{:S(2)}, u32[]{:S(2)}) %collective-permute-start.22) | collective-permute-done | bytes 135200 | tf_op jit(solution)/shard_map/ppermute | solution.py:736
  147.5 1.7 %shard_map.176 = (bf16[66,1024]{1,0:T(8,128)(2,1)S(1)}, bf16[66,1024]{1,0:T(8,128)(2,1)S(1)}) custom-call(bf16[66,1024]{1,0:T(8,128)(2,1)S(1)} %get-tuple-element.88.refs_0_, bf16[66,1024]{1,0:T(8,128)(2,1)S(1)} %get-tuple-element.89.refs_1_, bf16[2,2048,640]{2,1,0:T(8,128)(2,1)S(1)} %shard_map.171.refs_4_.refs_2_, bf16[640,2048]{1,0:T(8,128)(2,1)S(1)} %copy-done), custom_call_target="tpu_custom_call" | custom-call | flops 519045120 | bytes 8388608 | tf_op jit(solution)/shard_map/pallas_call | solution.py:627
  149.3 3.1 %collective-permute-done.23.rest_1_ = bf16[66,1024]{1,0:T(8,128)(2,1)S(1)} collective-permute-done((bf16[66,1024]{1,0:T(8,128)(2,1)S(1)}, bf16[66,1024]{1,0:T(8,128)(2,1)S(1)}, u32[]{:S(2)}, u32[]{:S(2)}) %collective-permute-start.23) | collective-permute-done | bytes 135200 | tf_op jit(solution)/shard_map/ppermute | solution.py:737
  (70 shorter events, 13.6 us)
Async XLA Ops:
  0.6 22.0 %copy-start.3 = (f32[2048]{0:T(1024)S(1)}, f32[2048]{0:T(1024)}, u32[]{:S(2)}) copy-start(f32[2048]{0:T(1024)} %param.18) | copy-start | bytes 24580
  0.6 22.0 %copy-start.5 = (s32[8]{0:T(128)S(1)}, s32[8]{0:T(128)}, u32[]{:S(2)}) copy-start(s32[8]{0:T(128)} %home.7) | copy-start | bytes 100
  0.7 22.0 %copy-start.9 = (s32[1,48]{1,0:T(1,128)S(1)}, s32[1,48]{1,0:T(1,128)}, u32[]{:S(2)}) copy-start(s32[1,48]{1,0:T(1,128)} %param.25) | copy-start | bytes 580
  0.7 22.0 %copy-start.6 = (s32[8,32]{1,0:T(8,128)S(1)}, s32[8,32]{1,0:T(8,128)}, u32[]{:S(2)}) copy-start(s32[8,32]{1,0:T(8,128)} %pages.1) | copy-start | bytes 3076
  0.7 22.0 %copy-start.8 = (s32[8]{0:T(128)S(1)}, s32[8]{0:T(128)}, u32[]{:S(2)}) copy-start(s32[8]{0:T(128)} %lengths.2) | copy-start | bytes 100
  0.7 22.0 %copy-start.7 = (s32[64]{0:T(128)S(1)}, s32[64]{0:T(128)}, u32[]{:S(2)}) copy-start(s32[64]{0:T(128)} %slots_of.1) | copy-start | bytes 772
  2.2 16.2 %all-to-all-start = ((bf16[8,8,2048]{2,1,0:T(8,128)(2,1)}), bf16[8,8,2048]{2,1,0:T(8,128)(2,1)S(1)}, u32[]{:S(2)}, u32[]{:S(2)}) async-start(bf16[8,8,2048]{2,1,0:T(8,128)(2,1)} %broadcast_in_dim.2), calls=%async_computation | async-start | bytes 524288 | tf_op jit(solution)/shard_map/all_to_all | solution.py:686
  18.4 23.5 %all-to-all-start.1 = ((bf16[8,384,128]{2,1,0:T(8,128)(2,1)}), bf16[8,384,128]{2,1,0:T(8,128)(2,1)S(1)}, u32[]{:S(2)}, u32[]{:S(2)}) async-start(bf16[8,384,128]{2,1,0:T(8,128)(2,1)} %shard_map.167), calls=%async_computation.1 | async-start | bytes 1572864 | tf_op jit(solution)/shard_map/all_to_all | solution.py:689
  41.9 1.4 copy-start.10
  66.7 15.2 %all-to-all-start.2 = ((bf16[8,160,128]{2,1,0:T(8,128)(2,1)}), bf16[8,160,128]{2,1,0:T(8,128)(2,1)S(1)}, u32[]{:S(2)}, u32[]{:S(2)}) async-start(bf16[8,160,128]{2,1,0:T(8,128)(2,1)} %shard_map.169), calls=%async_computation.2 | async-start | bytes 655360 | tf_op jit(solution)/shard_map/all_to_all | solution.py:696
  72.5 9.4 %copy-start.2 = (bf16[512,2048]{1,0:T(8,128)(2,1)S(1)}, bf16[512,2048]{1,0:T(8,128)(2,1)}, u32[]{:S(2)}) copy-start(bf16[512,2048]{1,0:T(8,128)(2,1)} %w_out.1) | copy-start | bytes 6291460
  84.3 1.9 %collective-permute-start = (bf16[66,2048]{1,0:T(8,128)(2,1)}, bf16[66,2048]{1,0:T(8,128)(2,1)S(1)}, u32[]{:S(2)}, u32[]{:S(2)}) collective-permute-start(bf16[66,2048]{1,0:T(8,128)(2,1)} %get-tuple-element.66), channel_id=1, source_target_pairs={{0,1},{1,0},{2,3},{3,2},{4,5},{5,4},{6,7},{7,6},{8,9},{9,8},{10,11... | collective-permute-start | bytes 811016 | tf_op jit(solution)/shard_map/ppermute | solution.py:708
  84.4 11.0 %collective-permute-start.2 = (bf16[66,2048]{1,0:T(8,128)(2,1)S(1)}, bf16[66,2048]{1,0:T(8,128)(2,1)S(1)}, u32[]{:S(2)}, u32[]{:S(2)}) collective-permute-start(bf16[66,2048]{1,0:T(8,128)(2,1)S(1)} %get-tuple-element.69), channel_id=1, source_target_pairs={{0,1},{1,0},{2,3},{3,2},{4,5},{5,4},{6,7},{7,6},{8,9},{9,8},{10,11... | collective-permute-start | bytes 811016 | tf_op jit(solution)/shard_map/ppermute | solution.py:710
  86.3 9.1 %collective-permute-start.1 = (bf16[66,2048]{1,0:T(8,128)(2,1)S(1)}, bf16[66,2048]{1,0:T(8,128)(2,1)S(1)}, u32[]{:S(2)}, u32[]{:S(2)}) collective-permute-start(bf16[66,2048]{1,0:T(8,128)(2,1)S(1)} %add_convert_fusion), channel_id=1, source_target_pairs={{0,2},{1,3},{2,0},{3,1},{4,6},{5,7},{6,4},{7,5},{8,10},{9,11},{10,... | collective-permute-start | bytes 811016 | tf_op jit(solution)/shard_map/ppermute | solution.py:709
  89.6 2.5 %copy-start.1 = (bf16[2048,2,640]{2,0,1:T(8,128)(2,1)S(1)}, bf16[2048,2,640]{2,0,1:T(8,128)(2,1)}, u32[]{:S(2)}) copy-start(bf16[2048,2,640]{2,0,1:T(8,128)(2,1)} %copy.20) | copy-start | bytes 15728644
  92.1 3.3 %copy-start.4 = (f32[2048]{0:T(1024)S(1)}, f32[2048]{0:T(1024)}, u32[]{:S(2)}) copy-start(f32[2048]{0:T(1024)} %param.21) | copy-start | bytes 24580
  92.1 15.6 %copy-start = (bf16[640,2048]{1,0:T(8,128)(2,1)S(1)}, bf16[640,2048]{1,0:T(8,128)(2,1)}, u32[]{:S(2)}) copy-start(bf16[640,2048]{1,0:T(8,128)(2,1)} %refs_5_.5) | copy-start | bytes 7864324
  95.7 6.8 %collective-permute-start.3 = (bf16[66,1024]{1,0:T(8,128)(2,1)S(1)}, bf16[66,1024]{1,0:T(8,128)(2,1)S(1)}, u32[]{:S(2)}, u32[]{:S(2)}) collective-permute-start(bf16[66,1024]{1,0:T(8,128)(2,1)S(1)} %get-tuple-element.88.refs_0_), channel_id=1, source_target_pairs={{0,8},{8,16},{16,24},{24,28},{28,20},{20,12},{12,4},{4,0},{1,9},{9... | collective-permute-start | bytes 405512 | tf_op jit(solution)/shard_map/ppermute | solution.py:719
  96.8 6.8 %collective-permute-start.5 = (bf16[66,1024]{1,0:T(8,128)(2,1)S(1)}, bf16[66,1024]{1,0:T(8,128)(2,1)S(1)}, u32[]{:S(2)}, u32[]{:S(2)}) collective-permute-start(bf16[66,1024]{1,0:T(8,128)(2,1)S(1)} %get-tuple-element.89.refs_1_), channel_id=1, source_target_pairs={{8,0},{16,8},{24,16},{28,24},{20,28},{12,20},{4,12},{0,4},{9,1},{1... | collective-permute-start | bytes 405512 | tf_op jit(solution)/shard_map/ppermute | solution.py:720
  97.8 7.9 %collective-permute-start.7 = (bf16[66,1024]{1,0:T(8,128)(2,1)S(1)}, bf16[66,1024]{1,0:T(8,128)(2,1)S(1)}, u32[]{:S(2)}, u32[]{:S(2)}) collective-permute-start(bf16[66,1024]{1,0:T(8,128)(2,1)S(1)} %get-tuple-element.89.refs_1_), channel_id=1, source_target_pairs={{0,8},{8,16},{16,24},{24,28},{28,20},{20,12},{12,4},{4,0},{1,9},{9... | collective-permute-start | bytes 405512 | tf_op jit(solution)/shard_map/ppermute | solution.py:723
  98.8 7.9 %collective-permute-start.8 = (bf16[66,1024]{1,0:T(8,128)(2,1)S(1)}, bf16[66,1024]{1,0:T(8,128)(2,1)S(1)}, u32[]{:S(2)}, u32[]{:S(2)}) collective-permute-start(bf16[66,1024]{1,0:T(8,128)(2,1)S(1)} %get-tuple-element.88.refs_0_), channel_id=1, source_target_pairs={{8,0},{16,8},{24,16},{28,24},{20,28},{12,20},{4,12},{0,4},{9,1},{1... | collective-permute-start | bytes 405512 | tf_op jit(solution)/shard_map/ppermute | solution.py:722
  102.5 7.0 %collective-permute-start.4 = (bf16[66,1024]{1,0:T(8,128)(2,1)S(1)}, bf16[66,1024]{1,0:T(8,128)(2,1)S(1)}, u32[]{:S(2)}, u32[]{:S(2)}) collective-permute-start(bf16[66,1024]{1,0:T(8,128)(2,1)S(1)} %collective-permute-done.3.refs_0_), channel_id=1, source_target_pairs={{0,8},{8,16},{16,24},{24,28},{28,20},{20,12},{12,4},{4,0},{1,9},{9... | collective-permute-start | bytes 405512 | tf_op jit(solution)/shard_map/ppermute | solution.py:719
  103.6 6.7 %collective-permute-start.6 = (bf16[66,1024]{1,0:T(8,128)(2,1)S(1)}, bf16[66,1024]{1,0:T(8,128)(2,1)S(1)}, u32[]{:S(2)}, u32[]{:S(2)}) collective-permute-start(bf16[66,1024]{1,0:T(8,128)(2,1)S(1)} %collective-permute-done.5.refs_3_), channel_id=1, source_target_pairs={{8,0},{16,8},{24,16},{28,24},{20,28},{12,20},{4,12},{0,4},{9,1},{1... | collective-permute-start | bytes 405512 | tf_op jit(solution)/shard_map/ppermute | solution.py:720
  105.7 6.6 %collective-permute-start.11 = (bf16[66,1024]{1,0:T(8,128)(2,1)S(1)}, bf16[66,1024]{1,0:T(8,128)(2,1)S(1)}, u32[]{:S(2)}, u32[]{:S(2)}) collective-permute-start(bf16[66,1024]{1,0:T(8,128)(2,1)S(1)} %collective-permute-done.7.refs_1_), channel_id=1, source_target_pairs={{0,8},{8,16},{16,24},{24,28},{28,20},{20,12},{12,4},{4,0},{1,9},{9... | collective-permute-start | bytes 405512 | tf_op jit(solution)/shard_map/ppermute | solution.py:723
  106.7 6.8 %collective-permute-start.12 = (bf16[66,1024]{1,0:T(8,128)(2,1)S(1)}, bf16[66,1024]{1,0:T(8,128)(2,1)S(1)}, u32[]{:S(2)}, u32[]{:S(2)}) collective-permute-start(bf16[66,1024]{1,0:T(8,128)(2,1)S(1)} %collective-permute-done.8.refs_2_), channel_id=1, source_target_pairs={{8,0},{16,8},{24,16},{28,24},{20,28},{12,20},{4,12},{0,4},{9,1},{1... | collective-permute-start | bytes 405512 | tf_op jit(solution)/shard_map/ppermute | solution.py:722
  110.3 6.1 %collective-permute-start.10 = (bf16[66,1024]{1,0:T(8,128)(2,1)S(1)}, bf16[66,1024]{1,0:T(8,128)(2,1)S(1)}, u32[]{:S(2)}, u32[]{:S(2)}) collective-permute-start(bf16[66,1024]{1,0:T(8,128)(2,1)S(1)} %collective-permute-done.6.refs_3_), channel_id=1, source_target_pairs={{8,0},{16,8},{24,16},{28,24},{20,28},{12,20},{4,12},{0,4},{9,1},{1... | collective-permute-start | bytes 405512 | tf_op jit(solution)/shard_map/ppermute | solution.py:720
  111.1 6.4 %collective-permute-start.9 = (bf16[66,1024]{1,0:T(8,128)(2,1)S(1)}, bf16[66,1024]{1,0:T(8,128)(2,1)S(1)}, u32[]{:S(2)}, u32[]{:S(2)}) collective-permute-start(bf16[66,1024]{1,0:T(8,128)(2,1)S(1)} %collective-permute-done.4.refs_0_), channel_id=1, source_target_pairs={{0,8},{8,16},{16,24},{24,28},{28,20},{20,12},{12,4},{4,0},{1,9},{9... | collective-permute-start | bytes 405512 | tf_op jit(solution)/shard_map/ppermute | solution.py:719
  112.3 7.3 %collective-permute-start.15 = (bf16[66,1024]{1,0:T(8,128)(2,1)S(1)}, bf16[66,1024]{1,0:T(8,128)(2,1)S(1)}, u32[]{:S(2)}, u32[]{:S(2)}) collective-permute-start(bf16[66,1024]{1,0:T(8,128)(2,1)S(1)} %collective-permute-done.11.refs_1_), channel_id=1, source_target_pairs={{0,8},{8,16},{16,24},{24,28},{28,20},{20,12},{12,4},{4,0},{1,9},{9... | collective-permute-start | bytes 405512 | tf_op jit(solution)/shard_map/ppermute | solution.py:723
  113.5 6.1 %collective-permute-start.16 = (bf16[66,1024]{1,0:T(8,128)(2,1)S(1)}, bf16[66,1024]{1,0:T(8,128)(2,1)S(1)}, u32[]{:S(2)}, u32[]{:S(2)}) collective-permute-start(bf16[66,1024]{1,0:T(8,128)(2,1)S(1)} %collective-permute-done.12.refs_2_), channel_id=1, source_target_pairs={{8,0},{16,8},{24,16},{28,24},{20,28},{12,20},{4,12},{0,4},{9,1},{1... | collective-permute-start | bytes 405512 | tf_op jit(solution)/shard_map/ppermute | solution.py:722
  117.5 6.3 %collective-permute-start.13 = (bf16[66,1024]{1,0:T(8,128)(2,1)S(1)}, bf16[66,1024]{1,0:T(8,128)(2,1)S(1)}, u32[]{:S(2)}, u32[]{:S(2)}) collective-permute-start(bf16[66,1024]{1,0:T(8,128)(2,1)S(1)} %collective-permute-done.9.refs_0_), channel_id=1, source_target_pairs={{0,8},{8,16},{16,24},{24,28},{28,20},{20,12},{12,4},{4,0},{1,9},{9... | collective-permute-start | bytes 405512 | tf_op jit(solution)/shard_map/ppermute | solution.py:719
  118.7 6.4 %collective-permute-start.14 = (bf16[66,1024]{1,0:T(8,128)(2,1)S(1)}, bf16[66,1024]{1,0:T(8,128)(2,1)S(1)}, u32[]{:S(2)}, u32[]{:S(2)}) collective-permute-start(bf16[66,1024]{1,0:T(8,128)(2,1)S(1)} %collective-permute-done.10.refs_3_), channel_id=1, source_target_pairs={{8,0},{16,8},{24,16},{28,24},{20,28},{12,20},{4,12},{0,4},{9,1},{1... | collective-permute-start | bytes 405512 | tf_op jit(solution)/shard_map/ppermute | solution.py:720
  121.5 6.9 %collective-permute-start.24 = (bf16[66,1024]{1,0:T(8,128)(2,1)S(1)}, bf16[66,1024]{1,0:T(8,128)(2,1)S(1)}, u32[]{:S(2)}, u32[]{:S(2)}) collective-permute-start(bf16[66,1024]{1,0:T(8,128)(2,1)S(1)} %get-tuple-element.101), channel_id=1, source_target_pairs={{0,8},{8,16},{16,24},{24,28},{28,20},{20,12},{12,4},{4,0},{1,9},{9... | collective-permute-start | bytes 405512 | tf_op jit(solution)/shard_map/ppermute | solution.py:736
  123.3 7.0 %collective-permute-start.17 = (bf16[66,1024]{1,0:T(8,128)(2,1)S(1)}, bf16[66,1024]{1,0:T(8,128)(2,1)S(1)}, u32[]{:S(2)}, u32[]{:S(2)}) collective-permute-start(bf16[66,1024]{1,0:T(8,128)(2,1)S(1)} %get-tuple-element.94), channel_id=1, source_target_pairs={{8,0},{16,8},{24,16},{28,24},{20,28},{12,20},{4,12},{0,4},{9,1},{1... | collective-permute-start | bytes 405512 | tf_op jit(solution)/shard_map/ppermute | solution.py:736
  126.9 5.5 %collective-permute-start.27 = (bf16[66,1024]{1,0:T(8,128)(2,1)S(1)}, bf16[66,1024]{1,0:T(8,128)(2,1)S(1)}, u32[]{:S(2)}, u32[]{:S(2)}) collective-permute-start(bf16[66,1024]{1,0:T(8,128)(2,1)S(1)} %get-tuple-element.105), channel_id=1, source_target_pairs={{8,0},{16,8},{24,16},{28,24},{20,28},{12,20},{4,12},{0,4},{9,1},{1... | collective-permute-start | bytes 405512 | tf_op jit(solution)/shard_map/ppermute | solution.py:736
  128.5 6.3 %collective-permute-start.25 = (bf16[66,1024]{1,0:T(8,128)(2,1)S(1)}, bf16[66,1024]{1,0:T(8,128)(2,1)S(1)}, u32[]{:S(2)}, u32[]{:S(2)}) collective-permute-start(bf16[66,1024]{1,0:T(8,128)(2,1)S(1)} %add_convert_fusion.5), channel_id=1, source_target_pairs={{0,8},{8,16},{16,24},{24,28},{28,20},{20,12},{12,4},{4,0},{1,9},{9... | collective-permute-start | bytes 405512 | tf_op jit(solution)/shard_map/ppermute | solution.py:736
  129.5 6.8 %collective-permute-start.20 = (bf16[66,1024]{1,0:T(8,128)(2,1)S(1)}, bf16[66,1024]{1,0:T(8,128)(2,1)S(1)}, u32[]{:S(2)}, u32[]{:S(2)}) collective-permute-start(bf16[66,1024]{1,0:T(8,128)(2,1)S(1)} %get-tuple-element.98), channel_id=1, source_target_pairs={{0,8},{8,16},{16,24},{24,28},{28,20},{20,12},{12,4},{4,0},{1,9},{9... | collective-permute-start | bytes 405512 | tf_op jit(solution)/shard_map/ppermute | solution.py:736
  130.3 6.5 %collective-permute-start.18 = (bf16[66,1024]{1,0:T(8,128)(2,1)S(1)}, bf16[66,1024]{1,0:T(8,128)(2,1)S(1)}, u32[]{:S(2)}, u32[]{:S(2)}) collective-permute-start(bf16[66,1024]{1,0:T(8,128)(2,1)S(1)} %add_convert_fusion.10), channel_id=1, source_target_pairs={{8,0},{16,8},{24,16},{28,24},{20,28},{12,20},{4,12},{0,4},{9,1},{1... | collective-permute-start | bytes 405512 | tf_op jit(solution)/shard_map/ppermute | solution.py:736
  132.5 6.1 %collective-permute-start.28 = (bf16[66,1024]{1,0:T(8,128)(2,1)S(1)}, bf16[66,1024]{1,0:T(8,128)(2,1)S(1)}, u32[]{:S(2)}, u32[]{:S(2)}) collective-permute-start(bf16[66,1024]{1,0:T(8,128)(2,1)S(1)} %add_convert_fusion.3), channel_id=1, source_target_pairs={{8,0},{16,8},{24,16},{28,24},{20,28},{12,20},{4,12},{0,4},{9,1},{1... | collective-permute-start | bytes 405512 | tf_op jit(solution)/shard_map/ppermute | solution.py:736
  134.8 14.5 %collective-permute-start.26 = (bf16[66,1024]{1,0:T(8,128)(2,1)S(1)}, bf16[66,1024]{1,0:T(8,128)(2,1)S(1)}, u32[]{:S(2)}, u32[]{:S(2)}) collective-permute-start(bf16[66,1024]{1,0:T(8,128)(2,1)S(1)} %add_convert_fusion.4), channel_id=1, source_target_pairs={{0,8},{8,16},{16,24},{24,28},{28,20},{20,12},{12,4},{4,0},{1,9},{9... | collective-permute-start | bytes 405512 | tf_op jit(solution)/shard_map/ppermute | solution.py:737
  136.4 5.5 %collective-permute-start.21 = (bf16[66,1024]{1,0:T(8,128)(2,1)S(1)}, bf16[66,1024]{1,0:T(8,128)(2,1)S(1)}, u32[]{:S(2)}, u32[]{:S(2)}) collective-permute-start(bf16[66,1024]{1,0:T(8,128)(2,1)S(1)} %add_convert_fusion.8), channel_id=1, source_target_pairs={{0,8},{8,16},{16,24},{24,28},{28,20},{20,12},{12,4},{4,0},{1,9},{9... | collective-permute-start | bytes 405512 | tf_op jit(solution)/shard_map/ppermute | solution.py:736
  136.9 12.4 %collective-permute-start.19 = (bf16[66,1024]{1,0:T(8,128)(2,1)S(1)}, bf16[66,1024]{1,0:T(8,128)(2,1)S(1)}, u32[]{:S(2)}, u32[]{:S(2)}) collective-permute-start(bf16[66,1024]{1,0:T(8,128)(2,1)S(1)} %add_convert_fusion.9), channel_id=1, source_target_pairs={{8,0},{16,8},{24,16},{28,24},{20,28},{12,20},{4,12},{0,4},{9,1},{1... | collective-permute-start | bytes 405512 | tf_op jit(solution)/shard_map/ppermute | solution.py:737
  138.6 5.4 %collective-permute-start.29 = (bf16[66,1024]{1,0:T(8,128)(2,1)S(1)}, bf16[66,1024]{1,0:T(8,128)(2,1)S(1)}, u32[]{:S(2)}, u32[]{:S(2)}) collective-permute-start(bf16[66,1024]{1,0:T(8,128)(2,1)S(1)} %add_convert_fusion.2), channel_id=1, source_target_pairs={{8,0},{16,8},{24,16},{28,24},{20,28},{12,20},{4,12},{0,4},{9,1},{1... | collective-permute-start | bytes 405512 | tf_op jit(solution)/shard_map/ppermute | solution.py:736
  142.0 5.2 %collective-permute-start.22 = (bf16[66,1024]{1,0:T(8,128)(2,1)S(1)}, bf16[66,1024]{1,0:T(8,128)(2,1)S(1)}, u32[]{:S(2)}, u32[]{:S(2)}) collective-permute-start(bf16[66,1024]{1,0:T(8,128)(2,1)S(1)} %add_convert_fusion.7), channel_id=1, source_target_pairs={{0,8},{8,16},{16,24},{24,28},{28,20},{20,12},{12,4},{4,0},{1,9},{9... | collective-permute-start | bytes 405512 | tf_op jit(solution)/shard_map/ppermute | solution.py:736
  144.1 5.2 %collective-permute-start.30 = (bf16[66,1024]{1,0:T(8,128)(2,1)S(1)}, bf16[66,1024]{1,0:T(8,128)(2,1)S(1)}, u32[]{:S(2)}, u32[]{:S(2)}) collective-permute-start(bf16[66,1024]{1,0:T(8,128)(2,1)S(1)} %add_convert_fusion.1), channel_id=1, source_target_pairs={{8,0},{16,8},{24,16},{28,24},{20,28},{12,20},{4,12},{0,4},{9,1},{1... | collective-permute-start | bytes 405512 | tf_op jit(solution)/shard_map/ppermute | solution.py:737
  147.2 5.2 %collective-permute-start.23 = (bf16[66,1024]{1,0:T(8,128)(2,1)S(1)}, bf16[66,1024]{1,0:T(8,128)(2,1)S(1)}, u32[]{:S(2)}, u32[]{:S(2)}) collective-permute-start(bf16[66,1024]{1,0:T(8,128)(2,1)S(1)} %add_convert_fusion.6), channel_id=1, source_target_pairs={{0,8},{8,16},{16,24},{24,28},{28,20},{20,12},{12,4},{4,0},{1,9},{9... | collective-permute-start | bytes 405512 | tf_op jit(solution)/shard_map/ppermute | solution.py:737
